TPU v7x, 128 devices: a whole 4x4x4 slice. The times are simulated.
128 devices in a mesh: seg: 16 (over y, z), head: 8 (over x, core).
Axes of the slice: x: 4, y: 4, z: 4, core: 2. Of those that a mesh axis runs over, the one named last changes fastest.
Arguments:
- ssm_input: bfloat16 [3, 16, 1536, 3072], P(None, 'seg', None, 'head'), may hold values from -6 to 6
- gate_input: bfloat16 [3, 16, 1536, 3072], P(None, 'seg', None, 'head'), may hold values from -300 to 300
- b_input: bfloat16 [3, 16, 1536, 256], P(None, 'seg'), may hold values from -0.375 to 0.375
- c_output: bfloat16 [3, 16, 1536, 256], P(None, 'seg'), may hold values from -0.375 to 0.375
- log_decay: float32 [3, 16, 24, 1536], P(None, 'seg', 'head'), may hold values from 0 to 1, as said below
- root_state: float32 [16, 24, 128, 256], P('seg', 'head'), may hold values from -12 to 12
- norm_gain: float32 [3072], P('head'), may hold values from 0.1 to 1.9
- out_grad: bfloat16 [3, 16, 1536, 3072], P(None, 'seg', None, 'head'), may hold values from -6 to 6
- parent_ids: int32 [2, 16], replicated, may hold values from 0 to 15
Outputs:
- input_grad: bfloat16 [3, 16, 1536, 3072], P(None, 'seg', None, 'head')
- state_grad: float32 [3, 16, 24, 128, 256], P(None, 'seg', 'head')
Inputs may be any that keep to these rules, and one draw needn't show every extreme that they name: parent_ids[0, j] is the level-0 parent of level-1 segment j and parent_ids[1, j] the level-1 parent of level-2 segment j; a segment may have any number of children. `log_decay`: positive decay rates.
All inputs are finite; a program needn't handle non-finite values.
Results may differ from a plain program's by a relative error of at most 0.0062.
Values sent between devices are 32-bit elements; how exact they have to be, the bound alone decides.
No kernel may reach another device: no remote copies, remote signals or barrier semaphores. Data moves between devices by JAX's collectives and lax.ppermute only.
A program may use at most 192 MiB of HBM per device.

v0:
```python
import jax
import jax.numpy as jnp
from jax import lax
from jax.sharding import PartitionSpec as P

BLOCK = 256
HEADS = 24
HDIM = 128


EPSILON = 1e-05


def block_prep(ssm_input, b_input, c_output, log_decay):
    segments, length, columns = ssm_input.shape
    head_count = log_decay.shape[1]
    head_size = columns // head_count
    blocks = length // BLOCK
    cumulative = -jnp.cumsum(log_decay.reshape(segments, head_count, blocks, BLOCK), axis=3)
    b_blocks = b_input.reshape(segments, blocks, BLOCK, b_input.shape[2])
    c_blocks = c_output.reshape(segments, blocks, BLOCK, c_output.shape[2])
    scores = jnp.einsum("sktn,skun->sktu", c_blocks, b_blocks, preferred_element_type=jnp.float32)
    causal = jnp.arange(BLOCK)[:, None] >= jnp.arange(BLOCK)[None, :]
    exponent = jnp.where(causal, cumulative[..., :, None] - cumulative[..., None, :], 0.0)
    weights = jnp.where(causal, scores[:, None] * jnp.exp(exponent), 0.0).astype(jnp.bfloat16)
    to_end = jnp.transpose(jnp.exp(cumulative[..., -1:] - cumulative), (0, 2, 3, 1))[..., None]
    x_blocks = ssm_input.reshape(segments, blocks, BLOCK, head_count, head_size)
    decayed = (x_blocks * to_end).astype(jnp.bfloat16)
    block_state = jnp.einsum(
        "skuhp,skun->skhpn", decayed, b_blocks, preferred_element_type=jnp.float32
    )
    return (cumulative, weights, block_state)


def run_blocks(block_state, cumulative, start_state):
    factor = jnp.exp(cumulative[..., -1])
    entries = []
    current = start_state
    for number in range(block_state.shape[1]):
        entries.append(current)
        current = factor[:, :, number, None, None] * current + block_state[:, number]
    return (jnp.stack(entries, axis=1), current)


def run_back(block_grad, cumulative, end_grad):
    factor = jnp.exp(cumulative[..., -1])
    exit_grads = []
    current = end_grad
    for number in range(block_grad.shape[1] - 1, -1, -1):
        exit_grads.insert(0, current)
        current = block_grad[:, number] + factor[:, :, number, None, None] * current
    return (jnp.stack(exit_grads, axis=1), current)


def readout(weights, ssm_input, c_output, cumulative, entries):
    segments, length, columns = ssm_input.shape
    head_count, blocks = (cumulative.shape[1], cumulative.shape[2])
    x_blocks = ssm_input.reshape(segments, blocks, BLOCK, head_count, columns // head_count)
    c_blocks = c_output.reshape(segments, blocks, BLOCK, c_output.shape[2])
    within = jnp.einsum("shktu,skuhp->skthp", weights, x_blocks, preferred_element_type=jnp.float32)
    from_start = jnp.transpose(jnp.exp(cumulative), (0, 2, 3, 1))[..., None]
    carried = (
        jnp.einsum(
            "sktn,skhpn->skthp",
            c_blocks,
            entries.astype(jnp.bfloat16),
            preferred_element_type=jnp.float32,
        )
        * from_start
    )
    return (within + carried).reshape(segments, length, columns)


def grad_prep(ssm_grad, c_output, cumulative):
    segments, length, columns = ssm_grad.shape
    head_count, blocks = (cumulative.shape[1], cumulative.shape[2])
    grad_blocks = ssm_grad.reshape(segments, blocks, BLOCK, head_count, columns // head_count)
    c_blocks = c_output.reshape(segments, blocks, BLOCK, c_output.shape[2])
    from_start = jnp.transpose(jnp.exp(cumulative), (0, 2, 3, 1))[..., None]
    decayed = (grad_blocks * from_start).astype(jnp.bfloat16)
    return jnp.einsum("skthp,sktn->skhpn", decayed, c_blocks, preferred_element_type=jnp.float32)


def input_grad(weights, ssm_grad, b_input, cumulative, exit_grads):
    segments, length, columns = ssm_grad.shape
    head_count, blocks = (cumulative.shape[1], cumulative.shape[2])
    grad_blocks = ssm_grad.reshape(segments, blocks, BLOCK, head_count, columns // head_count)
    b_blocks = b_input.reshape(segments, blocks, BLOCK, b_input.shape[2])
    within = jnp.einsum(
        "shktu,skthp->skuhp", weights, grad_blocks, preferred_element_type=jnp.float32
    )
    to_end = jnp.transpose(jnp.exp(cumulative[..., -1:] - cumulative), (0, 2, 3, 1))[..., None]
    carried = (
        jnp.einsum(
            "skhpn,skun->skuhp",
            exit_grads.astype(jnp.bfloat16),
            b_blocks,
            preferred_element_type=jnp.float32,
        )
        * to_end
    )
    return (within + carried).astype(jnp.bfloat16).reshape(segments, length, columns)


def place_rows(values, targets, row_count):
    matches = (jnp.arange(row_count, dtype=jnp.int32)[:, None] == targets[None, :]).astype(
        jnp.float32
    )
    return jnp.einsum("rs,shpn->rhpn", matches, values, precision=lax.Precision.HIGHEST)


def shards(
    ssm_input, gate_input, b_input, c_output, log_decay, root_state, norm_gain, out_grad, parent_ids
):
    seg_dev = ssm_input.shape[1]
    seg_total = parent_ids.shape[1]
    features = HEADS * HDIM
    own_ids = lax.axis_index("seg") * seg_dev + jnp.arange(seg_dev, dtype=jnp.int32)
    first_parent = jnp.take(parent_ids[0], own_ids)
    second_parent = jnp.take(parent_ids[1], own_ids)
    preps = [
        block_prep(ssm_input[depth], b_input[depth], c_output[depth], log_decay[depth])
        for depth in range(3)
    ]
    zeros_state = jnp.zeros_like(root_state)
    start_states = [root_state]
    entry_list = []
    for depth in range(2):
        entries, end_state = run_blocks(preps[depth][2], preps[depth][0], start_states[depth])
        entry_list.append(entries)
        every_end = lax.all_gather(end_state, "seg", axis=0, tiled=True)
        start_states.append(
            jnp.take(every_end, first_parent if depth == 0 else second_parent, axis=0)
        )
    entry_list.append(run_blocks(preps[2][2], preps[2][0], start_states[2])[0])
    ssm_grads = []
    for depth in range(3):
        ssm_out = readout(
            preps[depth][1], ssm_input[depth], c_output[depth], preps[depth][0], entry_list[depth]
        )
        gate_act = jax.nn.silu(gate_input[depth].astype(jnp.float32))
        gated_out = ssm_out * gate_act
        scaled = out_grad[depth].astype(jnp.float32) * norm_gain
        squares, products = lax.psum(
            (jnp.sum(gated_out * gated_out, axis=-1), jnp.sum(scaled * gated_out, axis=-1)), "head"
        )
        inv_rms = lax.rsqrt(squares / features + EPSILON)[..., None]
        dot_term = (products / features)[..., None]
        ssm_grads.append(
            (
                (inv_rms * scaled - gated_out * inv_rms * inv_rms * inv_rms * dot_term) * gate_act
            ).astype(jnp.bfloat16)
        )
    block_grads = [
        grad_prep(ssm_grads[depth], c_output[depth], preps[depth][0]) for depth in range(3)
    ]
    exit_list = [None, None, None]
    state_list = [None, None, None]
    end_grad = zeros_state
    for depth in (2, 1):
        exit_list[depth], state_list[depth] = run_back(
            block_grads[depth], preps[depth][0], end_grad
        )
        targets = second_parent if depth == 2 else first_parent
        end_grad = lax.psum_scatter(
            place_rows(state_list[depth], targets, seg_total),
            "seg",
            scatter_dimension=0,
            tiled=True,
        )
    exit_list[0], state_list[0] = run_back(block_grads[0], preps[0][0], end_grad)
    input_grads = [
        input_grad(
            preps[depth][1], ssm_grads[depth], b_input[depth], preps[depth][0], exit_list[depth]
        )
        for depth in range(3)
    ]
    return (jnp.stack(input_grads), jnp.stack(state_list))


def solution(mesh):
    in_specs = (
        P(None, "seg", None, "head"),
        P(None, "seg", None, "head"),
        P(None, "seg", None, None),
        P(None, "seg", None, None),
        P(None, "seg", "head", None),
        P("seg", "head", None, None),
        P("head"),
        P(None, "seg", None, "head"),
        P(),
    )
    out_specs = (P(None, "seg", None, "head"), P(None, "seg", "head", None, None))
    return jax.shard_map(shards, mesh=mesh, in_specs=in_specs, out_specs=out_specs, check_vma=False)
```

profile of v0, /device:TPU:0, one launch (start us, length us, event | category | flops | bytes accessed | tf_op | source)
XLA Modules:
  0.0 458.6 jit_solution(12964263884978514680)
XLA Ops:
  8.6 5.4 %reduce-window.20 = f32[1,3,6,2,128]{4,3,2,1,0:T(2,128)S(1)} reduce-window(f32[1,3,6,2,128]{4,3,2,1,0:T(2,128)S(1)} %bitcast.597, f32[]{:T(128)} %constant.54.clone.1), window={size=1x1x1x1x128 pad=0_0x0_0x0_0x0_0x127_0}, to_apply=%region_0.1 | reduce-window | flops 585216 | bytes 36868 | tf_op jit(solution)/shard_map/reduce-window
  16.8 3.1 fusion.122
  22.1 2.0 copy.147
  30.8 10.2 %reduce-window.24 = f32[1,3,6,2,128]{4,3,2,1,0:T(2,128)} reduce-window(f32[1,3,6,2,128]{4,3,2,1,0:T(2,128)} %bitcast.596, f32[]{:T(128)} %constant.54.clone.1), window={size=1x1x1x1x128 pad=0_0x0_0x0_0x0_0x127_0}, to_apply=%region_6.7 | reduce-window | flops 585216 | bytes 36868 | tf_op jit(solution)/shard_map/reduce-window.2
  46.4 4.1 reshape.1851
  50.5 3.5 copy.163
  54.8 3.5 convolution_bitcast_fusion.3
  58.3 32.9 %all-gather.3.cloned.1.call-done = f32[16,3,128,256]{3,2,1,0:T(8,128)} async-done(((f32[1,3,128,256]{3,2,1,0:T(8,128)}), f32[16,3,128,256]{3,2,1,0:T(8,128)}) %all-gather.3.cloned.1.call-update) | async-done | bytes 6291472 | tf_op jit(solution)/shard_map/all_gather | solution.py:131
  91.2 3.0 fusion.62
  98.9 10.1 %reduce-window.26 = f32[1,3,6,2,128]{4,3,2,1,0:T(2,128)} reduce-window(f32[1,3,6,2,128]{4,3,2,1,0:T(2,128)} %bitcast.595, f32[]{:T(128)} %constant.54.clone.1), window={size=1x1x1x1x128 pad=0_0x0_0x0_0x0_0x127_0}, to_apply=%region_12.14 | reduce-window | flops 585216 | bytes 36868 | tf_op jit(solution)/shard_map/reduce-window.4
  126.6 4.1 reshape.1852
  130.7 3.5 copy.179
  134.3 4.1 fusion.119
  138.4 2.4 copy.216
  140.8 2.4 copy.214
  143.2 2.4 copy.212
  145.6 3.9 reshape.1798
  156.9 2.7 multiply_reduce_fusion.2
  159.6 2.4 reshape.1803
  162.0 2.3 reshape.1808
  164.3 3.0 copy.156
  169.2 3.3 fusion.121
  173.8 2.0 copy.217
  175.8 2.3 reshape.1809
  178.2 2.6 reshape.1804
  180.7 2.3 reshape.1799
  184.0 3.2 convolution_bitcast_fusion.1
  189.6 2.7 fusion.38
  208.3 3.2 multiply_reduce_fusion
  214.2 1.9 reshape.1728
  216.1 7.1 %fusion.30 = (f32[1536]{0:T(1024)S(1)}, f32[1536]{0:T(1024)S(1)}, f32[1536]{0:T(1024)S(1)}) fusion(f32[1,1536,384]{1,2,0:T(8,128)} %reshape.1701, f32[384]{0:T(512)S(1)} %copy-done.102, bf16[1,1,1536,384]{2,3,1,0:T(8,128)(2,1)} %copy-done.16, bf16[1,1,1536,384]{2,3,1,0:T(8,128)(2,1)} %copy.212, f32[1,1536,384]{1,2,0:T(8,128)} %reshape.1715, ...), kind=kLoop, calls=%fused_computation.72 | loop fusion | flops 17690112 | bytes 14175744 | tf_op jit(solution)/shard_map/reduce_sum | solution.py:145
  223.2 26.0 %all-reduce.2 = (f32[1,1536]{1,0:T(1,128)S(1)}, f32[1,1536]{1,0:T(1,128)S(1)}, f32[1,1536]{1,0:T(1,128)S(1)}, f32[1,1536]{1,0:T(1,128)S(1)}, f32[1,1536]{1,0:T(1,128)S(1)}, /*index=5*/f32[1,1536]{1,0:T(1,128)S(1)}) all-reduce(f32[1,1536]{1,0:T(1,128)S(1)} %reduce_sum.77, ...), channel_id=1, replica_groups=mesh['seg'=16,'head'=8] {'head'}, use_global_device_ids=true, to_apply=%region_17.19 | all-reduce | flops 9216 | bytes 73728 | tf_op jit(solution)/shard_map/psum | solution.py:144
  249.5 14.0 %fusion.29 = (bf16[1,6,256,3,128]{2,4,3,1,0:T(8,128)(2,1)}, bf16[1,6,256,3,128]{2,4,3,1,0:T(8,128)(2,1)}, bf16[1,6,256,3,128]{2,4,3,1,0:T(8,128)(2,1)S(1)}) fusion(f32[1,6,256,3,128]{2,1,4,3,0:T(8,128)} %reshape.1799, f32[6,256]{1,0:T(8,128)S(1)} %mul.1053, f32[3,128]{1,0:T(4,128)S(1)} %bitcast.604, f32[6,256]{1,0:T(8,128)S(1)} %mul.1039, ...), kind=kLoop, calls=%fused_computation.59 | loop fusion | flops 24772608 | bytes 24811008 | tf_op jit(solution)/shard_map/convert_element_type | solution.py:152
  267.3 3.4 broadcast_multiply_fusion.1
  273.9 75.6 %reduce-scatter.7.cloned.1.call-done = f32[1,3,128,256]{3,2,1,0:T(8,128)} async-done(((f32[16,3,128,256]{3,2,1,0:T(8,128)}), f32[1,3,128,256]{3,2,1,0:T(8,128)}) %reduce-scatter.7.cloned.1.call-update) | async-done | bytes 393232
  349.5 2.2 fusion.93
  351.9 3.5 broadcast_multiply_fusion
  363.7 3.9 stack_reshape.11
  367.6 3.4 convolution_bitcast_fusion.4
  371.1 2.6 fusion.33
  377.1 1.9 copy.191
  379.0 3.7 stack_reshape.10
  382.7 53.6 %reduce-scatter.9.cloned.1.call-done = f32[1,3,128,256]{3,2,1,0:T(8,128)} async-done(((f32[16,3,128,256]{3,2,1,0:T(8,128)}), f32[1,3,128,256]{3,2,1,0:T(8,128)}) %reduce-scatter.9.cloned.1.call-update) | async-done | bytes 393232
  436.4 2.0 fusion.55
  441.7 2.1 stack_reshape.9
  443.8 2.2 pad_maximum_fusion
  446.0 3.6 copy.193
  449.6 2.3 pad_maximum_fusion.1
  (362 shorter events, 91.5 us)
Async XLA Ops:
  7.2 84.1 %all-gather.3.cloned.1.call-start = ((), (), s32[]{:S(2)}) async-start(), calls=%async_computation.2 | async-start | bytes 6684672 | tf_op jit(solution)/shard_map/all_gather | solution.py:131
  16.1 9.7 %copy-start.79 = (f32[3]{0:T(128)}, f32[3]{0:T(128)S(1)}, u32[]{:S(2)}) copy-start(f32[3]{0:T(128)S(1)} %get-tuple-element.64) | copy-start | bytes 40
  16.1 9.7 %copy-start.81 = (f32[3]{0:T(128)}, f32[3]{0:T(128)S(1)}, u32[]{:S(2)}) copy-start(f32[3]{0:T(128)S(1)} %get-tuple-element.65) | copy-start | bytes 40
  16.1 9.7 %copy-start.83 = (f32[3]{0:T(128)}, f32[3]{0:T(128)S(1)}, u32[]{:S(2)}) copy-start(f32[3]{0:T(128)S(1)} %get-tuple-element.67) | copy-start | bytes 40
  16.2 9.7 %copy-start.85 = (f32[3]{0:T(128)}, f32[3]{0:T(128)S(1)}, u32[]{:S(2)}) copy-start(f32[3]{0:T(128)S(1)} %get-tuple-element.63) | copy-start | bytes 40
  19.9 133.0 %copy-start.2 = (bf16[1,1,1536,256]{3,2,1,0:T(8,128)(2,1)}, bf16[1,1,1536,256]{3,2,1,0:T(8,128)(2,1)S(1)}, u32[]{:S(2)}) copy-start(bf16[1,1,1536,256]{3,2,1,0:T(8,128)(2,1)S(1)} %get-tuple-element.112) | copy-start | bytes 2359300
  27.2 176.4 %all-gather.5.cloned.1.call-start = ((), (), s32[]{:S(2)}) async-start(), calls=%async_computation.3 | async-start | bytes 6684672 | tf_op jit(solution)/shard_map/all_gather | solution.py:131
  54.8 39.4 %copy-start.94 = (f32[3]{0:T(128)}, f32[3]{0:T(128)S(1)}, u32[]{:S(2)}) copy-start(f32[3]{0:T(128)S(1)} %get-tuple-element.58) | copy-start | bytes 40
  54.8 39.4 %copy-start.96 = (f32[3]{0:T(128)}, f32[3]{0:T(128)S(1)}, u32[]{:S(2)}) copy-start(f32[3]{0:T(128)S(1)} %get-tuple-element.60) | copy-start | bytes 40
  54.8 39.4 %copy-start.98 = (f32[3]{0:T(128)}, f32[3]{0:T(128)S(1)}, u32[]{:S(2)}) copy-start(f32[3]{0:T(128)S(1)} %get-tuple-element.59) | copy-start | bytes 40
  54.8 36.4 %copy-start.100 = (f32[3]{0:T(128)S(1)}, f32[3]{0:T(128)}, u32[]{:S(2)}) copy-start(f32[3]{0:T(128)} %get-tuple-element.61) | copy-start | bytes 40
  94.3 255.2 %reduce-scatter.7.cloned.1.call-start = ((), (), s32[]{:S(2)}) async-start(), calls=%async_computation.4 | async-start | bytes 6684672
  145.6 4.0 copy-start.92
  145.6 5.3 %copy-start.89 = (f32[3]{0:T(128)S(1)}, f32[3]{0:T(128)}, u32[]{:S(2)}) copy-start(f32[3]{0:T(128)} %get-tuple-element.66) | copy-start | bytes 40
  149.5 3.8 copy-start.67
  173.1 5.0 %copy-start.15 = (bf16[1,1,1536,384]{2,3,1,0:T(8,128)(2,1)}, bf16[1,1,1536,384]{2,3,1,0:T(8,128)(2,1)S(1)}, u32[]{:S(2)}) copy-start(bf16[1,1,1536,384]{2,3,1,0:T(8,128)(2,1)S(1)} %copy.215) | copy-start | bytes 3538948
  173.8 6.9 %copy-start.16 = (bf16[1,1,1536,384]{2,3,1,0:T(8,128)(2,1)}, bf16[1,1,1536,384]{2,3,1,0:T(8,128)(2,1)S(1)}, u32[]{:S(2)}) copy-start(bf16[1,1,1536,384]{2,3,1,0:T(8,128)(2,1)S(1)} %copy.213) | copy-start | bytes 3538948
  175.8 4.9 %copy-start.17 = (bf16[1,1,1536,384]{2,3,1,0:T(8,128)(2,1)}, bf16[1,1,1536,384]{2,3,1,0:T(8,128)(2,1)S(1)}, u32[]{:S(2)}) copy-start(bf16[1,1,1536,384]{2,3,1,0:T(8,128)(2,1)S(1)} %copy.217) | copy-start | bytes 3538948
  183.1 4.1 copy-start.24
  183.9 80.1 %copy-start.77 = (f32[3]{0:T(128)}, f32[3]{0:T(128)S(1)}, u32[]{:S(2)}) copy-start(f32[3]{0:T(128)S(1)} %get-tuple-element.55) | copy-start | bytes 40
  183.9 80.1 %copy-start.104 = (f32[3]{0:T(128)}, f32[3]{0:T(128)S(1)}, u32[]{:S(2)}) copy-start(f32[3]{0:T(128)S(1)} %get-tuple-element.51) | copy-start | bytes 40
  187.6 4.7 %copy-start.53 = (f32[6,256,256]{2,1,0:T(8,128)}, f32[6,256,256]{2,1,0:T(8,128)S(1)}, u32[]{:S(2)}) copy-start(f32[6,256,256]{2,1,0:T(8,128)S(1)} %fusion.130) | copy-start | bytes 4718596
  192.3 3.8 copy-start.34
  192.3 3.9 copy-start.99
  193.8 3.6 copy-start.56
  193.8 3.6 copy-start.10
  193.8 3.6 copy-start.65
  203.6 3.7 copy-start.12
  216.1 33.4 %copy-start.9 = (f32[1,6,256,3,128]{2,1,4,3,0:T(8,128)S(1)}, f32[1,6,256,3,128]{2,1,4,3,0:T(8,128)}, u32[]{:S(2)}) copy-start(f32[1,6,256,3,128]{2,1,4,3,0:T(8,128)} %reshape.1798) | copy-start | bytes 7077892
  249.5 14.0 %copy-start.26 = (bf16[1,1,1536,256]{3,2,1,0:T(8,128)(2,1)S(1)}, bf16[1,1,1536,256]{3,2,1,0:T(8,128)(2,1)}, u32[]{:S(2)}) copy-start(bf16[1,1,1536,256]{3,2,1,0:T(8,128)(2,1)} %get-tuple-element.116) | copy-start | bytes 2359300
  270.7 78.8 %copy-start.95 = (f32[3]{0:T(128)S(1)}, f32[3]{0:T(128)}, u32[]{:S(2)}) copy-start(f32[3]{0:T(128)} %copy-done.94) | copy-start | bytes 40
  270.7 78.8 %copy-start.97 = (f32[3]{0:T(128)S(1)}, f32[3]{0:T(128)}, u32[]{:S(2)}) copy-start(f32[3]{0:T(128)} %copy-done.96) | copy-start | bytes 40
  270.8 165.6 %reduce-scatter.9.cloned.1.call-start = ((), (), s32[]{:S(2)}) async-start(), calls=%async_computation.5 | async-start | bytes 6684672
  351.7 3.6 copy-start.40
  355.4 4.5 copy-start.30
  355.4 4.5 copy-start.54
  355.4 4.5 copy-start.69
  355.4 4.5 copy-start.76
  361.9 5.8 %copy-start.21 = (bf16[1,1,1536,256]{3,2,1,0:T(8,128)(2,1)S(1)}, bf16[1,1,1536,256]{3,2,1,0:T(8,128)(2,1)}, u32[]{:S(2)}) copy-start(bf16[1,1,1536,256]{3,2,1,0:T(8,128)(2,1)} %copy-done.20) | copy-start | bytes 2359300
  367.6 3.4 copy-start.70
  367.6 3.4 copy-start.72
  377.0 59.4 %copy-start.1 = (f32[1,6,3,128,256]{4,3,2,1,0:T(8,128)S(1)}, f32[1,6,3,128,256]{4,3,2,1,0:T(8,128)}, u32[]{:S(2)}) copy-start(f32[1,6,3,128,256]{4,3,2,1,0:T(8,128)} %convolution_bitcast_fusion.4) | copy-start | bytes 7077892
  377.0 59.3 %copy-start.80 = (f32[3]{0:T(128)S(1)}, f32[3]{0:T(128)}, u32[]{:S(2)}) copy-start(f32[3]{0:T(128)} %copy-done.79) | copy-start | bytes 40
  377.0 59.3 %copy-start.82 = (f32[3]{0:T(128)S(1)}, f32[3]{0:T(128)}, u32[]{:S(2)}) copy-start(f32[3]{0:T(128)} %copy-done.81) | copy-start | bytes 40
  377.0 59.3 %copy-start.84 = (f32[3]{0:T(128)S(1)}, f32[3]{0:T(128)}, u32[]{:S(2)}) copy-start(f32[3]{0:T(128)} %copy-done.83) | copy-start | bytes 40
  377.0 59.3 %copy-start.87 = (f32[3]{0:T(128)S(1)}, f32[3]{0:T(128)}, u32[]{:S(2)}) copy-start(f32[3]{0:T(128)} %copy-done.85) | copy-start | bytes 40
  377.0 59.3 %copy-start.90 = (f32[3]{0:T(128)S(1)}, f32[3]{0:T(128)}, u32[]{:S(2)}) copy-start(f32[3]{0:T(128)} %get-tuple-element.66) | copy-start | bytes 40
  377.0 59.3 %copy-start.93 = (f32[3]{0:T(128)S(1)}, f32[3]{0:T(128)}, u32[]{:S(2)}) copy-start(f32[3]{0:T(128)} %get-tuple-element.68) | copy-start | bytes 40
  (63 other events, 126.1 us)
Sparse Core Ops, SparseCore 0:
  27.3 63.8 all-gather.2
  94.4 61.0 all-gather.4
  270.9 78.6 reduce-scatter.6
  355.5 80.8 reduce-scatter.8
where the time goes:
time: 465 us; the launch traced here: 459 us
  waiting for transfers between devices  162 us (35%)
  local copies, waits for them, and re-layouts  126 us (27%)
  other arithmetic  89.7 us (19%)
  matrix products  35.2 us (8%)
  blocking collectives  26 us (6%)
  between operations  19.3 us (4%)
    unnamed x6, waiting for transfers between devices  129 us
    all_gather x2, waiting for transfers between devices, shards(): every_end = lax.all_gather(end_state, 'seg', axis=0, tiled=True)  32.9 us
    another operation x25, local copies, waits for them, and re-layouts  31.4 us
    unnamed x224, local copies, waits for them, and re-layouts  28.1 us
    another operation x9, other arithmetic  28 us
    psum x1, blocking collectives, shards(): lax.psum((jnp.sum(gated_out * gated_out, axis=-1), jnp.sum(scaled * gated...  26 us
    convert_element_type x1, other arithmetic, shards(): ssm_grads.append(((inv_rms * scaled - gated_out * inv_rms * inv_rms * inv...  14 us
    unnamed x30, other arithmetic  13 us
  transfers between devices with their start and end apart: 4, of which 3 were waited for; matrix products, arithmetic and copies ran while one was open for 34% of the time, Pallas kernels for 0%

commit v1 on v0

v1 whole, which is shorter than its diff:
```python
import functools
import math

import jax
import jax.numpy as jnp
from jax import lax
from jax.experimental import pallas as pl
from jax.experimental.pallas import tpu as pltpu
from jax.sharding import PartitionSpec as P

BLOCK = 256
HALF = BLOCK // 2
HEADS = 24
HDIM = 128
STATE = 256
CHUNK = 3
SPAN = CHUNK * BLOCK
FOLD = SPAN // 2
EPSILON = 1e-05
VMEM_LIMIT = 24 * 1024 * 1024
LOG2E = math.log2(math.e)

WIDTH = 8 * CHUNK
CUM = 0
FROM_BLOCK = WIDTH
TO_BLOCK = 2 * WIDTH
FROM_LEVEL = 3 * WIDTH
TO_LEVEL = 4 * WIDTH

F32 = jnp.float32
BF16 = jnp.bfloat16
shaped = jax.ShapeDtypeStruct
pin = pltpu.with_memory_space_constraint


def call(body, name, micros, **kwargs):
    return pl.pallas_call(
        body,
        name=name,
        compiler_params=pltpu.CompilerParams(vmem_limit_bytes=VMEM_LIMIT),
        cost_estimate=pl.CostEstimate(
            flops=int(micros * 1e9), bytes_accessed=int(micros * 3e6), transcendentals=0
        ),
        **kwargs,
    )


def whole(array):
    rank = len(array.shape)
    return pl.BlockSpec(array.shape, lambda *_: (0,) * rank)


def dot(left, right, left_dim, right_dim, precision=None):
    return lax.dot_general(
        left,
        right,
        (((left_dim,), (right_dim,)), ((), ())),
        precision=precision,
        preferred_element_type=F32,
    )


def spread(packed, group, j, heads):
    at = group + 8 * j
    return jnp.concatenate(
        [
            jnp.broadcast_to(packed[:, at + h : at + h + 1], (packed.shape[0], HDIM))
            for h in range(heads)
        ],
        axis=1,
    )


def block(j):
    return slice(j * BLOCK, (j + 1) * BLOCK)


def head(h):
    return slice(h * HDIM, (h + 1) * HDIM)


def turn(values):
    size = values.shape[0]
    unit = lax.broadcasted_iota(jnp.int32, (size, size), 0) == lax.broadcasted_iota(
        jnp.int32, (size, size), 1
    )
    return dot(jnp.where(unit, 1.0, 0.0).astype(BF16), values, 1, 1).astype(BF16)


def silu(values):
    half = 0.5 * values
    return half + half * jnp.tanh(half)


def scatter_pieces(send, number, state, heads):
    rows = STATE // send.shape[0]
    for piece in range(send.shape[0]):
        for h in range(heads):
            at = (number * heads + h) * rows
            send[piece, at : at + rows] = state[piece * rows : (piece + 1) * rows, head(h)]


def gather_pieces(got, number, h, heads):
    rows = STATE // got.shape[0]
    at = (number * heads + h) * rows
    return got[:, at : at + rows].reshape(STATE, HDIM)


def start_all(copies):
    for copy in copies:
        copy.start()


def wait_all(copies):
    for copy in copies:
        copy.wait()


def piece_copies(sources, targets, sems, pieces):
    result = []
    for i, (at, first, count) in enumerate(pieces):
        rows = pl.ds(first * BLOCK, count * BLOCK)
        result.append(
            [
                pltpu.make_async_copy(source(at, rows), target.at[at, rows], sems.at[i, a])
                for a, (source, target) in enumerate(zip(sources, targets))
            ]
        )
    return result


def block_ends(parts):
    lasts = [part[:, BLOCK - 1 :] for part in parts]
    before = [jnp.zeros((8, 1), F32)]
    for last in lasts[:-1]:
        before.append(before[-1] + last)
    after = [jnp.zeros((8, 1), F32)]
    for last in lasts[:0:-1]:
        after.insert(0, after[0] + last)
    return lasts, before, after


def states_body(heads, steps, decay_hbm, root_hbm, x_hbm, b_hbm, send_out, rows_ref, rates, decay,
                send, root, x, b, decay_sem, root_sem, sems, out_sems):
    chunks = rows_ref.shape[0]
    blocks = steps * CHUNK
    decay_copy = pltpu.make_async_copy(decay_hbm, decay, decay_sem)
    decay_copy.start()
    pieces = [(0, 0, CHUNK), (0, CHUNK, CHUNK), (1, 0, CHUNK), (1, CHUNK, CHUNK)]
    copies = piece_copies(
        [lambda at, span: x_hbm.at[at, 0, span], lambda at, span: b_hbm.at[at, 0, span]],
        [x, b],
        sems,
        pieces,
    )
    root_copy = pltpu.make_async_copy(root_hbm.at[0], root, root_sem)
    start_all(copies[0])
    root_copy.start()
    for some in copies[1:]:
        start_all(some)

    rates[...] = jnp.zeros_like(rates)
    decay_copy.wait()
    for level in range(decay.shape[0]):
        for number in range(blocks):
            for h in range(heads):
                row = 8 * (level * blocks + number) + h
                rates[row : row + 1] = decay[level, h, :, block(number)]
    upper = (
        lax.broadcasted_iota(jnp.int32, (BLOCK, BLOCK), 0)
        <= lax.broadcasted_iota(jnp.int32, (BLOCK, BLOCK), 1)
    )
    upper = jnp.where(upper, 1.0, 0.0).astype(BF16)
    rest = rates[...]
    sums = jnp.zeros_like(rest)
    for _ in range(3):
        part = rest.astype(BF16)
        rest = rest - part.astype(F32)
        sums = sums + dot(part, upper, 1, 0)
    sums = sums * -LOG2E
    for chunk in range(chunks):
        rows_ref[chunk] = sums[WIDTH * chunk : WIDTH * (chunk + 1)]

    lines = []
    totals = []
    for level in range(2):
        numbers = range(level * blocks, (level + 1) * blocks)
        parts = [sums[8 * number : 8 * number + 8] for number in numbers]
        lasts, _, after = block_ends(parts)
        for part, last, suffix in zip(parts, lasts, after):
            lines.append(jnp.exp2(last - part + suffix))
        totals.append(jnp.exp2(after[0] + lasts[0]))
    lines.append(jnp.zeros((128 - 16 * blocks, BLOCK), F32))
    to_level = jnp.concatenate(lines, axis=0).T

    root_copy.wait()
    state = jnp.concatenate([(root[h] * totals[0][h : h + 1]).T for h in range(heads)], axis=1)
    half = heads * STATE // send.shape[0]
    outs = []
    for i, (level, first, count) in enumerate(pieces):
        if (level, first) == (1, 0):
            scatter_pieces(send, 0, state, heads)
            part = pl.ds(0, half)
            outs.append(
                pltpu.make_async_copy(send.at[:, part], send_out.at[:, part], out_sems.at[0])
            )
            outs[0].start()
            state = jnp.zeros((STATE, heads * HDIM), F32)
        wait_all(copies[i])
        for number in range(first, first + count):
            at = 8 * (level * blocks + number)
            scale = jnp.concatenate(
                [
                    jnp.broadcast_to(to_level[:, at + h : at + h + 1], (BLOCK, HDIM))
                    for h in range(heads)
                ],
                axis=1,
            )
            decayed = (x[level, block(number)].astype(F32) * scale).astype(BF16)
            state = state + dot(turn(b[level, block(number)]), decayed, 1, 0)
    scatter_pieces(send, 1, state, heads)
    decays = jnp.broadcast_to(totals[1], (8, HDIM))
    for piece in range(send.shape[0]):
        send[piece, send.shape[1] - 8 :] = decays
    part = pl.ds(half, send.shape[1] - half)
    outs.append(pltpu.make_async_copy(send.at[:, part], send_out.at[:, part], out_sems.at[1]))
    outs[1].start()
    wait_all(outs)


def pack(rows, packed):
    steps = packed.shape[0]
    parts = [rows[step, 8 * j : 8 * j + 8] for step in range(steps) for j in range(CHUNK)]
    lasts, before, after = block_ends(parts)
    for step in range(steps):
        mine = slice(step * CHUNK, (step + 1) * CHUNK)
        part = rows[step]
        last = jnp.concatenate(lasts[mine], axis=0)
        packed[step] = jnp.concatenate(
            [
                part,
                jnp.exp2(part),
                jnp.exp2(last - part),
                jnp.exp2(jnp.concatenate(before[mine], axis=0) + part),
                jnp.exp2(last - part + jnp.concatenate(after[mine], axis=0)),
                jnp.zeros((128 - 5 * WIDTH, BLOCK), F32),
            ],
            axis=0,
        ).T


def pick_body(heads, parent_ref, got_ref, send_out, send, sems):
    segments = got_ref.shape[0]
    rows = STATE // segments
    pair = send.shape[1]
    half = pair // 2
    quarter = segments // 4
    copies = []
    for seg in range(segments):
        first = parent_ref[0, seg]
        second = parent_ref[1, seg]
        root = parent_ref[0, second]
        send[seg, :half] = got_ref[first, :half]
        decay = got_ref[second, pair : pair + 8]
        for h in range(heads):
            a = slice(h * rows, (h + 1) * rows)
            b = slice(half + h * rows, half + (h + 1) * rows)
            send[seg, b] = decay[h : h + 1] * got_ref[root, a] + got_ref[second, b]
        if (seg + 1) % quarter == 0:
            part = pl.ds(seg + 1 - quarter, quarter)
            copies.append(
                pltpu.make_async_copy(send.at[part], send_out.at[part], sems.at[len(copies)])
            )
            copies[-1].start()
    wait_all(copies)


def fold_body(heads, parent_ref, decay_ref, got_ref, send_out, send, sems):
    rows = STATE // got_ref.shape[0]
    half = send.shape[1] // 2
    send[...] = jnp.zeros_like(send)
    copies = [
        pltpu.make_async_copy(send.at[:, part], send_out.at[:, part], sems.at[i])
        for i, part in enumerate([pl.ds(0, half), pl.ds(half, half)])
    ]
    for seg in range(got_ref.shape[0]):
        second = parent_ref[1, seg]
        send[second, :half] += got_ref[seg, :half]
    copies[0].start()
    for seg in range(got_ref.shape[0]):
        first = parent_ref[0, seg]
        decay = decay_ref[seg]
        for h in range(heads):
            a = slice(h * rows, (h + 1) * rows)
            b = slice(half + h * rows, half + (h + 1) * rows)
            send[first, b] += decay[h : h + 1] * send[seg, a] + got_ref[seg, b]
    copies[1].start()
    wait_all(copies)


def causal_mask(transposed):
    first = lax.broadcasted_iota(jnp.int32, (HALF, HALF), 0)
    second = lax.broadcasted_iota(jnp.int32, (HALF, HALF), 1)
    return first <= second if transposed else first >= second


def weighted(heads, j, rows, packed, x, b, c):
    scores = dot(c, b, 1, 1)
    causal = causal_mask(False)
    results = []
    for h in range(heads):
        row = rows[8 * j + h : 8 * j + h + 1]
        col = packed[:, CUM + 8 * j + h : CUM + 8 * j + h + 1]
        first = jnp.where(causal, col[:HALF] - row[:, :HALF], -jnp.inf)
        last = jnp.where(causal, col[HALF:] - row[:, HALF:], -jnp.inf)
        across = col[HALF:] - row[:, :HALF]
        top = jnp.concatenate(
            [(scores[:HALF, :HALF] * jnp.exp2(first)).astype(BF16), jnp.zeros((HALF, HALF), BF16)],
            axis=1,
        )
        bottom = jnp.concatenate(
            [
                (scores[HALF:, :HALF] * jnp.exp2(across)).astype(BF16),
                (scores[HALF:, HALF:] * jnp.exp2(last)).astype(BF16),
            ],
            axis=1,
        )
        results.append(dot(jnp.concatenate([top, bottom], axis=0), x[:, head(h)], 1, 0))
    return jnp.concatenate(results, axis=1)


def weighted_back(heads, j, rows, packed, grad, b, c):
    scores = dot(b, c, 1, 1)
    causal = causal_mask(True)
    results = []
    for h in range(heads):
        row = rows[8 * j + h : 8 * j + h + 1]
        col = packed[:, CUM + 8 * j + h : CUM + 8 * j + h + 1]
        first = jnp.where(causal, row[:, :HALF] - col[:HALF], -jnp.inf)
        last = jnp.where(causal, row[:, HALF:] - col[HALF:], -jnp.inf)
        across = row[:, HALF:] - col[:HALF]
        top = jnp.concatenate(
            [
                (scores[:HALF, :HALF] * jnp.exp2(first)).astype(BF16),
                (scores[:HALF, HALF:] * jnp.exp2(across)).astype(BF16),
            ],
            axis=1,
        )
        bottom = jnp.concatenate(
            [jnp.zeros((HALF, HALF), BF16), (scores[HALF:, HALF:] * jnp.exp2(last)).astype(BF16)],
            axis=1,
        )
        results.append(dot(jnp.concatenate([top, bottom], axis=0), grad[:, head(h)], 1, 0))
    return jnp.concatenate(results, axis=1)


def gated_sums(ssm_out, gate, out_grad, gain):
    gated = ssm_out * silu(gate.astype(F32))
    scaled = out_grad.astype(F32) * gain
    squares = jnp.sum(gated * gated, axis=1, keepdims=True)
    products = jnp.sum(scaled * gated, axis=1, keepdims=True)
    return gated, jnp.concatenate([squares, products, jnp.zeros((BLOCK, 6), F32)], axis=1).T


def store_sums(sums, step, at, pairs):
    both = jnp.concatenate(pairs, axis=1)
    for q in range(2):
        for half in range(2):
            sums[4 * step + 2 * q + half : 4 * step + 2 * q + half + 1, at : at + FOLD] = both[
                q : q + 1, half * FOLD : (half + 1) * FOLD
            ]


def norm_columns(total, step, at, features):
    lines = [total[4 * step + i : 4 * step + i + 1, at : at + FOLD] for i in range(4)]
    squares = jnp.concatenate(lines[:2], axis=1) / features
    dots = jnp.concatenate(lines[2:], axis=1) / features
    inv_rms = lax.rsqrt(squares + EPSILON)
    back = inv_rms * inv_rms * inv_rms * dots
    return jnp.concatenate([inv_rms, back, jnp.zeros((6, SPAN), F32)], axis=0).T


def ssm_gradient(j, norm, gain, gate, out_grad, gated):
    inv_rms, back = norm[block(j), 0:1], norm[block(j), 1:2]
    grad = inv_rms * (out_grad.astype(F32) * gain) - gated.astype(F32) * back
    return (grad * silu(gate.astype(F32))).astype(BF16)


def forward0_body(heads, steps, rows_ref, root_ref, gain_ref, x_ref, gate_ref, b_ref, c_ref,
                  out_grad_ref, gated_ref, sums_ref, state, packs):
    step = pl.program_id(0)

    @pl.when(step == 0)
    def _():
        pack(rows_ref, packs)
        for h in range(heads):
            state[:, head(h)] = root_ref[0, h].T

    rows, packed = rows_ref[step], packs[step]
    current = state[...]
    pairs = []
    for j in range(CHUNK):
        x, b, c = x_ref[0, 0, block(j)], b_ref[0, 0, block(j)], c_ref[0, 0, block(j)]
        within = weighted(heads, j, rows, packed, x, b, c)
        carried = dot(c, current.astype(BF16), 1, 0) * spread(packed, FROM_BLOCK, j, heads)
        gated, pair = gated_sums(
            within + carried, gate_ref[0, 0, block(j)], out_grad_ref[0, 0, block(j)], gain_ref[...]
        )
        gated_ref[0, block(j)] = gated.astype(BF16)
        pairs.append(pair)
        decayed = (x.astype(F32) * spread(packed, TO_BLOCK, j, heads)).astype(BF16)
        factor = spread(packed[BLOCK - 1 :], FROM_BLOCK, j, heads)
        current = current * factor + dot(turn(b), decayed, 1, 0)
    state[...] = current
    for part in range(steps):

        @pl.when(step == part)
        def _():
            store_sums(sums_ref, part, 0, pairs)


def local_body(heads, steps, rows_ref, x_ref, b_ref, c_ref, out_ref, turned_ref, state, packs):
    step = pl.program_id(1)

    @pl.when(step == 0)
    def _():
        pack(rows_ref, packs)
        state[...] = jnp.zeros_like(state)

    rows, packed = rows_ref[step], packs[step]
    current = state[...]
    for j in range(CHUNK):
        x, b, c = x_ref[0, 0, block(j)], b_ref[0, 0, block(j)], c_ref[0, 0, block(j)]
        within = weighted(heads, j, rows, packed, x, b, c)
        carried = dot(c, current.astype(BF16), 1, 0) * spread(packed, FROM_BLOCK, j, heads)
        out_ref[0, block(j)] = (within + carried).astype(BF16)
        turned_ref[0, block(j)] = turn(c)
        decayed = (x.astype(F32) * spread(packed, TO_BLOCK, j, heads)).astype(BF16)
        factor = spread(packed[BLOCK - 1 :], FROM_BLOCK, j, heads)
        current = current * factor + dot(turn(b), decayed, 1, 0)
    state[...] = current


def readout_body(heads, steps, local_hbm, gate_hbm, c_hbm, out_grad_hbm, turned_hbm, rows_hbm,
                 start_ref, gain_ref, first_sums_ref, gated_ref, gate, out_grad, turned, packed,
                 sums_out, local, c, rows, sums, sems, rows_sem, turned_sem, out_sem):
    rows_copy = pltpu.make_async_copy(rows_hbm.at[pl.ds(steps, 2 * steps)], rows, rows_sem)
    rows_copy.start()
    half = CHUNK * steps // 2
    pieces = [(0, 0, 1), (0, 1, 2), (0, half, half), (1, 0, half), (1, half, half)]
    copies = piece_copies(
        [
            lambda at, span: c_hbm.at[at + 1, 0, span],
            lambda at, span: local_hbm.at[at, span],
            lambda at, span: gate_hbm.at[at + 1, 0, span],
            lambda at, span: out_grad_hbm.at[at + 1, 0, span],
        ],
        [c, local, gate, out_grad],
        sems,
        pieces,
    )
    for some in copies:
        start_all(some)
    turned_copy = pltpu.make_async_copy(turned_hbm, turned, turned_sem)
    turned_copy.start()
    sums[0, :, :FOLD] = first_sums_ref[...]
    rows_copy.wait()
    for at in range(2):
        pack(rows.at[pl.ds(at * steps, steps)], packed.at[pl.ds(at * steps, steps)])
    pairs = []
    for i, (at, first, count) in enumerate(pieces):
        if first == 0:
            start = jnp.concatenate(
                [gather_pieces(start_ref, at, h, heads) for h in range(heads)], axis=1
            ).astype(BF16)
        wait_all(copies[i])
        for number in range(first, first + count):
            step, j = number // CHUNK, number % CHUNK
            place = block(number)
            carried = dot(c[at, place], start, 1, 0)
            carried = carried * spread(packed[at * steps + step], FROM_LEVEL, j, heads)
            gated, pair = gated_sums(
                carried + local[at, place].astype(F32),
                gate[at, place],
                out_grad[at, place],
                gain_ref[...],
            )
            gated_ref[at, place] = gated.astype(BF16)
            pairs.append(pair)
            if j == CHUNK - 1:
                store_sums(sums.at[0], step, (at + 1) * FOLD, pairs)
                pairs = []
    for copy in range(1, sums.shape[0]):
        sums[copy] = sums[0]
    out = pltpu.make_async_copy(sums, sums_out, out_sem)
    out.start()
    turned_copy.wait()
    out.wait()


def grads_body(heads, steps, features, packed_ref, turned_ref, gate_ref, out_grad_ref, gated_ref,
               total_ref, gain_ref, grad_out, send_out, grads, send, grad_sems, sems):
    total = jnp.sum(total_ref[...], axis=0)
    half = send.shape[1] // 2
    outs = []
    for at in (1, 0):
        state = jnp.zeros((STATE, heads * HDIM), F32)
        for step in range(steps):
            packed = packed_ref[at * steps + step]
            norm = norm_columns(total, step, (at + 1) * FOLD, features)
            for j in range(CHUNK):
                place = block(step * CHUNK + j)
                grad = ssm_gradient(
                    j,
                    norm,
                    gain_ref[...],
                    gate_ref[at, place],
                    out_grad_ref[at, place],
                    gated_ref[at, place],
                )
                grads[at, place] = grad
                decayed = (grad.astype(F32) * spread(packed, FROM_LEVEL, j, heads)).astype(BF16)
                state = state + dot(turned_ref[at, place], decayed, 1, 0)
            span = pl.ds(step * SPAN, SPAN)
            outs.append(
                pltpu.make_async_copy(
                    grads.at[at, span], grad_out.at[at, span], grad_sems.at[at * steps + step]
                )
            )
            outs[-1].start()
        scatter_pieces(send, 1 - at, state, heads)
        part = pl.ds((1 - at) * half, half)
        outs.append(pltpu.make_async_copy(send.at[:, part], send_out.at[:, part], sems.at[at]))
        outs[-1].start()
    wait_all(outs)


def back_chunk(heads, rows, packed, grad_of, b_ref, c_ref, state):
    current = state[...]
    for j in reversed(range(CHUNK)):
        b, c = b_ref[0, 0, block(j)], c_ref[0, 0, block(j)]
        grad = grad_of(j)
        within = weighted_back(heads, j, rows, packed, grad, b, c)
        carried = dot(b, current.astype(BF16), 1, 0) * spread(packed, TO_BLOCK, j, heads)
        yield j, (within + carried).astype(BF16)
        decayed = (grad.astype(F32) * spread(packed, FROM_BLOCK, j, heads)).astype(BF16)
        factor = spread(packed[BLOCK - 1 :], FROM_BLOCK, j, heads)
        current = current * factor + dot(turn(c), decayed, 1, 0)
    state[...] = current


def back0_body(heads, steps, features, rows_ref, gain_ref, total_ref, gate_ref, b_ref, c_ref,
               out_grad_ref, gated_ref, partial_ref, state_grad_ref, state, packs, norms):
    step = steps - 1 - pl.program_id(0)

    @pl.when(step == steps - 1)
    def _():
        pack(rows_ref, packs)
        total = jnp.sum(total_ref[...], axis=0)
        for part in range(steps):
            norms[part] = norm_columns(total, part, 0, features)
        state[...] = jnp.zeros_like(state)

    norm = norms[step]

    def grad_of(j):
        return ssm_gradient(
            j,
            norm,
            gain_ref[...],
            gate_ref[0, 0, block(j)],
            out_grad_ref[0, 0, block(j)],
            gated_ref[0, block(j)],
        )

    for j, part in back_chunk(heads, rows_ref[step], packs[step], grad_of, b_ref, c_ref, state):
        partial_ref[0, 0, block(j)] = part

    @pl.when(step == 0)
    def _():
        for h in range(heads):
            state_grad_ref[0, 0, h] = state[:, head(h)].T


def back_body(heads, steps, rows_ref, grad_ref, b_ref, c_ref, given_in, given_state, partial_ref,
              state_grad_ref, state, packs):
    step = steps - 1 - pl.program_id(1)

    @pl.when(step == steps - 1)
    def _():
        pack(rows_ref, packs)
        state[...] = jnp.zeros_like(state)

    def grad_of(j):
        return grad_ref[0, block(j)]

    for j, part in back_chunk(heads, rows_ref[step], packs[step], grad_of, b_ref, c_ref, state):
        partial_ref[0, 0, block(j)] = part

    @pl.when(step == 0)
    def _():
        for h in range(heads):
            state_grad_ref[0, 0, h] = state[:, head(h)].T


def inputs_body(heads, steps, b_hbm, partial_hbm, local_hbm, rows_hbm, end_ref, input_grad_out,
                state_grad_out, b, partial, grads, states, rows, packed, sems, local_sems,
                rows_sem, out_sems, state_sems):
    rows_copy = pltpu.make_async_copy(rows_hbm.at[pl.ds(0, 2 * steps)], rows, rows_sem)
    rows_copy.start()
    half = CHUNK * steps // 2
    pieces = [(1, 0, 1), (1, 1, 2), (1, half, half), (0, 0, half), (0, half, 2), (0, half + 2, 1)]
    copies = piece_copies(
        [lambda at, span: b_hbm.at[at, 0, span], lambda at, span: partial_hbm.at[at, 0, span]],
        [b, partial],
        sems,
        pieces,
    )
    locals_in = [
        pltpu.make_async_copy(local_hbm.at[level, 0], states.at[level], local_sems.at[level])
        for level in range(2)
    ]
    for i, (level, first, _) in enumerate(pieces):
        start_all(copies[i])
        if first == half:
            locals_in[level].start()
    rows_copy.wait()
    for level in range(2):
        pack(rows.at[pl.ds(level * steps, steps)], packed.at[pl.ds(level * steps, steps)])
    outs = []
    for i, (level, first, count) in enumerate(pieces):
        if first == 0:
            end = jnp.concatenate(
                [gather_pieces(end_ref, 1 - level, h, heads) for h in range(heads)], axis=1
            )
            rounded = end.astype(BF16)
        wait_all(copies[i])
        for number in range(first, first + count):
            place = block(number)
            extra = dot(b[level, place], rounded, 1, 0) * spread(
                packed[level * steps + number // CHUNK], TO_LEVEL, number % CHUNK, heads
            )
            grads[level, place] = (partial[level, place].astype(F32) + extra).astype(BF16)
        span = pl.ds(first * BLOCK, count * BLOCK)
        outs.append(
            pltpu.make_async_copy(
                grads.at[level, span], input_grad_out.at[level, 0, span], out_sems.at[i]
            )
        )
        outs[-1].start()
        if first == half:
            last = packed[(level + 1) * steps - 1, BLOCK - 1 :]
            total = spread(last, FROM_LEVEL, CHUNK - 1, heads)
            locals_in[level].wait()
            for h in range(heads):
                states[level, h] += (end[:, head(h)] * total[:, head(h)]).T
            outs.append(
                pltpu.make_async_copy(
                    states.at[level], state_grad_out.at[level, 0], state_sems.at[level]
                )
            )
            outs[-1].start()
    wait_all(outs)


def shards(features, head_devices, ssm_input, gate_input, b_input, c_output, log_decay,
           root_state, norm_gain, out_grad, parent_ids):
    levels, _, length, columns = ssm_input.shape
    heads = columns // HDIM
    blocks = length // BLOCK
    steps = blocks // CHUNK
    segments = parent_ids.shape[1]
    rows = STATE // segments
    gain = norm_gain.reshape(1, columns)
    decay = jnp.transpose(log_decay, (0, 2, 1, 3))

    smem = pl.BlockSpec(memory_space=pltpu.SMEM)
    vmem = pl.BlockSpec(memory_space=pltpu.VMEM)
    anywhere = pl.BlockSpec(memory_space=pl.ANY)
    rows_shape = (levels * steps, WIDTH, BLOCK)
    two_levels = (2 * steps, BLOCK, 128)
    pair_shape = (segments, 2 * heads * rows, HDIM)
    first_shape = (segments, 2 * heads * rows + 8, HDIM)
    sums_shape = (head_devices, 8, levels * FOLD)
    state_shape = (levels, 1, heads, HDIM, STATE)
    state_scratch = pltpu.VMEM((STATE, columns), F32)
    packs_scratch = pltpu.VMEM((steps, BLOCK, 128), F32)
    pair_scratch = pltpu.VMEM(pair_shape, F32)
    dma = pltpu.SemaphoreType.DMA

    far = lambda array: pin(array, pltpu.HBM)
    near = lambda array: pin(array, pltpu.VMEM)
    decay, x, gate, out_grad = far(decay), far(ssm_input), far(gate_input), far(out_grad)
    b, c, root = far(b_input), far(c_output), far(root_state)

    def pair_of_levels(width):
        return pltpu.VMEM((2, length, width), BF16)

    def tokens(width, place):
        return pl.BlockSpec((1, 1, SPAN, width), lambda *g: (place(*g)[0], 0, place(*g)[1], 0))

    def flat(width, place):
        return pl.BlockSpec((1, SPAN, width), lambda *g: (*place(*g), 0))

    def level_rows(place):
        return pl.BlockSpec((steps,) + rows_shape[1:], lambda *g: (place(*g)[0], 0, 0))

    def state_grads(place):
        return pl.BlockSpec((1, 1, heads, HDIM, STATE), lambda *g: (place(*g)[0], 0, 0, 0, 0))

    exchange = functools.partial(
        lax.all_to_all, axis_name="seg", split_axis=0, concat_axis=0, tiled=True
    )

    send, cum_rows = call(
        functools.partial(states_body, heads, steps),
        "states",
        6,
        in_specs=[anywhere] * 4,
        out_specs=[anywhere, vmem],
        out_shape=[pltpu.HBM(first_shape, F32), pltpu.HBM(rows_shape, F32)],
        scratch_shapes=[
            pltpu.VMEM((levels * blocks * 8, BLOCK), F32),
            pltpu.VMEM(decay.shape, F32),
            pltpu.VMEM(first_shape, F32),
            pltpu.VMEM(root_state.shape[1:], F32),
            pair_of_levels(columns),
            pair_of_levels(STATE),
            dma,
            dma,
            dma((4, 2)),
            dma((2,)),
        ],
    )(decay, root, x, b)
    got = exchange(send)

    own = lambda k: (0, k)
    gated0, sums0 = call(
        functools.partial(forward0_body, heads, steps),
        "forward0",
        6,
        grid=(steps,),
        in_specs=[
            level_rows(own),
            whole(root_state),
            whole(gain),
            tokens(columns, own),
            tokens(columns, own),
            tokens(STATE, own),
            tokens(STATE, own),
            tokens(columns, own),
        ],
        out_specs=[flat(columns, own), pl.BlockSpec((8, FOLD), lambda _: (0, 0))],
        out_shape=[pltpu.HBM((1, length, columns), BF16), pltpu.HBM((8, FOLD), F32)],
        scratch_shapes=[state_scratch, packs_scratch],
    )(far(cum_rows), root, gain, x, gate, b, c, out_grad)

    got, sums0 = lax.optimization_barrier((got, sums0))
    picked = call(
        functools.partial(pick_body, heads),
        "pick",
        1,
        in_specs=[smem, vmem],
        out_specs=anywhere,
        out_shape=pltpu.HBM(pair_shape, F32),
        scratch_shapes=[pair_scratch, dma((4,))],
    )(parent_ids, near(got))

    picked, late_rows = lax.optimization_barrier((picked, cum_rows))
    starts = exchange(picked)
    both = lambda l, k: (l, k)
    later = lambda l, k: (l + 1, k)
    local, turned = call(
        functools.partial(local_body, heads, steps),
        "local",
        7,
        grid=(2, steps),
        in_specs=[
            level_rows(later),
            tokens(columns, later),
            tokens(STATE, later),
            tokens(STATE, later),
        ],
        out_specs=[flat(columns, both), flat(BLOCK, both)],
        out_shape=[
            pltpu.HBM((2, length, columns), BF16),
            pltpu.HBM((2, blocks * STATE, BLOCK), BF16),
        ],
        scratch_shapes=[state_scratch, packs_scratch],
    )(far(late_rows), x, b, c)

    gated, gate_near, out_grad_near, turned_near, packed, sums = call(
        functools.partial(readout_body, heads, steps),
        "readout",
        5,
        in_specs=[anywhere] * 6 + [vmem] * 3,
        out_specs=[vmem] * 5 + [anywhere],
        out_shape=[
            pair_of_levels(columns),
            pair_of_levels(columns),
            pair_of_levels(columns),
            pair_of_levels(BLOCK),
            pltpu.VMEM(two_levels, F32),
            pltpu.HBM(sums_shape, F32),
        ],
        scratch_shapes=[
            pair_of_levels(columns),
            pair_of_levels(STATE),
            pltpu.VMEM((2 * steps,) + rows_shape[1:], F32),
            pltpu.VMEM(sums_shape, F32),
            dma((5, 4)),
            dma,
            dma,
            dma,
        ],
    )(
        far(local),
        gate,
        c,
        out_grad,
        far(turned),
        far(late_rows),
        near(starts),
        gain,
        sums0,
    )
    totals = lax.all_to_all(sums, "head", split_axis=0, concat_axis=0, tiled=True)

    grads, send_back = call(
        functools.partial(grads_body, heads, steps, features),
        "grads",
        5,
        in_specs=[vmem] * 7,
        out_specs=[anywhere, anywhere],
        out_shape=[pltpu.HBM((2, length, columns), BF16), pltpu.HBM(pair_shape, F32)],
        scratch_shapes=[pair_of_levels(columns), pair_scratch, dma((2 * steps,)), dma((2,))],
    )(
        near(packed),
        near(turned_near),
        near(gate_near),
        near(out_grad_near),
        near(gated),
        near(totals),
        gain,
    )
    got_back = exchange(send_back)

    own_back = lambda k: (0, steps - 1 - k)
    given = call(
        functools.partial(back0_body, heads, steps, features),
        "back0",
        6,
        grid=(steps,),
        in_specs=[
            level_rows(own_back),
            whole(gain),
            pl.BlockSpec(sums_shape, lambda _: (0, 0, 0)),
            tokens(columns, own_back),
            tokens(STATE, own_back),
            tokens(STATE, own_back),
            tokens(columns, own_back),
            flat(columns, own_back),
        ],
        out_specs=[tokens(columns, own_back), state_grads(own_back)],
        out_shape=[pltpu.HBM(ssm_input.shape, BF16), pltpu.HBM(state_shape, F32)],
        scratch_shapes=[state_scratch, packs_scratch, pltpu.VMEM((steps, SPAN, 8), F32)],
    )(far(cum_rows), gain, totals, gate, b, c, out_grad, far(gated0))

    got_back, *given = lax.optimization_barrier((got_back, *given))
    folded = call(
        functools.partial(fold_body, heads),
        "fold",
        1,
        in_specs=[smem, vmem, vmem],
        out_specs=anywhere,
        out_shape=pltpu.HBM(pair_shape, F32),
        scratch_shapes=[pair_scratch, dma((2,))],
    )(parent_ids, got[:, pair_shape[1] :], near(got_back))

    folded, late_rows = lax.optimization_barrier((folded, cum_rows))
    ends = exchange(folded)
    down_back = lambda l, k: (2 - l, steps - 1 - k)
    both_down_back = lambda l, k: (1 - l, steps - 1 - k)
    given = call(
        functools.partial(back_body, heads, steps),
        "back",
        8,
        grid=(2, steps),
        in_specs=[
            level_rows(down_back),
            flat(columns, both_down_back),
            tokens(STATE, down_back),
            tokens(STATE, down_back),
            anywhere,
            anywhere,
        ],
        out_specs=[tokens(columns, down_back), state_grads(down_back)],
        out_shape=[pltpu.HBM(ssm_input.shape, BF16), pltpu.HBM(state_shape, F32)],
        input_output_aliases={4: 0, 5: 1},
        scratch_shapes=[state_scratch, packs_scratch],
    )(far(late_rows), far(grads), b, c, *given)

    return call(
        functools.partial(inputs_body, heads, steps),
        "inputs",
        4,
        in_specs=[anywhere] * 4 + [vmem],
        out_specs=[anywhere, anywhere],
        out_shape=[pltpu.HBM(ssm_input.shape, BF16), pltpu.HBM(state_shape, F32)],
        input_output_aliases={1: 0, 2: 1},
        scratch_shapes=[
            pair_of_levels(STATE),
            pair_of_levels(columns),
            pair_of_levels(columns),
            pltpu.VMEM((2,) + state_shape[2:], F32),
            pltpu.VMEM((2 * steps,) + rows_shape[1:], F32),
            pltpu.VMEM(two_levels, F32),
            dma((6, 2)),
            dma((2,)),
            dma,
            dma((6,)),
            dma((2,)),
        ],
    )(b, *given, far(late_rows), near(ends))


def solution(mesh):
    in_specs = (
        P(None, "seg", None, "head"),
        P(None, "seg", None, "head"),
        P(None, "seg", None, None),
        P(None, "seg", None, None),
        P(None, "seg", "head", None),
        P("seg", "head", None, None),
        P("head"),
        P(None, "seg", None, "head"),
        P(),
    )
    out_specs = (P(None, "seg", None, "head"), P(None, "seg", "head", None, None))

    def run(*arrays):
        body = functools.partial(shards, arrays[0].shape[3], mesh.shape["head"])
        return tuple(
            jax.shard_map(
                body, mesh=mesh, in_specs=in_specs, out_specs=out_specs, check_vma=False
            )(*arrays)
        )

    return run
```

time: 465 us -> 119 us (0.26); the launches traced: 459 us -> 119 us
  waiting for transfers between devices: 162 us -> 19.7 us
  local copies, waits for them, and re-layouts: 126 us -> 0.02 us
  other arithmetic: 89.7 us -> 0 us
  Pallas kernels: 0 us -> 65.9 us
  matrix products: 35.2 us -> 0 us
  starting transfers between devices: 0.34 us -> 19.8 us
  between operations: 19.3 us -> 0.91 us
  blocking collectives: 26 us -> 12.2 us
    unnamed x6 -> x0, waiting for transfers between devices: 129 us -> none
    pallas_call x0 -> x10, Pallas kernels: none -> 65.9 us  [the longest x1 10.6 us: shards(): call(functools.partial(back_body, heads, steps), 'back', 8, grid=(2, step...]
    another operation x30 -> x0, local copies, waits for them, and re-layouts: 41.2 us -> none
    another operation x17 -> x0, other arithmetic: 36.9 us -> none
    dot_general x21 -> x0, matrix products: 35.2 us -> none  [the longest x3 8.51 us: block_prep(): jnp.einsum('skuhp,skun->skhpn', decayed, b_blocks, preferred_element_type...]
    all_gather x2 -> x0, waiting for transfers between devices: 32.9 us -> none  [shards(): every_end = lax.all_gather(end_state, 'seg', axis=0, tiled=True)]
    unnamed x224 -> x6, local copies, waits for them, and re-layouts: 28.1 us -> 0.01 us
    psum x1 -> x0, blocking collectives: 26 us -> none  [shards(): lax.psum((jnp.sum(gated_out * gated_out, axis=-1), jnp.sum(scaled * gated...]
  transfers between devices with their start and end apart: 4 -> 4, of which waited for: 3 -> 4; matrix products, arithmetic and copies ran while one was open for 34% -> 0% of each run, Pallas kernels for 0% -> 30%
where the time goes in v1:
time: 119 us
  Pallas kernels  65.9 us (55%)
  starting transfers between devices  19.8 us (17%)
  waiting for transfers between devices  19.7 us (17%)
  blocking collectives  12.2 us (10%)
    all_to_all x1, blocking collectives, shards(): lax.all_to_all(sums, 'head', split_axis=0, concat_axis=0, tiled=True)  12.2 us
    pallas_call x1, Pallas kernels, shards(): call(functools.partial(back_body, heads, steps), 'back', 8, grid=(2, step...  10.6 us
    pallas_call x1, Pallas kernels, shards(): call(functools.partial(local_body, heads, steps), 'local', 7, grid=(2, st...  10.1 us
    pallas_call x1, Pallas kernels, shards(): call(functools.partial(readout_body, heads, steps), 'readout', 5, in_spec...  8.82 us
    all_to_all x1, starting transfers between devices, shards(): got = exchange(send)  8.14 us
    all_to_all x1, waiting for transfers between devices, shards(): got = exchange(send)  7.84 us
    pallas_call x1, Pallas kernels, shards(): call(functools.partial(back0_body, heads, steps, features), 'back0', 6, g...  7.78 us
    pallas_call x1, Pallas kernels, shards(): call(functools.partial(forward0_body, heads, steps), 'forward0', 6, grid=...  7.31 us
  transfers between devices with their start and end apart: 4, of which 4 were waited for; matrix products, arithmetic and copies ran while one was open for 0% of the time, Pallas kernels for 30%

profile of v1, /device:TPU:0, one launch (start us, length us, event | category | flops | bytes accessed | tf_op | source)
XLA Modules:
  0.0 118.7 jit_solution(11878396208086976081)
XLA Ops:
  0.6 0.0 copy-start.2
  0.6 7.3 %states.1 = (f32[16,104,128]{2,1,0:T(8,128)}, f32[6,24,256]{2,1,0:T(8,128)}) custom-call(f32[3,3,1,1536]{3,2,1,0:T(1,128)} %bitcast.1, f32[1,3,128,256]{3,2,1,0:T(8,128)} %root_ref.1, bf16[3,1,1536,384]{3,2,1,0:T(8,128)(2,1)} %x_ref.3, bf16[3,1,1536,256]{3,2,1,0:T(8,128)(2,1)} %b_hbm.3), custom_call_target="tpu_custom_call" | custom-call | flops 6000000000 | bytes 18000000 | tf_op jit(solution)/shard_map/states/pallas_call | solution.py:715
  7.9 8.1 %all-to-all-start = ((f32[16,104,128]{2,1,0:T(8,128)}), f32[16,104,128]{2,1,0:T(8,128)S(1)}, u32[]{:S(2)}, u32[]{:S(2)}) async-start(f32[16,104,128]{2,1,0:T(8,128)} %get-tuple-element.29), calls=%async_computation | async-start | bytes 1703936 | tf_op jit(solution)/shard_map/all_to_all | solution.py:735
  16.1 0.0 copy-done.2
  16.1 0.0 copy-start
  16.1 7.3 %forward0.1 = (bf16[1,1536,384]{2,1,0:T(8,128)(2,1)}, f32[8,384]{1,0:T(8,128)}) custom-call(f32[6,24,256]{2,1,0:T(8,128)} %get-tuple-element.49.rows_ref.rows_hbm, f32[1,3,128,256]{3,2,1,0:T(8,128)} %root_ref.1, f32[1,384]{1,0:T(1,128)S(1)} %reshape.7.gain_ref, bf16[3,1,1536,384]{3,2,1,0:T(8,128)(2,1)} %x_ref.3, bf16[3,1,1536,384]{3,2,1,0:T(8,128)(2,1)} %gate_ref.3, ...), custom_call_target="tpu_custom_call" | custom-call | flops 6000000000 | bytes 18000000 | tf_op jit(solution)/shard_map/forward0/pallas_call | solution.py:738
  23.4 7.8 %all-to-all-done.got_ref = f32[16,104,128]{2,1,0:T(8,128)S(1)} async-done(((f32[16,104,128]{2,1,0:T(8,128)}), f32[16,104,128]{2,1,0:T(8,128)S(1)}, u32[]{:S(2)}, u32[]{:S(2)}) %all-to-all-start) | async-done | bytes 852000 | tf_op jit(solution)/shard_map/all_to_all | solution.py:735
  31.3 0.0 copy-done
  31.3 1.5 %pick.1 = f32[16,96,128]{2,1,0:T(8,128)} custom-call(s32[2,16]{1,0:T(2,128)S(1)} %copy-done, f32[16,104,128]{2,1,0:T(8,128)S(1)} %all-to-all-done.got_ref), custom_call_target="tpu_custom_call" | custom-call | flops 1000000000 | bytes 3000000 | tf_op jit(solution)/shard_map/pick/pallas_call | solution.py:759
  32.8 3.6 %all-to-all-start.1 = ((f32[16,96,128]{2,1,0:T(8,128)}), f32[16,96,128]{2,1,0:T(8,128)S(1)}, u32[]{:S(2)}, u32[]{:S(2)}) async-start(f32[16,96,128]{2,1,0:T(8,128)} %pick.1), calls=%async_computation.1 | async-start | bytes 1572864 | tf_op jit(solution)/shard_map/all_to_all | solution.py:770
  36.4 0.0 copy-start.1
  36.4 10.1 %local.1 = (bf16[2,1536,384]{2,1,0:T(8,128)(2,1)}, bf16[2,1536,256]{2,1,0:T(8,128)(2,1)}) custom-call(f32[6,24,256]{2,1,0:T(8,128)} %get-tuple-element.49.rows_ref.rows_hbm, bf16[3,1,1536,384]{3,2,1,0:T(8,128)(2,1)} %x_ref.3, bf16[3,1,1536,256]{3,2,1,0:T(8,128)(2,1)} %b_hbm.3, bf16[3,1,1536,256]{3,2,1,0:T(8,128)(2,1)} %c_ref.7), custom_call_target="tpu_custom_call" | custom-call | flops 7000000000 | bytes 21000000 | tf_op jit(solution)/shard_map/local/pallas_call | solution.py:773
  46.5 2.8 %all-to-all-done.1.start_ref = f32[16,96,128]{2,1,0:T(8,128)S(1)} async-done(((f32[16,96,128]{2,1,0:T(8,128)}), f32[16,96,128]{2,1,0:T(8,128)S(1)}, u32[]{:S(2)}, u32[]{:S(2)}) %all-to-all-start.1) | async-done | bytes 786464 | tf_op jit(solution)/shard_map/all_to_all | solution.py:770
  49.2 0.0 copy-done.1
  49.2 8.8 %readout.1 = (bf16[2,1536,384]{2,1,0:T(8,128)(2,1)S(1)}, bf16[2,1536,384]{2,1,0:T(8,128)(2,1)S(1)}, bf16[2,1536,384]{2,1,0:T(8,128)(2,1)S(1)}, bf16[2,1536,256]{...) custom-call(bf16[2,1536,384]{2,1,0:T(8,128)(2,1)} %get-tuple-element.34.local_hbm, ...), custom_call_target="tpu_custom_call" | custom-call | flops 5000000000 | bytes 15000000 | tf_op jit(solution)/shard_map/readout/pallas_call | solution.py:792
  58.1 12.2 %all_to_all.25.total_ref = f32[8,8,1152]{2,1,0:T(8,128)S(1)} all-to-all(f32[8,8,1152]{2,1,0:T(8,128)} %get-tuple-element.43), channel_id=1, replica_groups=mesh['seg'=16,'head'=8] {'head'}, dimensions={0} | all-to-all | bytes 589824 | tf_op jit(solution)/shard_map/all_to_all | solution.py:827
  70.3 5.2 %grads.1 = (bf16[2,1536,384]{2,1,0:T(8,128)(2,1)}, f32[16,96,128]{2,1,0:T(8,128)}) custom-call(f32[4,256,128]{2,1,0:T(8,128)S(1)} %get-tuple-element.38.packed_ref, bf16[2,1536,256]{2,1,0:T(8,128)(2,1)S(1)} %get-tuple-element.39.turned_ref, bf16[2,1536,384]{2,1,0:T(8,128)(2,1)S(1)} %get-tuple-element.40.gate_ref, ...), custom_call_target="tpu_custom_call" | custom-call | flops 5000000000 | bytes 15000000 | tf_op jit(solution)/shard_map/grads/pallas_call | solution.py:829
  75.5 4.4 %all-to-all-start.3 = ((f32[16,96,128]{2,1,0:T(8,128)}), f32[16,96,128]{2,1,0:T(8,128)S(1)}, u32[]{:S(2)}, u32[]{:S(2)}) async-start(f32[16,96,128]{2,1,0:T(8,128)} %get-tuple-element.44), calls=%async_computation.3 | async-start | bytes 1572864 | tf_op jit(solution)/shard_map/all_to_all | solution.py:846
  79.9 7.8 %back0.1 = (bf16[3,1,1536,384]{3,2,1,0:T(8,128)(2,1)}, f32[3,1,3,128,256]{4,3,2,1,0:T(8,128)}) custom-call(f32[6,24,256]{2,1,0:T(8,128)} %get-tuple-element.49.rows_ref.rows_hbm, f32[1,384]{1,0:T(1,128)S(1)} %reshape.7.gain_ref, f32[8,8,1152]{2,1,0:T(8,128)S(1)} %all_to_all.25.total_ref, bf16[3,1,1536,384]{3,2,1,0:T(8,128)(2,1)} %gate_ref.3, ...), custom_call_target="tpu_custom_call" | custom-call | flops 6000000000 | bytes 18000000 | tf_op jit(solution)/shard_map/back0/pallas_call | solution.py:849
  87.7 6.7 %all-to-all-done.3.got_ref = f32[16,96,128]{2,1,0:T(8,128)S(1)} async-done(((f32[16,96,128]{2,1,0:T(8,128)}), f32[16,96,128]{2,1,0:T(8,128)S(1)}, u32[]{:S(2)}, u32[]{:S(2)}) %all-to-all-start.3) | async-done | bytes 786464 | tf_op jit(solution)/shard_map/all_to_all | solution.py:846
  94.4 1.7 %fold.1 = f32[16,96,128]{2,1,0:T(8,128)} custom-call(s32[2,16]{1,0:T(2,128)S(1)} %copy-done, f32[16,8,128]{2,1,0:T(8,128)S(1)} %slice.3.decay_ref, f32[16,96,128]{2,1,0:T(8,128)S(1)} %all-to-all-done.3.got_ref), custom_call_target="tpu_custom_call" | custom-call | flops 1000000000 | bytes 3000000 | tf_op jit(solution)/shard_map/fold/pallas_call | solution.py:870
  96.1 3.6 %all-to-all-start.4 = ((f32[16,96,128]{2,1,0:T(8,128)}), f32[16,96,128]{2,1,0:T(8,128)S(1)}, u32[]{:S(2)}, u32[]{:S(2)}) async-start(f32[16,96,128]{2,1,0:T(8,128)} %fold.1), calls=%async_computation.4 | async-start | bytes 1572864 | tf_op jit(solution)/shard_map/all_to_all | solution.py:881
  99.7 10.6 %back.1 = (bf16[3,1,1536,384]{3,2,1,0:T(8,128)(2,1)}, f32[3,1,3,128,256]{4,3,2,1,0:T(8,128)}) custom-call(f32[6,24,256]{2,1,0:T(8,128)} %get-tuple-element.49.rows_ref.rows_hbm, bf16[2,1536,384]{2,1,0:T(8,128)(2,1)} %get-tuple-element.50.grad_ref, bf16[3,1,1536,256]{3,2,1,0:T(8,128)(2,1)} %b_hbm.3, ...), custom_call_target="tpu_custom_call", output_to_operand_aliasing={{0}: (4, {}), {1}: (5, {})} | custom-call | flops 8000000000 | bytes 24000000 | tf_op jit(solution)/shard_map/back/pallas_call | solution.py:884
  110.3 2.4 %all-to-all-done.4.end_ref = f32[16,96,128]{2,1,0:T(8,128)S(1)} async-done(((f32[16,96,128]{2,1,0:T(8,128)}), f32[16,96,128]{2,1,0:T(8,128)S(1)}, u32[]{:S(2)}, u32[]{:S(2)}) %all-to-all-start.4) | async-done | bytes 786464 | tf_op jit(solution)/shard_map/all_to_all | solution.py:881
  112.8 5.7 %inputs.1 = (bf16[3,1,1536,384]{3,2,1,0:T(8,128)(2,1)}, f32[3,1,3,128,256]{4,3,2,1,0:T(8,128)}) custom-call(bf16[3,1,1536,256]{3,2,1,0:T(8,128)(2,1)} %b_hbm.3, bf16[3,1,1536,384]{3,2,1,0:T(8,128)(2,1)} %get-tuple-element.53.partial_hbm, f32[3,1,3,128,256]{4,3,2,1,0:T(8,128)} %get-tuple-element.54.local_hbm, ...), custom_call_target="tpu_custom_call", output_to_operand_aliasing={{0}: (1, {}), {1}: (2, {})} | custom-call | flops 4000000000 | bytes 12000000 | tf_op jit(solution)/shard_map/inputs/pallas_call | solution.py:903
  (2 shorter events, 0.0 us)
Async XLA Ops:
  0.6 15.5 %copy-start.2 = (f32[384]{0:T(512)S(1)}, f32[384]{0:T(512)}, u32[]{:S(2)}) copy-start(f32[384]{0:T(512)} %param.15) | copy-start | bytes 4612
  7.9 23.3 %all-to-all-start = ((f32[16,104,128]{2,1,0:T(8,128)}), f32[16,104,128]{2,1,0:T(8,128)S(1)}, u32[]{:S(2)}, u32[]{:S(2)}) async-start(f32[16,104,128]{2,1,0:T(8,128)} %get-tuple-element.29), calls=%async_computation | async-start | bytes 1703936 | tf_op jit(solution)/shard_map/all_to_all | solution.py:735
  16.1 15.2 %copy-start = (s32[2,16]{1,0:T(2,128)S(1)}, s32[2,16]{1,0:T(2,128)}, u32[]{:S(2)}) copy-start(s32[2,16]{1,0:T(2,128)} %parent_ref.3) | copy-start | bytes 388
  32.8 16.5 %all-to-all-start.1 = ((f32[16,96,128]{2,1,0:T(8,128)}), f32[16,96,128]{2,1,0:T(8,128)S(1)}, u32[]{:S(2)}, u32[]{:S(2)}) async-start(f32[16,96,128]{2,1,0:T(8,128)} %pick.1), calls=%async_computation.1 | async-start | bytes 1572864 | tf_op jit(solution)/shard_map/all_to_all | solution.py:770
  36.4 12.8 %copy-start.1 = (f32[8,384]{1,0:T(8,128)S(1)}, f32[8,384]{1,0:T(8,128)}, u32[]{:S(2)}) copy-start(f32[8,384]{1,0:T(8,128)} %get-tuple-element.37.first_sums_ref) | copy-start | bytes 36868
  75.5 18.9 %all-to-all-start.3 = ((f32[16,96,128]{2,1,0:T(8,128)}), f32[16,96,128]{2,1,0:T(8,128)S(1)}, u32[]{:S(2)}, u32[]{:S(2)}) async-start(f32[16,96,128]{2,1,0:T(8,128)} %get-tuple-element.44), calls=%async_computation.3 | async-start | bytes 1572864 | tf_op jit(solution)/shard_map/all_to_all | solution.py:846
  96.1 16.6 %all-to-all-start.4 = ((f32[16,96,128]{2,1,0:T(8,128)}), f32[16,96,128]{2,1,0:T(8,128)S(1)}, u32[]{:S(2)}, u32[]{:S(2)}) async-start(f32[16,96,128]{2,1,0:T(8,128)} %fold.1), calls=%async_computation.4 | async-start | bytes 1572864 | tf_op jit(solution)/shard_map/all_to_all | solution.py:881

commit v2 on v1

--- a/solution.py
+++ b/solution.py
@@ -140,12 +140,10 @@
     return lasts, before, after
 
 
-def states_body(heads, steps, decay_hbm, root_hbm, x_hbm, b_hbm, send_out, rows_ref, rates, decay,
-                send, root, x, b, decay_sem, root_sem, sems, out_sems):
-    chunks = rows_ref.shape[0]
+def states_body(heads, steps, decay, root_hbm, x_hbm, b_hbm, send_out, rows_out, rates, rows, send,
+                root, x, b, root_sem, sems, out_sems):
+    chunks = rows.shape[0]
     blocks = steps * CHUNK
-    decay_copy = pltpu.make_async_copy(decay_hbm, decay, decay_sem)
-    decay_copy.start()
     pieces = [(0, 0, CHUNK), (0, CHUNK, CHUNK), (1, 0, CHUNK), (1, CHUNK, CHUNK)]
     copies = piece_copies(
         [lambda at, span: x_hbm.at[at, 0, span], lambda at, span: b_hbm.at[at, 0, span]],
@@ -154,13 +152,10 @@
         pieces,
     )
     root_copy = pltpu.make_async_copy(root_hbm.at[0], root, root_sem)
+    root_copy.start()
     start_all(copies[0])
-    root_copy.start()
-    for some in copies[1:]:
-        start_all(some)
 
     rates[...] = jnp.zeros_like(rates)
-    decay_copy.wait()
     for level in range(decay.shape[0]):
         for number in range(blocks):
             for h in range(heads):
@@ -179,7 +174,9 @@
         sums = sums + dot(part, upper, 1, 0)
     sums = sums * -LOG2E
     for chunk in range(chunks):
-        rows_ref[chunk] = sums[WIDTH * chunk : WIDTH * (chunk + 1)]
+        rows[chunk] = sums[WIDTH * chunk : WIDTH * (chunk + 1)]
+    outs = [pltpu.make_async_copy(rows, rows_out, out_sems.at[2])]
+    outs[0].start()
 
     lines = []
     totals = []
@@ -194,9 +191,9 @@
     to_level = jnp.concatenate(lines, axis=0).T
 
     root_copy.wait()
+    start_all(copies[1])
     state = jnp.concatenate([(root[h] * totals[0][h : h + 1]).T for h in range(heads)], axis=1)
     half = heads * STATE // send.shape[0]
-    outs = []
     for i, (level, first, count) in enumerate(pieces):
         if (level, first) == (1, 0):
             scatter_pieces(send, 0, state, heads)
@@ -204,9 +201,12 @@
             outs.append(
                 pltpu.make_async_copy(send.at[:, part], send_out.at[:, part], out_sems.at[0])
             )
-            outs[0].start()
+            outs[-1].start()
             state = jnp.zeros((STATE, heads * HDIM), F32)
         wait_all(copies[i])
+        if i > 0:
+            start_all(sum(copies[i + 1 : i + 2], []))
+        turned, decayed = [], []
         for number in range(first, first + count):
             at = 8 * (level * blocks + number)
             scale = jnp.concatenate(
@@ -216,15 +216,18 @@
                 ],
                 axis=1,
             )
-            decayed = (x[level, block(number)].astype(F32) * scale).astype(BF16)
-            state = state + dot(turn(b[level, block(number)]), decayed, 1, 0)
+            decayed.append((x[level, block(number)].astype(F32) * scale).astype(BF16))
+            turned.append(turn(b[level, block(number)]))
+        state = state + dot(
+            jnp.concatenate(turned, axis=1), jnp.concatenate(decayed, axis=0), 1, 0
+        )
     scatter_pieces(send, 1, state, heads)
     decays = jnp.broadcast_to(totals[1], (8, HDIM))
     for piece in range(send.shape[0]):
         send[piece, send.shape[1] - 8 :] = decays
     part = pl.ds(half, send.shape[1] - half)
     outs.append(pltpu.make_async_copy(send.at[:, part], send_out.at[:, part], out_sems.at[1]))
-    outs[1].start()
+    outs[-1].start()
     wait_all(outs)
 
 
@@ -355,11 +358,13 @@
 
 
 def gated_sums(ssm_out, gate, out_grad, gain):
-    gated = ssm_out * silu(gate.astype(F32))
+    act = silu(gate.astype(F32))
+    gated = ssm_out * act
     scaled = out_grad.astype(F32) * gain
     squares = jnp.sum(gated * gated, axis=1, keepdims=True)
     products = jnp.sum(scaled * gated, axis=1, keepdims=True)
-    return gated, jnp.concatenate([squares, products, jnp.zeros((BLOCK, 6), F32)], axis=1).T
+    pair = jnp.concatenate([squares, products, jnp.zeros((BLOCK, 6), F32)], axis=1).T
+    return gated, scaled * act, gated * act, pair
 
 
 def store_sums(sums, step, at, pairs):
@@ -403,14 +408,14 @@
         x, b, c = x_ref[0, 0, block(j)], b_ref[0, 0, block(j)], c_ref[0, 0, block(j)]
         within = weighted(heads, j, rows, packed, x, b, c)
         carried = dot(c, current.astype(BF16), 1, 0) * spread(packed, FROM_BLOCK, j, heads)
-        gated, pair = gated_sums(
+        gated, _, _, pair = gated_sums(
             within + carried, gate_ref[0, 0, block(j)], out_grad_ref[0, 0, block(j)], gain_ref[...]
         )
         gated_ref[0, block(j)] = gated.astype(BF16)
         pairs.append(pair)
         decayed = (x.astype(F32) * spread(packed, TO_BLOCK, j, heads)).astype(BF16)
         factor = spread(packed[BLOCK - 1 :], FROM_BLOCK, j, heads)
-        current = current * factor + dot(turn(b), decayed, 1, 0)
+        current = current * factor + dot(b, decayed, 0, 0)
     state[...] = current
     for part in range(steps):
 
@@ -434,16 +439,16 @@
         within = weighted(heads, j, rows, packed, x, b, c)
         carried = dot(c, current.astype(BF16), 1, 0) * spread(packed, FROM_BLOCK, j, heads)
         out_ref[0, block(j)] = (within + carried).astype(BF16)
-        turned_ref[0, block(j)] = turn(c)
+        turned_ref[0, :, block(j)] = turn(c)
         decayed = (x.astype(F32) * spread(packed, TO_BLOCK, j, heads)).astype(BF16)
         factor = spread(packed[BLOCK - 1 :], FROM_BLOCK, j, heads)
-        current = current * factor + dot(turn(b), decayed, 1, 0)
+        current = current * factor + dot(b, decayed, 0, 0)
     state[...] = current
 
 
 def readout_body(heads, steps, local_hbm, gate_hbm, c_hbm, out_grad_hbm, turned_hbm, rows_hbm,
-                 start_ref, gain_ref, first_sums_ref, gated_ref, gate, out_grad, turned, packed,
-                 sums_out, local, c, rows, sums, sems, rows_sem, turned_sem, out_sem):
+                 start_ref, gain_ref, first_sums_ref, scaled_act, gated_act, turned, packed,
+                 sums_out, local, gate, out_grad, c, rows, sums, sems, rows_sem, turned_sem, out_sem):
     rows_copy = pltpu.make_async_copy(rows_hbm.at[pl.ds(steps, 2 * steps)], rows, rows_sem)
     rows_copy.start()
     half = CHUNK * steps // 2
@@ -459,14 +464,14 @@
         sems,
         pieces,
     )
-    for some in copies:
-        start_all(some)
     turned_copy = pltpu.make_async_copy(turned_hbm, turned, turned_sem)
-    turned_copy.start()
+    copies.append([turned_copy])
+    start_all(copies[0] + copies[1])
     sums[0, :, :FOLD] = first_sums_ref[...]
     rows_copy.wait()
     for at in range(2):
         pack(rows.at[pl.ds(at * steps, steps)], packed.at[pl.ds(at * steps, steps)])
+    start_all(copies[2])
     pairs = []
     for i, (at, first, count) in enumerate(pieces):
         if first == 0:
@@ -474,18 +479,19 @@
                 [gather_pieces(start_ref, at, h, heads) for h in range(heads)], axis=1
             ).astype(BF16)
         wait_all(copies[i])
+        start_all(sum(copies[i + 3 : i + 4], []))
+        piece = dot(c[at, first * BLOCK : (first + count) * BLOCK], start, 1, 0)
         for number in range(first, first + count):
             step, j = number // CHUNK, number % CHUNK
             place = block(number)
-            carried = dot(c[at, place], start, 1, 0)
+            carried = piece[block(number - first)]
             carried = carried * spread(packed[at * steps + step], FROM_LEVEL, j, heads)
-            gated, pair = gated_sums(
+            _, scaled_act[at, place], gated_act[at, place], pair = gated_sums(
                 carried + local[at, place].astype(F32),
                 gate[at, place],
                 out_grad[at, place],
                 gain_ref[...],
             )
-            gated_ref[at, place] = gated.astype(BF16)
             pairs.append(pair)
             if j == CHUNK - 1:
                 store_sums(sums.at[0], step, (at + 1) * FOLD, pairs)
@@ -498,8 +504,8 @@
     out.wait()
 
 
-def grads_body(heads, steps, features, packed_ref, turned_ref, gate_ref, out_grad_ref, gated_ref,
-               total_ref, gain_ref, grad_out, send_out, grads, send, grad_sems, sems):
+def grads_body(heads, steps, features, packed_ref, turned_ref, scaled_act_ref, gated_act_ref,
+               total_ref, grad_out, send_out, grads, send, grad_sems, sems):
     total = jnp.sum(total_ref[...], axis=0)
     half = send.shape[1] // 2
     outs = []
@@ -508,19 +514,20 @@
         for step in range(steps):
             packed = packed_ref[at * steps + step]
             norm = norm_columns(total, step, (at + 1) * FOLD, features)
+            decayed = []
             for j in range(CHUNK):
                 place = block(step * CHUNK + j)
-                grad = ssm_gradient(
-                    j,
-                    norm,
-                    gain_ref[...],
-                    gate_ref[at, place],
-                    out_grad_ref[at, place],
-                    gated_ref[at, place],
+                inv_rms, back = norm[block(j), 0:1], norm[block(j), 1:2]
+                grad = inv_rms * scaled_act_ref[at, place] - back * gated_act_ref[at, place]
+                grad = grad.astype(BF16)
+                grads[at, place] = grad
+                decayed.append(
+                    (grad.astype(F32) * spread(packed, FROM_LEVEL, j, heads)).astype(BF16)
                 )
-                grads[at, place] = grad
-                decayed = (grad.astype(F32) * spread(packed, FROM_LEVEL, j, heads)).astype(BF16)
-                state = state + dot(turned_ref[at, place], decayed, 1, 0)
+            span = slice(step * SPAN, (step + 1) * SPAN)
+            state = state + dot(
+                turned_ref[at, :, span], jnp.concatenate(decayed, axis=0), 1, 0
+            )
             span = pl.ds(step * SPAN, SPAN)
             outs.append(
                 pltpu.make_async_copy(
@@ -545,7 +552,7 @@
         yield j, (within + carried).astype(BF16)
         decayed = (grad.astype(F32) * spread(packed, FROM_BLOCK, j, heads)).astype(BF16)
         factor = spread(packed[BLOCK - 1 :], FROM_BLOCK, j, heads)
-        current = current * factor + dot(turn(c), decayed, 1, 0)
+        current = current * factor + dot(c, decayed, 0, 0)
     state[...] = current
 
 
@@ -621,9 +628,9 @@
         for level in range(2)
     ]
     for i, (level, first, _) in enumerate(pieces):
-        start_all(copies[i])
         if first == half:
-            locals_in[level].start()
+            copies[i].append(locals_in[level])
+    start_all(copies[0] + copies[1] + copies[2])
     rows_copy.wait()
     for level in range(2):
         pack(rows.at[pl.ds(level * steps, steps)], packed.at[pl.ds(level * steps, steps)])
@@ -635,9 +642,11 @@
             )
             rounded = end.astype(BF16)
         wait_all(copies[i])
+        start_all(sum(copies[i + 3 : i + 4], []))
+        piece = dot(b[level, first * BLOCK : (first + count) * BLOCK], rounded, 1, 0)
         for number in range(first, first + count):
             place = block(number)
-            extra = dot(b[level, place], rounded, 1, 0) * spread(
+            extra = piece[block(number - first)] * spread(
                 packed[level * steps + number // CHUNK], TO_LEVEL, number % CHUNK, heads
             )
             grads[level, place] = (partial[level, place].astype(F32) + extra).astype(BF16)
@@ -651,7 +660,6 @@
         if first == half:
             last = packed[(level + 1) * steps - 1, BLOCK - 1 :]
             total = spread(last, FROM_LEVEL, CHUNK - 1, heads)
-            locals_in[level].wait()
             for h in range(heads):
                 states[level, h] += (end[:, head(h)] * total[:, head(h)]).T
             outs.append(
@@ -690,7 +698,8 @@
 
     far = lambda array: pin(array, pltpu.HBM)
     near = lambda array: pin(array, pltpu.VMEM)
-    decay, x, gate, out_grad = far(decay), far(ssm_input), far(gate_input), far(out_grad)
+    x, gate, out_grad = far(ssm_input), far(gate_input), far(out_grad)
+    decay = near(decay)
     b, c, root = far(b_input), far(c_output), far(root_state)
 
     def pair_of_levels(width):
@@ -716,20 +725,19 @@
         functools.partial(states_body, heads, steps),
         "states",
         6,
-        in_specs=[anywhere] * 4,
-        out_specs=[anywhere, vmem],
+        in_specs=[vmem] + [anywhere] * 3,
+        out_specs=[anywhere, anywhere],
         out_shape=[pltpu.HBM(first_shape, F32), pltpu.HBM(rows_shape, F32)],
         scratch_shapes=[
             pltpu.VMEM((levels * blocks * 8, BLOCK), F32),
-            pltpu.VMEM(decay.shape, F32),
+            pltpu.VMEM(rows_shape, F32),
             pltpu.VMEM(first_shape, F32),
             pltpu.VMEM(root_state.shape[1:], F32),
             pair_of_levels(columns),
             pair_of_levels(STATE),
             dma,
-            dma,
             dma((4, 2)),
-            dma((2,)),
+            dma((3,)),
         ],
     )(decay, root, x, b)
     got = exchange(send)
@@ -781,29 +789,33 @@
             tokens(STATE, later),
             tokens(STATE, later),
         ],
-        out_specs=[flat(columns, both), flat(BLOCK, both)],
+        out_specs=[
+            flat(columns, both),
+            pl.BlockSpec((1, STATE, SPAN), lambda l, k: (l, 0, k)),
+        ],
         out_shape=[
             pltpu.HBM((2, length, columns), BF16),
-            pltpu.HBM((2, blocks * STATE, BLOCK), BF16),
+            pltpu.HBM((2, STATE, length), BF16),
         ],
         scratch_shapes=[state_scratch, packs_scratch],
     )(far(late_rows), x, b, c)
 
-    gated, gate_near, out_grad_near, turned_near, packed, sums = call(
+    scaled_act, gated_act, turned, packed, sums = call(
         functools.partial(readout_body, heads, steps),
         "readout",
         5,
         in_specs=[anywhere] * 6 + [vmem] * 3,
-        out_specs=[vmem] * 5 + [anywhere],
+        out_specs=[vmem] * 4 + [anywhere],
         out_shape=[
+            pltpu.VMEM((2, length, columns), F32),
+            pltpu.VMEM((2, length, columns), F32),
+            pltpu.VMEM((2, STATE, length), BF16),
+            pltpu.VMEM(two_levels, F32),
+            pltpu.HBM(sums_shape, F32),
+        ],
+        scratch_shapes=[
             pair_of_levels(columns),
             pair_of_levels(columns),
-            pair_of_levels(columns),
-            pair_of_levels(BLOCK),
-            pltpu.VMEM(two_levels, F32),
-            pltpu.HBM(sums_shape, F32),
-        ],
-        scratch_shapes=[
             pair_of_levels(columns),
             pair_of_levels(STATE),
             pltpu.VMEM((2 * steps,) + rows_shape[1:], F32),
@@ -829,20 +841,12 @@
     grads, send_back = call(
         functools.partial(grads_body, heads, steps, features),
         "grads",
-        5,
-        in_specs=[vmem] * 7,
+        4,
+        in_specs=[vmem] * 5,
         out_specs=[anywhere, anywhere],
         out_shape=[pltpu.HBM((2, length, columns), BF16), pltpu.HBM(pair_shape, F32)],
         scratch_shapes=[pair_of_levels(columns), pair_scratch, dma((2 * steps,)), dma((2,))],
-    )(
-        near(packed),
-        near(turned_near),
-        near(gate_near),
-        near(out_grad_near),
-        near(gated),
-        near(totals),
-        gain,
-    )
+    )(near(packed), near(turned), near(scaled_act), near(gated_act), near(totals))
     got_back = exchange(send_back)
 
     own_back = lambda k: (0, steps - 1 - k)

time: 119 us -> 117 us (0.983)
  Pallas kernels: 65.9 us -> 61.4 us
  waiting for transfers between devices: 19.7 us -> 21.6 us
    pallas_call x1, Pallas kernels: 8.82 us -> 7.22 us  [shards(): call(functools.partial(readout_body, heads, steps), 'readout', 5, in_spec...]
    all_to_all x1, waiting for transfers between devices: 2.45 us -> 3.81 us  [shards(): ends = exchange(folded)]
where the time goes in v2:
time: 117 us; the launch traced here: 116 us
  Pallas kernels  61.4 us (52%)
  waiting for transfers between devices  21.6 us (18%)
  starting transfers between devices  19 us (16%)
  blocking collectives  12.2 us (10%)
    all_to_all x1, blocking collectives, shards(): lax.all_to_all(sums, 'head', split_axis=0, concat_axis=0, tiled=True)  12.2 us
    pallas_call x1, Pallas kernels, shards(): call(functools.partial(back_body, heads, steps), 'back', 8, grid=(2, step...  9.5 us
    pallas_call x1, Pallas kernels, shards(): call(functools.partial(local_body, heads, steps), 'local', 7, grid=(2, st...  9.01 us
    pallas_call x1, Pallas kernels, shards(): call(functools.partial(forward0_body, heads, steps), 'forward0', 6, grid=...  8.41 us
    all_to_all x1, starting transfers between devices, shards(): got = exchange(send)  8.14 us
    pallas_call x1, Pallas kernels, shards(): call(functools.partial(back0_body, heads, steps, features), 'back0', 6, g...  7.68 us
    pallas_call x1, Pallas kernels, shards(): call(functools.partial(readout_body, heads, steps), 'readout', 5, in_spec...  7.22 us
    all_to_all x1, waiting for transfers between devices, shards(): got_back = exchange(send_back)  7.2 us
  transfers between devices with their start and end apart: 4, of which 4 were waited for; matrix products, arithmetic and copies ran while one was open for 0% of the time, Pallas kernels for 30%

profile of v2, /device:TPU:0, one launch (start us, length us, event | category | flops | bytes accessed | tf_op | source)
XLA Modules:
  0.0 116.0 jit_solution(14135200327285762836)
XLA Ops:
  0.6 0.0 copy-start
  0.6 0.8 copy-done
  1.4 0.0 copy-start.3
  1.4 6.6 %states.1 = (f32[16,104,128]{2,1,0:T(8,128)}, f32[6,24,256]{2,1,0:T(8,128)}) custom-call(f32[3,3,1,1536]{3,2,1,0:T(1,128)S(1)} %bitcast.1, f32[1,3,128,256]{3,2,1,0:T(8,128)} %root_ref.1, bf16[3,1,1536,384]{3,2,1,0:T(8,128)(2,1)} %x_ref.3, bf16[3,1,1536,256]{3,2,1,0:T(8,128)(2,1)} %b_hbm.3), custom_call_target="tpu_custom_call" | custom-call | flops 6000000000 | bytes 18000000 | tf_op jit(solution)/shard_map/states/pallas_call | solution.py:724
  8.0 8.1 %all-to-all-start = ((f32[16,104,128]{2,1,0:T(8,128)}), f32[16,104,128]{2,1,0:T(8,128)S(1)}, u32[]{:S(2)}, u32[]{:S(2)}) async-start(f32[16,104,128]{2,1,0:T(8,128)} %get-tuple-element.28), calls=%async_computation | async-start | bytes 1703936 | tf_op jit(solution)/shard_map/all_to_all | solution.py:743
  16.2 0.0 copy-done.3
  16.2 0.0 copy-start.1
  16.2 8.4 %forward0.1 = (bf16[1,1536,384]{2,1,0:T(8,128)(2,1)}, f32[8,384]{1,0:T(8,128)}) custom-call(f32[6,24,256]{2,1,0:T(8,128)} %get-tuple-element.47.rows_ref.rows_hbm, f32[1,3,128,256]{3,2,1,0:T(8,128)} %root_ref.1, f32[1,384]{1,0:T(1,128)S(1)} %reshape.7.gain_ref, bf16[3,1,1536,384]{3,2,1,0:T(8,128)(2,1)} %x_ref.3, bf16[3,1,1536,384]{3,2,1,0:T(8,128)(2,1)} %gate_ref.3, ...), custom_call_target="tpu_custom_call" | custom-call | flops 6000000000 | bytes 18000000 | tf_op jit(solution)/shard_map/forward0/pallas_call | solution.py:746
  24.6 6.8 %all-to-all-done.got_ref = f32[16,104,128]{2,1,0:T(8,128)S(1)} async-done(((f32[16,104,128]{2,1,0:T(8,128)}), f32[16,104,128]{2,1,0:T(8,128)S(1)}, u32[]{:S(2)}, u32[]{:S(2)}) %all-to-all-start) | async-done | bytes 852000 | tf_op jit(solution)/shard_map/all_to_all | solution.py:743
  31.4 0.0 copy-done.1
  31.4 1.5 %pick.1 = f32[16,96,128]{2,1,0:T(8,128)} custom-call(s32[2,16]{1,0:T(2,128)S(1)} %copy-done.1, f32[16,104,128]{2,1,0:T(8,128)S(1)} %all-to-all-done.got_ref), custom_call_target="tpu_custom_call" | custom-call | flops 1000000000 | bytes 3000000 | tf_op jit(solution)/shard_map/pick/pallas_call | solution.py:767
  32.9 3.6 %all-to-all-start.1 = ((f32[16,96,128]{2,1,0:T(8,128)}), f32[16,96,128]{2,1,0:T(8,128)S(1)}, u32[]{:S(2)}, u32[]{:S(2)}) async-start(f32[16,96,128]{2,1,0:T(8,128)} %pick.1), calls=%async_computation.1 | async-start | bytes 1572864 | tf_op jit(solution)/shard_map/all_to_all | solution.py:778
  36.5 0.0 copy-start.2
  36.5 9.0 %local.1 = (bf16[2,1536,384]{2,1,0:T(8,128)(2,1)}, bf16[2,256,1536]{2,1,0:T(8,128)(2,1)}) custom-call(f32[6,24,256]{2,1,0:T(8,128)} %get-tuple-element.47.rows_ref.rows_hbm, bf16[3,1,1536,384]{3,2,1,0:T(8,128)(2,1)} %x_ref.3, bf16[3,1,1536,256]{3,2,1,0:T(8,128)(2,1)} %b_hbm.3, bf16[3,1,1536,256]{3,2,1,0:T(8,128)(2,1)} %c_ref.7), custom_call_target="tpu_custom_call" | custom-call | flops 7000000000 | bytes 21000000 | tf_op jit(solution)/shard_map/local/pallas_call | solution.py:781
  45.5 3.8 %all-to-all-done.1.start_ref = f32[16,96,128]{2,1,0:T(8,128)S(1)} async-done(((f32[16,96,128]{2,1,0:T(8,128)}), f32[16,96,128]{2,1,0:T(8,128)S(1)}, u32[]{:S(2)}, u32[]{:S(2)}) %all-to-all-start.1) | async-done | bytes 786464 | tf_op jit(solution)/shard_map/all_to_all | solution.py:778
  49.4 0.0 copy-done.2
  49.4 7.2 %readout.1 = (f32[2,1536,384]{2,1,0:T(8,128)S(1)}, f32[2,1536,384]{2,1,0:T(8,128)S(1)}, bf16[2,256,1536]{2,1,0:T(8,128)(2,1)S(1)}, f32[4,256,128]{2,1,0:T(8,128)S(1)}, f32[8,8,1152]{2,1,0:T(8,128)}) custom-call(bf16[2,1536,384]{2,1,0:T(8,128)(2,1)} %get-tuple-element.33.local_hbm, bf16[3,1,1536,384]{3,2,1,0:T(8,128)(2,1)} %gate_ref.3, ...), custom_call_target="tpu_custom_call" | custom-call | flops 5000000000 | bytes 15000000 | tf_op jit(solution)/shard_map/readout/pallas_call | solution.py:803
  56.6 12.2 %all_to_all.25.total_ref = f32[8,8,1152]{2,1,0:T(8,128)S(1)} all-to-all(f32[8,8,1152]{2,1,0:T(8,128)} %get-tuple-element.41), channel_id=1, replica_groups=mesh['seg'=16,'head'=8] {'head'}, dimensions={0} | all-to-all | bytes 589824 | tf_op jit(solution)/shard_map/all_to_all | solution.py:839
  68.8 4.8 %grads.1 = (bf16[2,1536,384]{2,1,0:T(8,128)(2,1)}, f32[16,96,128]{2,1,0:T(8,128)}) custom-call(f32[4,256,128]{2,1,0:T(8,128)S(1)} %get-tuple-element.37.packed_ref, bf16[2,256,1536]{2,1,0:T(8,128)(2,1)S(1)} %get-tuple-element.38.turned_ref, f32[2,1536,384]{2,1,0:T(8,128)S(1)} %get-tuple-element.39.scaled_act_ref, ...), custom_call_target="tpu_custom_call" | custom-call | flops 4000000000 | bytes 12000000 | tf_op jit(solution)/shard_map/grads/pallas_call | solution.py:841
  73.6 3.6 %all-to-all-start.3 = ((f32[16,96,128]{2,1,0:T(8,128)}), f32[16,96,128]{2,1,0:T(8,128)S(1)}, u32[]{:S(2)}, u32[]{:S(2)}) async-start(f32[16,96,128]{2,1,0:T(8,128)} %get-tuple-element.42), calls=%async_computation.3 | async-start | bytes 1572864 | tf_op jit(solution)/shard_map/all_to_all | solution.py:850
  77.2 7.7 %back0.1 = (bf16[3,1,1536,384]{3,2,1,0:T(8,128)(2,1)}, f32[3,1,3,128,256]{4,3,2,1,0:T(8,128)}) custom-call(f32[6,24,256]{2,1,0:T(8,128)} %get-tuple-element.47.rows_ref.rows_hbm, f32[1,384]{1,0:T(1,128)S(1)} %reshape.7.gain_ref, f32[8,8,1152]{2,1,0:T(8,128)S(1)} %all_to_all.25.total_ref, bf16[3,1,1536,384]{3,2,1,0:T(8,128)(2,1)} %gate_ref.3, ...), custom_call_target="tpu_custom_call" | custom-call | flops 6000000000 | bytes 18000000 | tf_op jit(solution)/shard_map/back0/pallas_call | solution.py:853
  84.9 7.2 %all-to-all-done.3.got_ref = f32[16,96,128]{2,1,0:T(8,128)S(1)} async-done(((f32[16,96,128]{2,1,0:T(8,128)}), f32[16,96,128]{2,1,0:T(8,128)S(1)}, u32[]{:S(2)}, u32[]{:S(2)}) %all-to-all-start.3) | async-done | bytes 786464 | tf_op jit(solution)/shard_map/all_to_all | solution.py:850
  92.1 1.7 %fold.1 = f32[16,96,128]{2,1,0:T(8,128)} custom-call(s32[2,16]{1,0:T(2,128)S(1)} %copy-done.1, f32[16,8,128]{2,1,0:T(8,128)S(1)} %slice.3.decay_ref, f32[16,96,128]{2,1,0:T(8,128)S(1)} %all-to-all-done.3.got_ref), custom_call_target="tpu_custom_call" | custom-call | flops 1000000000 | bytes 3000000 | tf_op jit(solution)/shard_map/fold/pallas_call | solution.py:874
  93.8 3.6 %all-to-all-start.4 = ((f32[16,96,128]{2,1,0:T(8,128)}), f32[16,96,128]{2,1,0:T(8,128)S(1)}, u32[]{:S(2)}, u32[]{:S(2)}) async-start(f32[16,96,128]{2,1,0:T(8,128)} %fold.1), calls=%async_computation.4 | async-start | bytes 1572864 | tf_op jit(solution)/shard_map/all_to_all | solution.py:885
  97.4 9.5 %back.1 = (bf16[3,1,1536,384]{3,2,1,0:T(8,128)(2,1)}, f32[3,1,3,128,256]{4,3,2,1,0:T(8,128)}) custom-call(f32[6,24,256]{2,1,0:T(8,128)} %get-tuple-element.47.rows_ref.rows_hbm, bf16[2,1536,384]{2,1,0:T(8,128)(2,1)} %get-tuple-element.48.grad_ref, bf16[3,1,1536,256]{3,2,1,0:T(8,128)(2,1)} %b_hbm.3, ...), custom_call_target="tpu_custom_call", output_to_operand_aliasing={{0}: (4, {}), {1}: (5, {})} | custom-call | flops 8000000000 | bytes 24000000 | tf_op jit(solution)/shard_map/back/pallas_call | solution.py:888
  106.9 3.8 %all-to-all-done.4.end_ref = f32[16,96,128]{2,1,0:T(8,128)S(1)} async-done(((f32[16,96,128]{2,1,0:T(8,128)}), f32[16,96,128]{2,1,0:T(8,128)S(1)}, u32[]{:S(2)}, u32[]{:S(2)}) %all-to-all-start.4) | async-done | bytes 786464 | tf_op jit(solution)/shard_map/all_to_all | solution.py:885
  110.7 5.1 %inputs.1 = (bf16[3,1,1536,384]{3,2,1,0:T(8,128)(2,1)}, f32[3,1,3,128,256]{4,3,2,1,0:T(8,128)}) custom-call(bf16[3,1,1536,256]{3,2,1,0:T(8,128)(2,1)} %b_hbm.3, bf16[3,1,1536,384]{3,2,1,0:T(8,128)(2,1)} %get-tuple-element.51.partial_hbm, f32[3,1,3,128,256]{4,3,2,1,0:T(8,128)} %get-tuple-element.52.local_hbm, ...), custom_call_target="tpu_custom_call", output_to_operand_aliasing={{0}: (1, {}), {1}: (2, {})} | custom-call | flops 4000000000 | bytes 12000000 | tf_op jit(solution)/shard_map/inputs/pallas_call | solution.py:907
  (2 shorter events, 0.0 us)
Async XLA Ops:
  0.6 0.8 copy-start
  1.4 14.7 %copy-start.3 = (f32[384]{0:T(512)S(1)}, f32[384]{0:T(512)}, u32[]{:S(2)}) copy-start(f32[384]{0:T(512)} %param.15) | copy-start | bytes 4612
  8.0 23.4 %all-to-all-start = ((f32[16,104,128]{2,1,0:T(8,128)}), f32[16,104,128]{2,1,0:T(8,128)S(1)}, u32[]{:S(2)}, u32[]{:S(2)}) async-start(f32[16,104,128]{2,1,0:T(8,128)} %get-tuple-element.28), calls=%async_computation | async-start | bytes 1703936 | tf_op jit(solution)/shard_map/all_to_all | solution.py:743
  16.2 15.2 %copy-start.1 = (s32[2,16]{1,0:T(2,128)S(1)}, s32[2,16]{1,0:T(2,128)}, u32[]{:S(2)}) copy-start(s32[2,16]{1,0:T(2,128)} %parent_ref.3) | copy-start | bytes 388
  32.9 16.5 %all-to-all-start.1 = ((f32[16,96,128]{2,1,0:T(8,128)}), f32[16,96,128]{2,1,0:T(8,128)S(1)}, u32[]{:S(2)}, u32[]{:S(2)}) async-start(f32[16,96,128]{2,1,0:T(8,128)} %pick.1), calls=%async_computation.1 | async-start | bytes 1572864 | tf_op jit(solution)/shard_map/all_to_all | solution.py:778
  36.5 12.8 %copy-start.2 = (f32[8,384]{1,0:T(8,128)S(1)}, f32[8,384]{1,0:T(8,128)}, u32[]{:S(2)}) copy-start(f32[8,384]{1,0:T(8,128)} %get-tuple-element.36.first_sums_ref) | copy-start | bytes 36868
  73.6 18.5 %all-to-all-start.3 = ((f32[16,96,128]{2,1,0:T(8,128)}), f32[16,96,128]{2,1,0:T(8,128)S(1)}, u32[]{:S(2)}, u32[]{:S(2)}) async-start(f32[16,96,128]{2,1,0:T(8,128)} %get-tuple-element.42), calls=%async_computation.3 | async-start | bytes 1572864 | tf_op jit(solution)/shard_map/all_to_all | solution.py:850
  93.8 16.9 %all-to-all-start.4 = ((f32[16,96,128]{2,1,0:T(8,128)}), f32[16,96,128]{2,1,0:T(8,128)S(1)}, u32[]{:S(2)}, u32[]{:S(2)}) async-start(f32[16,96,128]{2,1,0:T(8,128)} %fold.1), calls=%async_computation.4 | async-start | bytes 1572864 | tf_op jit(solution)/shard_map/all_to_all | solution.py:885

commit v3 on v2

--- a/solution.py
+++ b/solution.py
@@ -24,8 +24,6 @@
 CUM = 0
 FROM_BLOCK = WIDTH
 TO_BLOCK = 2 * WIDTH
-FROM_LEVEL = 3 * WIDTH
-TO_LEVEL = 4 * WIDTH
 
 F32 = jnp.float32
 BF16 = jnp.bfloat16
@@ -84,7 +82,7 @@
     unit = lax.broadcasted_iota(jnp.int32, (size, size), 0) == lax.broadcasted_iota(
         jnp.int32, (size, size), 1
     )
-    return dot(jnp.where(unit, 1.0, 0.0).astype(BF16), values, 1, 1).astype(BF16)
+    return dot(jnp.where(unit, 1.0, 0.0).astype(BF16), values, 1, 1)
 
 
 def silu(values):
@@ -92,12 +90,12 @@
     return half + half * jnp.tanh(half)
 
 
-def scatter_pieces(send, number, state, heads):
+def scatter_pieces(send, number, states):
     rows = STATE // send.shape[0]
     for piece in range(send.shape[0]):
-        for h in range(heads):
-            at = (number * heads + h) * rows
-            send[piece, at : at + rows] = state[piece * rows : (piece + 1) * rows, head(h)]
+        for h, state in enumerate(states):
+            at = (number * len(states) + h) * rows
+            send[piece, at : at + rows] = state[piece * rows : (piece + 1) * rows]
 
 
 def gather_pieces(got, number, h, heads):
@@ -140,10 +138,11 @@
     return lasts, before, after
 
 
-def states_body(heads, steps, decay, root_hbm, x_hbm, b_hbm, send_out, rows_out, rates, rows, send,
-                root, x, b, root_sem, sems, out_sems):
-    chunks = rows.shape[0]
+def states_body(heads, steps, decay_hbm, root_hbm, x_hbm, b_hbm, send_out, rows_out, rates, rows,
+                decay, send, root, x, b, decay_sem, root_sem, sems, out_sems):
     blocks = steps * CHUNK
+    decay_copy = pltpu.make_async_copy(decay_hbm, decay, decay_sem)
+    decay_copy.start()
     pieces = [(0, 0, CHUNK), (0, CHUNK, CHUNK), (1, 0, CHUNK), (1, CHUNK, CHUNK)]
     copies = piece_copies(
         [lambda at, span: x_hbm.at[at, 0, span], lambda at, span: b_hbm.at[at, 0, span]],
@@ -152,20 +151,22 @@
         pieces,
     )
     root_copy = pltpu.make_async_copy(root_hbm.at[0], root, root_sem)
+    start_all(copies[0])
     root_copy.start()
-    start_all(copies[0])
 
     rates[...] = jnp.zeros_like(rates)
+    upper = (
+        lax.broadcasted_iota(jnp.int32, (BLOCK, BLOCK), 0)
+        <= lax.broadcasted_iota(jnp.int32, (BLOCK, BLOCK), 1)
+    )
+    upper = jnp.where(upper, 1.0, 0.0).astype(BF16)
+    decay_copy.wait()
+    start_all(copies[1])
     for level in range(decay.shape[0]):
         for number in range(blocks):
             for h in range(heads):
                 row = 8 * (level * blocks + number) + h
                 rates[row : row + 1] = decay[level, h, :, block(number)]
-    upper = (
-        lax.broadcasted_iota(jnp.int32, (BLOCK, BLOCK), 0)
-        <= lax.broadcasted_iota(jnp.int32, (BLOCK, BLOCK), 1)
-    )
-    upper = jnp.where(upper, 1.0, 0.0).astype(BF16)
     rest = rates[...]
     sums = jnp.zeros_like(rest)
     for _ in range(3):
@@ -173,55 +174,48 @@
         rest = rest - part.astype(F32)
         sums = sums + dot(part, upper, 1, 0)
     sums = sums * -LOG2E
-    for chunk in range(chunks):
+    for chunk in range(rows.shape[0]):
         rows[chunk] = sums[WIDTH * chunk : WIDTH * (chunk + 1)]
     outs = [pltpu.make_async_copy(rows, rows_out, out_sems.at[2])]
     outs[0].start()
 
-    lines = []
+    to_level = []
     totals = []
     for level in range(2):
         numbers = range(level * blocks, (level + 1) * blocks)
         parts = [sums[8 * number : 8 * number + 8] for number in numbers]
         lasts, _, after = block_ends(parts)
         for part, last, suffix in zip(parts, lasts, after):
-            lines.append(jnp.exp2(last - part + suffix))
+            to_level.append(jnp.exp2(last - part + suffix))
         totals.append(jnp.exp2(after[0] + lasts[0]))
-    lines.append(jnp.zeros((128 - 16 * blocks, BLOCK), F32))
-    to_level = jnp.concatenate(lines, axis=0).T
 
     root_copy.wait()
-    start_all(copies[1])
-    state = jnp.concatenate([(root[h] * totals[0][h : h + 1]).T for h in range(heads)], axis=1)
+    states = [(root[h] * totals[0][h : h + 1]).T for h in range(heads)]
     half = heads * STATE // send.shape[0]
     for i, (level, first, count) in enumerate(pieces):
         if (level, first) == (1, 0):
-            scatter_pieces(send, 0, state, heads)
+            scatter_pieces(send, 0, states)
             part = pl.ds(0, half)
             outs.append(
                 pltpu.make_async_copy(send.at[:, part], send_out.at[:, part], out_sems.at[0])
             )
             outs[-1].start()
-            state = jnp.zeros((STATE, heads * HDIM), F32)
+            states = [jnp.zeros((STATE, HDIM), F32)] * heads
         wait_all(copies[i])
         if i > 0:
             start_all(sum(copies[i + 1 : i + 2], []))
-        turned, decayed = [], []
-        for number in range(first, first + count):
-            at = 8 * (level * blocks + number)
-            scale = jnp.concatenate(
-                [
-                    jnp.broadcast_to(to_level[:, at + h : at + h + 1], (BLOCK, HDIM))
-                    for h in range(heads)
-                ],
-                axis=1,
+        numbers = range(first, first + count)
+        turned = [turn(b[level, block(number)]) for number in numbers]
+        span = slice(first * BLOCK, (first + count) * BLOCK)
+        for h in range(heads):
+            decayed = [
+                (values * to_level[level * blocks + number][h : h + 1]).astype(BF16)
+                for number, values in zip(numbers, turned)
+            ]
+            states[h] = states[h] + dot(
+                jnp.concatenate(decayed, axis=1), x[level, span, head(h)], 1, 0
             )
-            decayed.append((x[level, block(number)].astype(F32) * scale).astype(BF16))
-            turned.append(turn(b[level, block(number)]))
-        state = state + dot(
-            jnp.concatenate(turned, axis=1), jnp.concatenate(decayed, axis=0), 1, 0
-        )
-    scatter_pieces(send, 1, state, heads)
+    scatter_pieces(send, 1, states)
     decays = jnp.broadcast_to(totals[1], (8, HDIM))
     for piece in range(send.shape[0]):
         send[piece, send.shape[1] - 8 :] = decays
@@ -231,22 +225,36 @@
     wait_all(outs)
 
 
-def pack(rows, packed):
-    steps = packed.shape[0]
+def level_decays(rows, to_end):
+    steps = rows.shape[0]
     parts = [rows[step, 8 * j : 8 * j + 8] for step in range(steps) for j in range(CHUNK)]
     lasts, before, after = block_ends(parts)
-    for step in range(steps):
-        mine = slice(step * CHUNK, (step + 1) * CHUNK)
+    if to_end:
+        lines = [last - part + end for part, last, end in zip(parts, lasts, after)]
+    else:
+        lines = [start + part for part, start in zip(parts, before)]
+    return [
+        jnp.exp2(jnp.concatenate(lines[step * CHUNK : (step + 1) * CHUNK], axis=0))
+        for step in range(steps)
+    ]
+
+
+def pack(rows, packed):
+    for step in range(packed.shape[0]):
         part = rows[step]
-        last = jnp.concatenate(lasts[mine], axis=0)
+        last = jnp.concatenate(
+            [
+                jnp.broadcast_to(part[8 * j : 8 * j + 8, BLOCK - 1 :], (8, BLOCK))
+                for j in range(CHUNK)
+            ],
+            axis=0,
+        )
         packed[step] = jnp.concatenate(
             [
                 part,
                 jnp.exp2(part),
                 jnp.exp2(last - part),
-                jnp.exp2(jnp.concatenate(before[mine], axis=0) + part),
-                jnp.exp2(last - part + jnp.concatenate(after[mine], axis=0)),
-                jnp.zeros((128 - 5 * WIDTH, BLOCK), F32),
+                jnp.zeros((128 - 3 * WIDTH, BLOCK), F32),
             ],
             axis=0,
         ).T
@@ -424,8 +432,26 @@
             store_sums(sums_ref, part, 0, pairs)
 
 
-def local_body(heads, steps, rows_ref, x_ref, b_ref, c_ref, out_ref, turned_ref, state, packs):
-    step = pl.program_id(1)
+def local_body(heads, steps, rows_ref, x_ref, b_ref, c_ref, gate_hbm, c_hbm, out_grad_hbm,
+               rows_hbm, out_ref, turned_ref, first_ref, gate_out, c_out, out_grad_out, rows_out,
+               state, packs, sems):
+    level, step = pl.program_id(0), pl.program_id(1)
+    span = pl.ds(0, SPAN)
+    copies = [
+        pltpu.make_async_copy(source, target, sems.at[i])
+        for i, (source, target) in enumerate(
+            [
+                (gate_hbm.at[1, 0, span], gate_out),
+                (c_hbm.at[1, 0, span], c_out),
+                (out_grad_hbm.at[1, 0, span], out_grad_out),
+                (rows_hbm.at[pl.ds(steps, 2 * steps)], rows_out),
+            ]
+        )
+    ]
+
+    @pl.when((level == 0) & (step == 0))
+    def _():
+        start_all(copies)
 
     @pl.when(step == 0)
     def _():
@@ -439,20 +465,27 @@
         within = weighted(heads, j, rows, packed, x, b, c)
         carried = dot(c, current.astype(BF16), 1, 0) * spread(packed, FROM_BLOCK, j, heads)
         out_ref[0, block(j)] = (within + carried).astype(BF16)
-        turned_ref[0, :, block(j)] = turn(c)
+        turned_ref[0, :, block(j)] = turn(c).astype(BF16)
         decayed = (x.astype(F32) * spread(packed, TO_BLOCK, j, heads)).astype(BF16)
         factor = spread(packed[BLOCK - 1 :], FROM_BLOCK, j, heads)
         current = current * factor + dot(b, decayed, 0, 0)
     state[...] = current
 
-
-def readout_body(heads, steps, local_hbm, gate_hbm, c_hbm, out_grad_hbm, turned_hbm, rows_hbm,
-                 start_ref, gain_ref, first_sums_ref, scaled_act, gated_act, turned, packed,
-                 sums_out, local, gate, out_grad, c, rows, sums, sems, rows_sem, turned_sem, out_sem):
-    rows_copy = pltpu.make_async_copy(rows_hbm.at[pl.ds(steps, 2 * steps)], rows, rows_sem)
-    rows_copy.start()
-    half = CHUNK * steps // 2
-    pieces = [(0, 0, 1), (0, 1, 2), (0, half, half), (1, 0, half), (1, half, half)]
+    @pl.when((level == 0) & (step == 0))
+    def _():
+        first_ref[...] = out_ref[0]
+
+    @pl.when((level == 1) & (step == steps - 1))
+    def _():
+        wait_all(copies)
+
+
+def readout_body(heads, steps, local_hbm, gate_hbm, c_hbm, out_grad_hbm, turned_hbm, local_ref,
+                 gate_ref, c_ref, out_grad_ref, rows_ref, start_ref, gain_ref, first_sums_ref,
+                 scaled_act, gated_act, turned, lines, sums_out, local, gate, out_grad, c, sums,
+                 sems, turned_sem, out_sem):
+    chunks = [(at, step) for at in range(2) for step in range(steps)]
+    pieces = [(at, step * CHUNK, CHUNK) for at, step in chunks[1:]]
     copies = piece_copies(
         [
             lambda at, span: c_hbm.at[at + 1, 0, span],
@@ -468,34 +501,39 @@
     copies.append([turned_copy])
     start_all(copies[0] + copies[1])
     sums[0, :, :FOLD] = first_sums_ref[...]
-    rows_copy.wait()
+    columns = []
     for at in range(2):
-        pack(rows.at[pl.ds(at * steps, steps)], packed.at[pl.ds(at * steps, steps)])
-    start_all(copies[2])
-    pairs = []
-    for i, (at, first, count) in enumerate(pieces):
-        if first == 0:
+        decays = level_decays(rows_ref.at[pl.ds(at * steps, steps)], False)
+        for step, line in enumerate(decays):
+            lines[at * steps + step] = line
+            columns.append(line.T)
+    for i, (at, step) in enumerate(chunks):
+        if step == 0:
             start = jnp.concatenate(
                 [gather_pieces(start_ref, at, h, heads) for h in range(heads)], axis=1
             ).astype(BF16)
-        wait_all(copies[i])
-        start_all(sum(copies[i + 3 : i + 4], []))
-        piece = dot(c[at, first * BLOCK : (first + count) * BLOCK], start, 1, 0)
-        for number in range(first, first + count):
-            step, j = number // CHUNK, number % CHUNK
-            place = block(number)
-            carried = piece[block(number - first)]
-            carried = carried * spread(packed[at * steps + step], FROM_LEVEL, j, heads)
+        if i == 0:
+            refs = [c_ref, local_ref, gate_ref, out_grad_ref]
+        else:
+            wait_all(copies[i - 1])
+            start_all(sum(copies[i + 1 : i + 2], []))
+            refs = [
+                buffer.at[at, step * SPAN : (step + 1) * SPAN]
+                for buffer in (c, local, gate, out_grad)
+            ]
+        piece = dot(refs[0][...], start, 1, 0)
+        pairs = []
+        for j in range(CHUNK):
+            carried = piece[block(j)] * spread(columns[i], 0, j, heads)
+            place = block(step * CHUNK + j)
             _, scaled_act[at, place], gated_act[at, place], pair = gated_sums(
-                carried + local[at, place].astype(F32),
-                gate[at, place],
-                out_grad[at, place],
+                carried + refs[1][block(j)].astype(F32),
+                refs[2][block(j)],
+                refs[3][block(j)],
                 gain_ref[...],
             )
             pairs.append(pair)
-            if j == CHUNK - 1:
-                store_sums(sums.at[0], step, (at + 1) * FOLD, pairs)
-                pairs = []
+        store_sums(sums.at[0], step, (at + 1) * FOLD, pairs)
     for copy in range(1, sums.shape[0]):
         sums[copy] = sums[0]
     out = pltpu.make_async_copy(sums, sums_out, out_sem)
@@ -504,30 +542,28 @@
     out.wait()
 
 
-def grads_body(heads, steps, features, packed_ref, turned_ref, scaled_act_ref, gated_act_ref,
+def grads_body(heads, steps, features, lines_ref, turned_ref, scaled_act_ref, gated_act_ref,
                total_ref, grad_out, send_out, grads, send, grad_sems, sems):
     total = jnp.sum(total_ref[...], axis=0)
     half = send.shape[1] // 2
     outs = []
     for at in (1, 0):
-        state = jnp.zeros((STATE, heads * HDIM), F32)
+        states = [jnp.zeros((STATE, HDIM), F32)] * heads
         for step in range(steps):
-            packed = packed_ref[at * steps + step]
             norm = norm_columns(total, step, (at + 1) * FOLD, features)
-            decayed = []
-            for j in range(CHUNK):
-                place = block(step * CHUNK + j)
-                inv_rms, back = norm[block(j), 0:1], norm[block(j), 1:2]
-                grad = inv_rms * scaled_act_ref[at, place] - back * gated_act_ref[at, place]
-                grad = grad.astype(BF16)
-                grads[at, place] = grad
-                decayed.append(
-                    (grad.astype(F32) * spread(packed, FROM_LEVEL, j, heads)).astype(BF16)
+            span = slice(step * SPAN, (step + 1) * SPAN)
+            inv_rms, back = norm[:, 0:1], norm[:, 1:2]
+            grad = inv_rms * scaled_act_ref[at, span] - back * gated_act_ref[at, span]
+            grad = grad.astype(BF16)
+            grads[at, span] = grad
+            turned = turned_ref[at, :, span].astype(F32)
+            lines = lines_ref[at * steps + step]
+            for h in range(heads):
+                line = jnp.concatenate(
+                    [lines[8 * j + h : 8 * j + h + 1] for j in range(CHUNK)], axis=1
                 )
-            span = slice(step * SPAN, (step + 1) * SPAN)
-            state = state + dot(
-                turned_ref[at, :, span], jnp.concatenate(decayed, axis=0), 1, 0
-            )
+                decayed = (turned * line).astype(BF16)
+                states[h] = states[h] + dot(decayed, grad[:, head(h)], 1, 0)
             span = pl.ds(step * SPAN, SPAN)
             outs.append(
                 pltpu.make_async_copy(
@@ -535,7 +571,7 @@
                 )
             )
             outs[-1].start()
-        scatter_pieces(send, 1 - at, state, heads)
+        scatter_pieces(send, 1 - at, states)
         part = pl.ds((1 - at) * half, half)
         outs.append(pltpu.make_async_copy(send.at[:, part], send_out.at[:, part], sems.at[at]))
         outs[-1].start()
@@ -589,9 +625,18 @@
             state_grad_ref[0, 0, h] = state[:, head(h)].T
 
 
-def back_body(heads, steps, rows_ref, grad_ref, b_ref, c_ref, given_in, given_state, partial_ref,
-              state_grad_ref, state, packs):
-    step = steps - 1 - pl.program_id(1)
+def back_body(heads, steps, rows_ref, grad_ref, b_ref, c_ref, b_hbm, rows_hbm, given_in,
+              given_state, partial_ref, state_grad_ref, near_ref, near_state_ref, b_out, rows_out,
+              state, packs, sems):
+    level, step = 2 - pl.program_id(0), steps - 1 - pl.program_id(1)
+    copies = [
+        pltpu.make_async_copy(b_hbm.at[1, 0], b_out, sems.at[0]),
+        pltpu.make_async_copy(rows_hbm.at[pl.ds(0, 2 * steps)], rows_out, sems.at[1]),
+    ]
+
+    @pl.when((level == 2) & (step == steps - 1))
+    def _():
+        start_all(copies)
 
     @pl.when(step == steps - 1)
     def _():
@@ -609,65 +654,69 @@
         for h in range(heads):
             state_grad_ref[0, 0, h] = state[:, head(h)].T
 
-
-def inputs_body(heads, steps, b_hbm, partial_hbm, local_hbm, rows_hbm, end_ref, input_grad_out,
-                state_grad_out, b, partial, grads, states, rows, packed, sems, local_sems,
-                rows_sem, out_sems, state_sems):
-    rows_copy = pltpu.make_async_copy(rows_hbm.at[pl.ds(0, 2 * steps)], rows, rows_sem)
-    rows_copy.start()
-    half = CHUNK * steps // 2
-    pieces = [(1, 0, 1), (1, 1, 2), (1, half, half), (0, 0, half), (0, half, 2), (0, half + 2, 1)]
+    @pl.when(level == 1)
+    def _():
+        near_ref[...] = partial_ref[0, 0]
+
+    @pl.when((level == 1) & (step == 0))
+    def _():
+        near_state_ref[...] = state_grad_ref[0, 0]
+        wait_all(copies)
+
+
+def inputs_body(heads, steps, b_hbm, partial_hbm, local_hbm, b_ref, partial_ref, local_ref,
+                rows_ref, end_ref, input_grad_out, state_grad_out, b, partial, grads, states, sems,
+                local_sem, out_sems, state_sems):
+    chunks = [(level, step) for level in (1, 0) for step in range(steps)]
+    pieces = [(0, step * CHUNK, CHUNK) for step in range(steps)]
     copies = piece_copies(
-        [lambda at, span: b_hbm.at[at, 0, span], lambda at, span: partial_hbm.at[at, 0, span]],
+        [lambda at, span: b_hbm.at[0, 0, span], lambda at, span: partial_hbm.at[0, 0, span]],
         [b, partial],
         sems,
         pieces,
     )
-    locals_in = [
-        pltpu.make_async_copy(local_hbm.at[level, 0], states.at[level], local_sems.at[level])
-        for level in range(2)
-    ]
-    for i, (level, first, _) in enumerate(pieces):
-        if first == half:
-            copies[i].append(locals_in[level])
-    start_all(copies[0] + copies[1] + copies[2])
-    rows_copy.wait()
-    for level in range(2):
-        pack(rows.at[pl.ds(level * steps, steps)], packed.at[pl.ds(level * steps, steps)])
+    local_copy = pltpu.make_async_copy(local_hbm.at[0, 0], states.at[0], local_sem)
+    local_copy.start()
+    for some in copies:
+        start_all(some)
     outs = []
-    for i, (level, first, count) in enumerate(pieces):
-        if first == 0:
-            end = jnp.concatenate(
-                [gather_pieces(end_ref, 1 - level, h, heads) for h in range(heads)], axis=1
+    for i, (level, step) in enumerate(chunks):
+        if step == 0:
+            ends = [gather_pieces(end_ref, 1 - level, h, heads) for h in range(heads)]
+            rounded = jnp.concatenate(ends, axis=1).astype(BF16)
+            level_rows = rows_ref.at[pl.ds(level * steps, steps)]
+            columns = [line.T for line in level_decays(level_rows, True)]
+            total = level_decays(level_rows, False)[-1][8 * (CHUNK - 1) :, BLOCK - 1 :]
+            if level == 0:
+                local_copy.wait()
+            for h in range(heads):
+                local = local_ref[h] if level == 1 else states[0, h]
+                states[level, h] = local + (ends[h] * total[h : h + 1]).T
+            outs.append(
+                pltpu.make_async_copy(
+                    states.at[level], state_grad_out.at[level, 0], state_sems.at[level]
+                )
             )
-            rounded = end.astype(BF16)
-        wait_all(copies[i])
-        start_all(sum(copies[i + 3 : i + 4], []))
-        piece = dot(b[level, first * BLOCK : (first + count) * BLOCK], rounded, 1, 0)
-        for number in range(first, first + count):
-            place = block(number)
-            extra = piece[block(number - first)] * spread(
-                packed[level * steps + number // CHUNK], TO_LEVEL, number % CHUNK, heads
-            )
-            grads[level, place] = (partial[level, place].astype(F32) + extra).astype(BF16)
-        span = pl.ds(first * BLOCK, count * BLOCK)
+            outs[-1].start()
+        span = slice(step * SPAN, (step + 1) * SPAN)
+        if level == 1:
+            some_b, some_partial = b_ref.at[span], partial_ref.at[span]
+        else:
+            wait_all(copies[step])
+            some_b, some_partial = b.at[0, span], partial.at[0, span]
+        piece = dot(some_b[...], rounded, 1, 0)
+        for j in range(CHUNK):
+            extra = piece[block(j)] * spread(columns[step], 0, j, heads)
+            grads[level, block(step * CHUNK + j)] = (
+                some_partial[block(j)].astype(F32) + extra
+            ).astype(BF16)
+        span = pl.ds(step * SPAN, SPAN)
         outs.append(
             pltpu.make_async_copy(
                 grads.at[level, span], input_grad_out.at[level, 0, span], out_sems.at[i]
             )
         )
         outs[-1].start()
-        if first == half:
-            last = packed[(level + 1) * steps - 1, BLOCK - 1 :]
-            total = spread(last, FROM_LEVEL, CHUNK - 1, heads)
-            for h in range(heads):
-                states[level, h] += (end[:, head(h)] * total[:, head(h)]).T
-            outs.append(
-                pltpu.make_async_copy(
-                    states.at[level], state_grad_out.at[level, 0], state_sems.at[level]
-                )
-            )
-            outs[-1].start()
     wait_all(outs)
 
 
@@ -686,7 +735,6 @@
     vmem = pl.BlockSpec(memory_space=pltpu.VMEM)
     anywhere = pl.BlockSpec(memory_space=pl.ANY)
     rows_shape = (levels * steps, WIDTH, BLOCK)
-    two_levels = (2 * steps, BLOCK, 128)
     pair_shape = (segments, 2 * heads * rows, HDIM)
     first_shape = (segments, 2 * heads * rows + 8, HDIM)
     sums_shape = (head_devices, 8, levels * FOLD)
@@ -699,7 +747,7 @@
     far = lambda array: pin(array, pltpu.HBM)
     near = lambda array: pin(array, pltpu.VMEM)
     x, gate, out_grad = far(ssm_input), far(gate_input), far(out_grad)
-    decay = near(decay)
+    decay = far(decay)
     b, c, root = far(b_input), far(c_output), far(root_state)
 
     def pair_of_levels(width):
@@ -725,16 +773,18 @@
         functools.partial(states_body, heads, steps),
         "states",
         6,
-        in_specs=[vmem] + [anywhere] * 3,
+        in_specs=[anywhere] * 4,
         out_specs=[anywhere, anywhere],
         out_shape=[pltpu.HBM(first_shape, F32), pltpu.HBM(rows_shape, F32)],
         scratch_shapes=[
             pltpu.VMEM((levels * blocks * 8, BLOCK), F32),
             pltpu.VMEM(rows_shape, F32),
+            pltpu.VMEM(decay.shape, F32),
             pltpu.VMEM(first_shape, F32),
             pltpu.VMEM(root_state.shape[1:], F32),
             pair_of_levels(columns),
             pair_of_levels(STATE),
+            dma,
             dma,
             dma((4, 2)),
             dma((3,)),
@@ -778,7 +828,7 @@
     starts = exchange(picked)
     both = lambda l, k: (l, k)
     later = lambda l, k: (l + 1, k)
-    local, turned = call(
+    local, turned, *first = call(
         functools.partial(local_body, heads, steps),
         "local",
         7,
@@ -788,29 +838,37 @@
             tokens(columns, later),
             tokens(STATE, later),
             tokens(STATE, later),
-        ],
+        ]
+        + [anywhere] * 4,
         out_specs=[
             flat(columns, both),
             pl.BlockSpec((1, STATE, SPAN), lambda l, k: (l, 0, k)),
-        ],
+            pl.BlockSpec((SPAN, columns), lambda l, k: (0, 0)),
+        ]
+        + [anywhere] * 4,
         out_shape=[
             pltpu.HBM((2, length, columns), BF16),
             pltpu.HBM((2, STATE, length), BF16),
+            pltpu.VMEM((SPAN, columns), BF16),
+            pltpu.VMEM((SPAN, columns), BF16),
+            pltpu.VMEM((SPAN, STATE), BF16),
+            pltpu.VMEM((SPAN, columns), BF16),
+            pltpu.VMEM((2 * steps,) + rows_shape[1:], F32),
         ],
-        scratch_shapes=[state_scratch, packs_scratch],
-    )(far(late_rows), x, b, c)
-
-    scaled_act, gated_act, turned, packed, sums = call(
+        scratch_shapes=[state_scratch, packs_scratch, dma((4,))],
+    )(far(late_rows), x, b, c, gate, c, out_grad, far(late_rows))
+
+    scaled_act, gated_act, turned, lines, sums = call(
         functools.partial(readout_body, heads, steps),
         "readout",
         5,
-        in_specs=[anywhere] * 6 + [vmem] * 3,
+        in_specs=[anywhere] * 5 + [vmem] * 8,
         out_specs=[vmem] * 4 + [anywhere],
         out_shape=[
             pltpu.VMEM((2, length, columns), F32),
             pltpu.VMEM((2, length, columns), F32),
             pltpu.VMEM((2, STATE, length), BF16),
-            pltpu.VMEM(two_levels, F32),
+            pltpu.VMEM((2 * steps,) + rows_shape[1:], F32),
             pltpu.HBM(sums_shape, F32),
         ],
         scratch_shapes=[
@@ -818,10 +876,8 @@
             pair_of_levels(columns),
             pair_of_levels(columns),
             pair_of_levels(STATE),
-            pltpu.VMEM((2 * steps,) + rows_shape[1:], F32),
             pltpu.VMEM(sums_shape, F32),
-            dma((5, 4)),
-            dma,
+            dma((2 * steps - 1, 4)),
             dma,
             dma,
         ],
@@ -831,7 +887,11 @@
         c,
         out_grad,
         far(turned),
-        far(late_rows),
+        near(first[0]),
+        near(first[1]),
+        near(first[2]),
+        near(first[3]),
+        near(first[4]),
         near(starts),
         gain,
         sums0,
@@ -846,7 +906,7 @@
         out_specs=[anywhere, anywhere],
         out_shape=[pltpu.HBM((2, length, columns), BF16), pltpu.HBM(pair_shape, F32)],
         scratch_shapes=[pair_of_levels(columns), pair_scratch, dma((2 * steps,)), dma((2,))],
-    )(near(packed), near(turned), near(scaled_act), near(gated_act), near(totals))
+    )(near(lines), near(turned), near(scaled_act), near(gated_act), near(totals))
     got_back = exchange(send_back)
 
     own_back = lambda k: (0, steps - 1 - k)
@@ -885,7 +945,8 @@
     ends = exchange(folded)
     down_back = lambda l, k: (2 - l, steps - 1 - k)
     both_down_back = lambda l, k: (1 - l, steps - 1 - k)
-    given = call(
+    late = lambda l, k: (l, jnp.where(l == 0, steps - 1, steps - 1 - k))
+    *given, near_partial, near_state, near_b, near_rows = call(
         functools.partial(back_body, heads, steps),
         "back",
         8,
@@ -895,37 +956,47 @@
             flat(columns, both_down_back),
             tokens(STATE, down_back),
             tokens(STATE, down_back),
+        ]
+        + [anywhere] * 4,
+        out_specs=[
+            tokens(columns, down_back),
+            state_grads(down_back),
+            pl.BlockSpec((SPAN, columns), lambda *g: (late(*g)[1], 0)),
+            pl.BlockSpec((heads, HDIM, STATE), lambda *g: (0, 0, 0)),
             anywhere,
             anywhere,
         ],
-        out_specs=[tokens(columns, down_back), state_grads(down_back)],
-        out_shape=[pltpu.HBM(ssm_input.shape, BF16), pltpu.HBM(state_shape, F32)],
-        input_output_aliases={4: 0, 5: 1},
-        scratch_shapes=[state_scratch, packs_scratch],
-    )(far(late_rows), far(grads), b, c, *given)
+        out_shape=[
+            pltpu.HBM(ssm_input.shape, BF16),
+            pltpu.HBM(state_shape, F32),
+            pltpu.VMEM((length, columns), BF16),
+            pltpu.VMEM(state_shape[2:], F32),
+            pltpu.VMEM((length, STATE), BF16),
+            pltpu.VMEM((2 * steps,) + rows_shape[1:], F32),
+        ],
+        input_output_aliases={6: 0, 7: 1},
+        scratch_shapes=[state_scratch, packs_scratch, dma((2,))],
+    )(far(late_rows), far(grads), b, c, b, far(late_rows), *given)
 
     return call(
         functools.partial(inputs_body, heads, steps),
         "inputs",
         4,
-        in_specs=[anywhere] * 4 + [vmem],
+        in_specs=[anywhere] * 3 + [vmem] * 5,
         out_specs=[anywhere, anywhere],
         out_shape=[pltpu.HBM(ssm_input.shape, BF16), pltpu.HBM(state_shape, F32)],
         input_output_aliases={1: 0, 2: 1},
         scratch_shapes=[
-            pair_of_levels(STATE),
-            pair_of_levels(columns),
+            pltpu.VMEM((1, length, STATE), BF16),
+            pltpu.VMEM((1, length, columns), BF16),
             pair_of_levels(columns),
             pltpu.VMEM((2,) + state_shape[2:], F32),
-            pltpu.VMEM((2 * steps,) + rows_shape[1:], F32),
-            pltpu.VMEM(two_levels, F32),
-            dma((6, 2)),
-            dma((2,)),
+            dma((steps, 2)),
             dma,
-            dma((6,)),
+            dma((2 * steps,)),
             dma((2,)),
         ],
-    )(b, *given, far(late_rows), near(ends))
+    )(b, *given, near(near_b), near(near_partial), near(near_state), near(near_rows), near(ends))
 
 
 def solution(mesh):

time: 117 us -> 116 us (level)
  Pallas kernels: 61.4 us -> 58.3 us
  local copies, waits for them, and re-layouts: 0.83 us -> 3.65 us
  waiting for transfers between devices: 21.6 us -> 19.8 us
  starting transfers between devices: 19 us -> 20.3 us
    unnamed x8 -> x14, local copies, waits for them, and re-layouts: 0.82 us -> 3.64 us
    all_to_all x1, waiting for transfers between devices: 3.82 us -> 2.23 us  [shards(): starts = exchange(picked)]
    all_to_all x1, starting transfers between devices: 3.63 us -> 4.92 us  [shards(): got_back = exchange(send_back)]
where the time goes in v3:
time: 116 us; the launch traced here: 115 us
  Pallas kernels  58.3 us (50%)
  starting transfers between devices  20.3 us (18%)
  waiting for transfers between devices  19.8 us (17%)
  blocking collectives  12.2 us (11%)
  local copies, waits for them, and re-layouts  3.65 us (3%)
    all_to_all x1, blocking collectives, shards(): lax.all_to_all(sums, 'head', split_axis=0, concat_axis=0, tiled=True)  12.2 us
    pallas_call x1, Pallas kernels, shards(): call(functools.partial(back_body, heads, steps), 'back', 8, grid=(2, step...  9.37 us
    pallas_call x1, Pallas kernels, shards(): call(functools.partial(local_body, heads, steps), 'local', 7, grid=(2, st...  9.02 us
    pallas_call x1, Pallas kernels, shards(): call(functools.partial(forward0_body, heads, steps), 'forward0', 6, grid=...  8.36 us
    all_to_all x1, starting transfers between devices, shards(): got = exchange(send)  8.15 us
    pallas_call x1, Pallas kernels, shards(): call(functools.partial(back0_body, heads, steps, features), 'back0', 6, g...  7.34 us
    all_to_all x1, waiting for transfers between devices, shards(): got_back = exchange(send_back)  7.17 us
    all_to_all x1, waiting for transfers between devices, shards(): got = exchange(send)  6.79 us
  transfers between devices with their start and end apart: 4, of which 4 were waited for; matrix products, arithmetic and copies ran while one was open for 0% of the time, Pallas kernels for 30%

profile of v3, /device:TPU:0, one launch (start us, length us, event | category | flops | bytes accessed | tf_op | source)
XLA Modules:
  0.0 115.3 jit_solution(821495180112339167)
XLA Ops:
  0.6 0.0 copy-start.6
  0.6 6.5 %states.1 = (f32[16,104,128]{2,1,0:T(8,128)}, f32[6,24,256]{2,1,0:T(8,128)}) custom-call(f32[3,3,1,1536]{3,2,1,0:T(1,128)} %bitcast.1, f32[1,3,128,256]{3,2,1,0:T(8,128)} %root_ref.1, bf16[3,1,1536,384]{3,2,1,0:T(8,128)(2,1)} %x_ref.3, bf16[3,1,1536,256]{3,2,1,0:T(8,128)(2,1)} %b_hbm.5), custom_call_target="tpu_custom_call" | custom-call | flops 6000000000 | bytes 18000000 | tf_op jit(solution)/shard_map/states/pallas_call | solution.py:772
  7.2 8.1 %all-to-all-start = ((f32[16,104,128]{2,1,0:T(8,128)}), f32[16,104,128]{2,1,0:T(8,128)S(1)}, u32[]{:S(2)}, u32[]{:S(2)}) async-start(f32[16,104,128]{2,1,0:T(8,128)} %get-tuple-element.37), calls=%async_computation | async-start | bytes 1703936 | tf_op jit(solution)/shard_map/all_to_all | solution.py:793
  15.3 0.0 copy-done.6
  15.3 0.0 copy-start
  15.3 8.4 %forward0.1 = (bf16[1,1536,384]{2,1,0:T(8,128)(2,1)}, f32[8,384]{1,0:T(8,128)}) custom-call(f32[6,24,256]{2,1,0:T(8,128)} %get-tuple-element.61.rows_ref.rows_hbm, f32[1,3,128,256]{3,2,1,0:T(8,128)} %root_ref.1, f32[1,384]{1,0:T(1,128)S(1)} %reshape.7.gain_ref, bf16[3,1,1536,384]{3,2,1,0:T(8,128)(2,1)} %x_ref.3, bf16[3,1,1536,384]{3,2,1,0:T(8,128)(2,1)} %gate_ref.3, ...), custom_call_target="tpu_custom_call" | custom-call | flops 6000000000 | bytes 18000000 | tf_op jit(solution)/shard_map/forward0/pallas_call | solution.py:796
  23.7 6.8 %all-to-all-done.got_ref = f32[16,104,128]{2,1,0:T(8,128)S(1)} async-done(((f32[16,104,128]{2,1,0:T(8,128)}), f32[16,104,128]{2,1,0:T(8,128)S(1)}, u32[]{:S(2)}, u32[]{:S(2)}) %all-to-all-start) | async-done | bytes 852000 | tf_op jit(solution)/shard_map/all_to_all | solution.py:793
  30.5 0.0 copy-done
  30.5 1.5 %pick.1 = f32[16,96,128]{2,1,0:T(8,128)} custom-call(s32[2,16]{1,0:T(2,128)S(1)} %copy-done, f32[16,104,128]{2,1,0:T(8,128)S(1)} %all-to-all-done.got_ref), custom_call_target="tpu_custom_call" | custom-call | flops 1000000000 | bytes 3000000 | tf_op jit(solution)/shard_map/pick/pallas_call | solution.py:817
  32.0 3.6 %all-to-all-start.1 = ((f32[16,96,128]{2,1,0:T(8,128)}), f32[16,96,128]{2,1,0:T(8,128)S(1)}, u32[]{:S(2)}, u32[]{:S(2)}) async-start(f32[16,96,128]{2,1,0:T(8,128)} %pick.1), calls=%async_computation.1 | async-start | bytes 1572864 | tf_op jit(solution)/shard_map/all_to_all | solution.py:828
  35.6 0.0 copy-start.5
  35.6 9.0 %local.1 = (bf16[2,1536,384]{2,1,0:T(8,128)(2,1)}, bf16[2,256,1536]{2,1,0:T(8,128)(2,1)}, bf16[768,384]{1,0:T(8,128)(2,1)S(1)}, bf16[768,384]{1,0:T(8,128)(2,1)S...) custom-call(f32[6,24,256]{2,1,0:T(8,128)} %get-tuple-element.61.rows_ref.rows_hbm, ...), custom_call_target="tpu_custom_call" | custom-call | flops 7000000000 | bytes 21000000 | tf_op jit(solution)/shard_map/local/pallas_call | solution.py:831
  44.7 0.0 copy-start.1
  44.7 0.8 copy-done.1
  45.5 0.0 copy-start.3
  45.5 0.8 copy-done.3
  46.2 2.2 %all-to-all-done.1.start_ref = f32[16,96,128]{2,1,0:T(8,128)S(1)} async-done(((f32[16,96,128]{2,1,0:T(8,128)}), f32[16,96,128]{2,1,0:T(8,128)S(1)}, u32[]{:S(2)}, u32[]{:S(2)}) %all-to-all-start.1) | async-done | bytes 786464 | tf_op jit(solution)/shard_map/all_to_all | solution.py:828
  48.5 0.0 copy-done.5
  48.5 0.0 copy-start.2
  48.5 1.1 copy-done.2
  49.5 0.0 copy-start.4
  49.5 1.0 copy-done.4
  50.5 6.5 %readout.1 = (f32[2,1536,384]{2,1,0:T(8,128)S(1)}, f32[2,1536,384]{2,1,0:T(8,128)S(1)}, bf16[2,256,1536]{2,1,0:T(8,128)(2,1)S(1)}, f32[4,24,256]{2,1,0:T(8,128)S(1)}, f32[8,8,1152]{2,1,0:T(8,128)}) custom-call(bf16[2,1536,384]{2,1,0:T(8,128)(2,1)} %get-tuple-element.42.local_hbm, bf16[3,1,1536,384]{3,2,1,0:T(8,128)(2,1)} %gate_ref.3, ...), custom_call_target="tpu_custom_call" | custom-call | flops 5000000000 | bytes 15000000 | tf_op jit(solution)/shard_map/readout/pallas_call | solution.py:861
  57.0 12.2 %all_to_all.25.total_ref = f32[8,8,1152]{2,1,0:T(8,128)S(1)} all-to-all(f32[8,8,1152]{2,1,0:T(8,128)} %get-tuple-element.55), channel_id=1, replica_groups=mesh['seg'=16,'head'=8] {'head'}, dimensions={0} | all-to-all | bytes 589824 | tf_op jit(solution)/shard_map/all_to_all | solution.py:899
  69.2 3.7 %grads.1 = (bf16[2,1536,384]{2,1,0:T(8,128)(2,1)}, f32[16,96,128]{2,1,0:T(8,128)}) custom-call(f32[4,24,256]{2,1,0:T(8,128)S(1)} %get-tuple-element.51.lines_ref, bf16[2,256,1536]{2,1,0:T(8,128)(2,1)S(1)} %get-tuple-element.52.turned_ref, f32[2,1536,384]{2,1,0:T(8,128)S(1)} %get-tuple-element.53.scaled_act_ref, ...), custom_call_target="tpu_custom_call" | custom-call | flops 4000000000 | bytes 12000000 | tf_op jit(solution)/shard_map/grads/pallas_call | solution.py:901
  73.0 4.9 %all-to-all-start.3 = ((f32[16,96,128]{2,1,0:T(8,128)}), f32[16,96,128]{2,1,0:T(8,128)S(1)}, u32[]{:S(2)}, u32[]{:S(2)}) async-start(f32[16,96,128]{2,1,0:T(8,128)} %get-tuple-element.56), calls=%async_computation.3 | async-start | bytes 1572864 | tf_op jit(solution)/shard_map/all_to_all | solution.py:910
  77.9 7.3 %back0.1 = (bf16[3,1,1536,384]{3,2,1,0:T(8,128)(2,1)}, f32[3,1,3,128,256]{4,3,2,1,0:T(8,128)}) custom-call(f32[6,24,256]{2,1,0:T(8,128)} %get-tuple-element.61.rows_ref.rows_hbm, f32[1,384]{1,0:T(1,128)S(1)} %reshape.7.gain_ref, f32[8,8,1152]{2,1,0:T(8,128)S(1)} %all_to_all.25.total_ref, bf16[3,1,1536,384]{3,2,1,0:T(8,128)(2,1)} %gate_ref.3, ...), custom_call_target="tpu_custom_call" | custom-call | flops 6000000000 | bytes 18000000 | tf_op jit(solution)/shard_map/back0/pallas_call | solution.py:913
  85.2 7.2 %all-to-all-done.3.got_ref = f32[16,96,128]{2,1,0:T(8,128)S(1)} async-done(((f32[16,96,128]{2,1,0:T(8,128)}), f32[16,96,128]{2,1,0:T(8,128)S(1)}, u32[]{:S(2)}, u32[]{:S(2)}) %all-to-all-start.3) | async-done | bytes 786464 | tf_op jit(solution)/shard_map/all_to_all | solution.py:910
  92.4 1.7 %fold.1 = f32[16,96,128]{2,1,0:T(8,128)} custom-call(s32[2,16]{1,0:T(2,128)S(1)} %copy-done, f32[16,8,128]{2,1,0:T(8,128)S(1)} %slice.3.decay_ref, f32[16,96,128]{2,1,0:T(8,128)S(1)} %all-to-all-done.3.got_ref), custom_call_target="tpu_custom_call" | custom-call | flops 1000000000 | bytes 3000000 | tf_op jit(solution)/shard_map/fold/pallas_call | solution.py:934
  94.1 3.6 %all-to-all-start.4 = ((f32[16,96,128]{2,1,0:T(8,128)}), f32[16,96,128]{2,1,0:T(8,128)S(1)}, u32[]{:S(2)}, u32[]{:S(2)}) async-start(f32[16,96,128]{2,1,0:T(8,128)} %fold.1), calls=%async_computation.4 | async-start | bytes 1572864 | tf_op jit(solution)/shard_map/all_to_all | solution.py:945
  97.7 9.4 %back.1 = (bf16[3,1,1536,384]{3,2,1,0:T(8,128)(2,1)}, f32[3,1,3,128,256]{4,3,2,1,0:T(8,128)}, bf16[1536,384]{1,0:T(8,128)(2,1)S(1)}, f32[3,128,256]{2,1,0:T(8,12...) custom-call(f32[6,24,256]{2,1,0:T(8,128)} %get-tuple-element.61.rows, ...), custom_call_target="tpu_custom_call", output_to_operand_aliasing={{0}: (6, {}), {1}: (7, {})} | custom-call | flops 8000000000 | bytes 24000000 | tf_op jit(solution)/shard_map/back/pallas_call | solution.py:949
  107.1 3.6 %all-to-all-done.4.end_ref = f32[16,96,128]{2,1,0:T(8,128)S(1)} async-done(((f32[16,96,128]{2,1,0:T(8,128)}), f32[16,96,128]{2,1,0:T(8,128)S(1)}, u32[]{:S(2)}, u32[]{:S(2)}) %all-to-all-start.4) | async-done | bytes 786464 | tf_op jit(solution)/shard_map/all_to_all | solution.py:945
  110.8 4.4 %inputs.1 = (bf16[3,1,1536,384]{3,2,1,0:T(8,128)(2,1)}, f32[3,1,3,128,256]{4,3,2,1,0:T(8,128)}) custom-call(bf16[3,1,1536,256]{3,2,1,0:T(8,128)(2,1)} %b_hbm.5, bf16[3,1,1536,384]{3,2,1,0:T(8,128)(2,1)} %get-tuple-element.65.partial_hbm, f32[3,1,3,128,256]{4,3,2,1,0:T(8,128)} %get-tuple-element.66.local_hbm, ...), custom_call_target="tpu_custom_call", output_to_operand_aliasing={{0}: (1, {}), {1}: (2, {})} | custom-call | flops 4000000000 | bytes 12000000 | tf_op jit(solution)/shard_map/inputs/pallas_call | solution.py:981
  (2 shorter events, 0.0 us)
Async XLA Ops:
  0.6 14.7 %copy-start.6 = (f32[384]{0:T(512)S(1)}, f32[384]{0:T(512)}, u32[]{:S(2)}) copy-start(f32[384]{0:T(512)} %param.15) | copy-start | bytes 4612
  7.2 23.3 %all-to-all-start = ((f32[16,104,128]{2,1,0:T(8,128)}), f32[16,104,128]{2,1,0:T(8,128)S(1)}, u32[]{:S(2)}, u32[]{:S(2)}) async-start(f32[16,104,128]{2,1,0:T(8,128)} %get-tuple-element.37), calls=%async_computation | async-start | bytes 1703936 | tf_op jit(solution)/shard_map/all_to_all | solution.py:793
  15.3 15.2 %copy-start = (s32[2,16]{1,0:T(2,128)S(1)}, s32[2,16]{1,0:T(2,128)}, u32[]{:S(2)}) copy-start(s32[2,16]{1,0:T(2,128)} %parent_ref.3) | copy-start | bytes 388
  32.0 16.5 %all-to-all-start.1 = ((f32[16,96,128]{2,1,0:T(8,128)}), f32[16,96,128]{2,1,0:T(8,128)S(1)}, u32[]{:S(2)}, u32[]{:S(2)}) async-start(f32[16,96,128]{2,1,0:T(8,128)} %pick.1), calls=%async_computation.1 | async-start | bytes 1572864 | tf_op jit(solution)/shard_map/all_to_all | solution.py:828
  35.6 12.8 %copy-start.5 = (f32[8,384]{1,0:T(8,128)S(1)}, f32[8,384]{1,0:T(8,128)}, u32[]{:S(2)}) copy-start(f32[8,384]{1,0:T(8,128)} %get-tuple-element.50.first_sums_ref) | copy-start | bytes 36868
  44.7 0.8 copy-start.1
  45.5 0.8 copy-start.3
  48.5 1.1 copy-start.2
  49.5 1.0 copy-start.4
  73.0 19.5 %all-to-all-start.3 = ((f32[16,96,128]{2,1,0:T(8,128)}), f32[16,96,128]{2,1,0:T(8,128)S(1)}, u32[]{:S(2)}, u32[]{:S(2)}) async-start(f32[16,96,128]{2,1,0:T(8,128)} %get-tuple-element.56), calls=%async_computation.3 | async-start | bytes 1572864 | tf_op jit(solution)/shard_map/all_to_all | solution.py:910
  94.1 16.7 %all-to-all-start.4 = ((f32[16,96,128]{2,1,0:T(8,128)}), f32[16,96,128]{2,1,0:T(8,128)S(1)}, u32[]{:S(2)}, u32[]{:S(2)}) async-start(f32[16,96,128]{2,1,0:T(8,128)} %fold.1), calls=%async_computation.4 | async-start | bytes 1572864 | tf_op jit(solution)/shard_map/all_to_all | solution.py:945

commit v4 on v3

--- a/solution.py
+++ b/solution.py
@@ -15,6 +15,7 @@
 STATE = 256
 CHUNK = 3
 SPAN = CHUNK * BLOCK
+FIRST = 2 * BLOCK
 FOLD = SPAN // 2
 EPSILON = 1e-05
 VMEM_LIMIT = 24 * 1024 * 1024
@@ -138,8 +139,8 @@
     return lasts, before, after
 
 
-def states_body(heads, steps, decay_hbm, root_hbm, x_hbm, b_hbm, send_out, rows_out, rates, rows,
-                decay, send, root, x, b, decay_sem, root_sem, sems, out_sems):
+def states_body(heads, steps, decay_hbm, root_hbm, x_hbm, b_hbm, send, rows_out, rates, rows, decay,
+                root, x, b, decay_sem, root_sem, sems, out_sem):
     blocks = steps * CHUNK
     decay_copy = pltpu.make_async_copy(decay_hbm, decay, decay_sem)
     decay_copy.start()
@@ -176,8 +177,8 @@
     sums = sums * -LOG2E
     for chunk in range(rows.shape[0]):
         rows[chunk] = sums[WIDTH * chunk : WIDTH * (chunk + 1)]
-    outs = [pltpu.make_async_copy(rows, rows_out, out_sems.at[2])]
-    outs[0].start()
+    rows_copy = pltpu.make_async_copy(rows, rows_out, out_sem)
+    rows_copy.start()
 
     to_level = []
     totals = []
@@ -191,15 +192,9 @@
 
     root_copy.wait()
     states = [(root[h] * totals[0][h : h + 1]).T for h in range(heads)]
-    half = heads * STATE // send.shape[0]
     for i, (level, first, count) in enumerate(pieces):
         if (level, first) == (1, 0):
             scatter_pieces(send, 0, states)
-            part = pl.ds(0, half)
-            outs.append(
-                pltpu.make_async_copy(send.at[:, part], send_out.at[:, part], out_sems.at[0])
-            )
-            outs[-1].start()
             states = [jnp.zeros((STATE, HDIM), F32)] * heads
         wait_all(copies[i])
         if i > 0:
@@ -219,10 +214,7 @@
     decays = jnp.broadcast_to(totals[1], (8, HDIM))
     for piece in range(send.shape[0]):
         send[piece, send.shape[1] - 8 :] = decays
-    part = pl.ds(half, send.shape[1] - half)
-    outs.append(pltpu.make_async_copy(send.at[:, part], send_out.at[:, part], out_sems.at[1]))
-    outs[-1].start()
-    wait_all(outs)
+    rows_copy.wait()
 
 
 def level_decays(rows, to_end):
@@ -260,44 +252,31 @@
         ).T
 
 
-def pick_body(heads, parent_ref, got_ref, send_out, send, sems):
+def pick_body(heads, parent_ref, got_ref, send, decay_out):
     segments = got_ref.shape[0]
     rows = STATE // segments
     pair = send.shape[1]
     half = pair // 2
-    quarter = segments // 4
-    copies = []
     for seg in range(segments):
         first = parent_ref[0, seg]
         second = parent_ref[1, seg]
         root = parent_ref[0, second]
         send[seg, :half] = got_ref[first, :half]
         decay = got_ref[second, pair : pair + 8]
+        decay_out[seg] = got_ref[seg, pair : pair + 8]
         for h in range(heads):
             a = slice(h * rows, (h + 1) * rows)
             b = slice(half + h * rows, half + (h + 1) * rows)
             send[seg, b] = decay[h : h + 1] * got_ref[root, a] + got_ref[second, b]
-        if (seg + 1) % quarter == 0:
-            part = pl.ds(seg + 1 - quarter, quarter)
-            copies.append(
-                pltpu.make_async_copy(send.at[part], send_out.at[part], sems.at[len(copies)])
-            )
-            copies[-1].start()
-    wait_all(copies)
-
-
-def fold_body(heads, parent_ref, decay_ref, got_ref, send_out, send, sems):
+
+
+def fold_body(heads, parent_ref, decay_ref, got_ref, send):
     rows = STATE // got_ref.shape[0]
     half = send.shape[1] // 2
     send[...] = jnp.zeros_like(send)
-    copies = [
-        pltpu.make_async_copy(send.at[:, part], send_out.at[:, part], sems.at[i])
-        for i, part in enumerate([pl.ds(0, half), pl.ds(half, half)])
-    ]
     for seg in range(got_ref.shape[0]):
         second = parent_ref[1, seg]
         send[second, :half] += got_ref[seg, :half]
-    copies[0].start()
     for seg in range(got_ref.shape[0]):
         first = parent_ref[0, seg]
         decay = decay_ref[seg]
@@ -305,8 +284,6 @@
             a = slice(h * rows, (h + 1) * rows)
             b = slice(half + h * rows, half + (h + 1) * rows)
             send[first, b] += decay[h : h + 1] * send[seg, a] + got_ref[seg, b]
-    copies[1].start()
-    wait_all(copies)
 
 
 def causal_mask(transposed):
@@ -436,7 +413,7 @@
                rows_hbm, out_ref, turned_ref, first_ref, gate_out, c_out, out_grad_out, rows_out,
                state, packs, sems):
     level, step = pl.program_id(0), pl.program_id(1)
-    span = pl.ds(0, SPAN)
+    span = pl.ds(0, FIRST)
     copies = [
         pltpu.make_async_copy(source, target, sems.at[i])
         for i, (source, target) in enumerate(
@@ -473,7 +450,7 @@
 
     @pl.when((level == 0) & (step == 0))
     def _():
-        first_ref[...] = out_ref[0]
+        first_ref[...] = out_ref[0, :FIRST]
 
     @pl.when((level == 1) & (step == steps - 1))
     def _():
@@ -482,10 +459,11 @@
 
 def readout_body(heads, steps, local_hbm, gate_hbm, c_hbm, out_grad_hbm, turned_hbm, local_ref,
                  gate_ref, c_ref, out_grad_ref, rows_ref, start_ref, gain_ref, first_sums_ref,
-                 scaled_act, gated_act, turned, lines, sums_out, local, gate, out_grad, c, sums,
-                 sems, turned_sem, out_sem):
-    chunks = [(at, step) for at in range(2) for step in range(steps)]
-    pieces = [(at, step * CHUNK, CHUNK) for at, step in chunks[1:]]
+                 scaled_act, gated_act, turned, lines, sums, local, gate, out_grad, c, sems,
+                 turned_sem):
+    early = FIRST // BLOCK
+    pieces = [(0, early, CHUNK - early)]
+    pieces += [(at, step * CHUNK, CHUNK) for at in range(2) for step in range(steps)][1:]
     copies = piece_copies(
         [
             lambda at, span: c_hbm.at[at + 1, 0, span],
@@ -507,8 +485,9 @@
         for step, line in enumerate(decays):
             lines[at * steps + step] = line
             columns.append(line.T)
-    for i, (at, step) in enumerate(chunks):
-        if step == 0:
+    pairs = []
+    for i, (at, first, count) in enumerate([(0, 0, early)] + pieces):
+        if first == 0:
             start = jnp.concatenate(
                 [gather_pieces(start_ref, at, h, heads) for h in range(heads)], axis=1
             ).astype(BF16)
@@ -517,45 +496,48 @@
         else:
             wait_all(copies[i - 1])
             start_all(sum(copies[i + 1 : i + 2], []))
-            refs = [
-                buffer.at[at, step * SPAN : (step + 1) * SPAN]
-                for buffer in (c, local, gate, out_grad)
-            ]
+            span = slice(first * BLOCK, (first + count) * BLOCK)
+            refs = [buffer.at[at, span] for buffer in (c, local, gate, out_grad)]
         piece = dot(refs[0][...], start, 1, 0)
-        pairs = []
-        for j in range(CHUNK):
-            carried = piece[block(j)] * spread(columns[i], 0, j, heads)
-            place = block(step * CHUNK + j)
+        for number in range(first, first + count):
+            step, j = number // CHUNK, number % CHUNK
+            mine = block(number - first)
+            carried = piece[mine] * spread(columns[at * steps + step], 0, j, heads)
+            place = block(number)
             _, scaled_act[at, place], gated_act[at, place], pair = gated_sums(
-                carried + refs[1][block(j)].astype(F32),
-                refs[2][block(j)],
-                refs[3][block(j)],
-                gain_ref[...],
+                carried + refs[1][mine].astype(F32), refs[2][mine], refs[3][mine], gain_ref[...]
             )
             pairs.append(pair)
-        store_sums(sums.at[0], step, (at + 1) * FOLD, pairs)
+            if j == CHUNK - 1:
+                store_sums(sums.at[0], step, (at + 1) * FOLD, pairs)
+                pairs = []
     for copy in range(1, sums.shape[0]):
         sums[copy] = sums[0]
-    out = pltpu.make_async_copy(sums, sums_out, out_sem)
-    out.start()
     turned_copy.wait()
-    out.wait()
 
 
 def grads_body(heads, steps, features, lines_ref, turned_ref, scaled_act_ref, gated_act_ref,
-               total_ref, grad_out, send_out, grads, send, grad_sems, sems):
+               total_ref, grad_out, send, grads, grad_sems):
     total = jnp.sum(total_ref[...], axis=0)
-    half = send.shape[1] // 2
     outs = []
     for at in (1, 0):
-        states = [jnp.zeros((STATE, HDIM), F32)] * heads
         for step in range(steps):
             norm = norm_columns(total, step, (at + 1) * FOLD, features)
             span = slice(step * SPAN, (step + 1) * SPAN)
             inv_rms, back = norm[:, 0:1], norm[:, 1:2]
             grad = inv_rms * scaled_act_ref[at, span] - back * gated_act_ref[at, span]
-            grad = grad.astype(BF16)
-            grads[at, span] = grad
+            grads[at, span] = grad.astype(BF16)
+            span = pl.ds(step * SPAN, SPAN)
+            outs.append(
+                pltpu.make_async_copy(
+                    grads.at[at, span], grad_out.at[at, span], grad_sems.at[at * steps + step]
+                )
+            )
+            outs[-1].start()
+    for at in (1, 0):
+        states = [jnp.zeros((STATE, HDIM), F32)] * heads
+        for step in range(steps):
+            span = slice(step * SPAN, (step + 1) * SPAN)
             turned = turned_ref[at, :, span].astype(F32)
             lines = lines_ref[at * steps + step]
             for h in range(heads):
@@ -563,18 +545,8 @@
                     [lines[8 * j + h : 8 * j + h + 1] for j in range(CHUNK)], axis=1
                 )
                 decayed = (turned * line).astype(BF16)
-                states[h] = states[h] + dot(decayed, grad[:, head(h)], 1, 0)
-            span = pl.ds(step * SPAN, SPAN)
-            outs.append(
-                pltpu.make_async_copy(
-                    grads.at[at, span], grad_out.at[at, span], grad_sems.at[at * steps + step]
-                )
-            )
-            outs[-1].start()
+                states[h] = states[h] + dot(decayed, grads[at, span, head(h)], 1, 0)
         scatter_pieces(send, 1 - at, states)
-        part = pl.ds((1 - at) * half, half)
-        outs.append(pltpu.make_async_copy(send.at[:, part], send_out.at[:, part], sems.at[at]))
-        outs[-1].start()
     wait_all(outs)
 
 
@@ -630,7 +602,7 @@
               state, packs, sems):
     level, step = 2 - pl.program_id(0), steps - 1 - pl.program_id(1)
     copies = [
-        pltpu.make_async_copy(b_hbm.at[1, 0], b_out, sems.at[0]),
+        pltpu.make_async_copy(b_hbm.at[1, 0, pl.ds(0, SPAN)], b_out, sems.at[0]),
         pltpu.make_async_copy(rows_hbm.at[pl.ds(0, 2 * steps)], rows_out, sems.at[1]),
     ]
 
@@ -654,12 +626,9 @@
         for h in range(heads):
             state_grad_ref[0, 0, h] = state[:, head(h)].T
 
-    @pl.when(level == 1)
+    @pl.when((level == 1) & (step == 0))
     def _():
         near_ref[...] = partial_ref[0, 0]
-
-    @pl.when((level == 1) & (step == 0))
-    def _():
         near_state_ref[...] = state_grad_ref[0, 0]
         wait_all(copies)
 
@@ -668,16 +637,17 @@
                 rows_ref, end_ref, input_grad_out, state_grad_out, b, partial, grads, states, sems,
                 local_sem, out_sems, state_sems):
     chunks = [(level, step) for level in (1, 0) for step in range(steps)]
-    pieces = [(0, step * CHUNK, CHUNK) for step in range(steps)]
+    pieces = [(level, step * CHUNK, CHUNK) for level, step in chunks[1:]]
     copies = piece_copies(
-        [lambda at, span: b_hbm.at[0, 0, span], lambda at, span: partial_hbm.at[0, 0, span]],
+        [lambda at, span: b_hbm.at[at, 0, span], lambda at, span: partial_hbm.at[at, 0, span]],
         [b, partial],
         sems,
         pieces,
     )
     local_copy = pltpu.make_async_copy(local_hbm.at[0, 0], states.at[0], local_sem)
+    start_all(copies[0])
     local_copy.start()
-    for some in copies:
+    for some in copies[1:]:
         start_all(some)
     outs = []
     for i, (level, step) in enumerate(chunks):
@@ -699,11 +669,11 @@
             )
             outs[-1].start()
         span = slice(step * SPAN, (step + 1) * SPAN)
-        if level == 1:
-            some_b, some_partial = b_ref.at[span], partial_ref.at[span]
+        if i == 0:
+            some_b, some_partial = b_ref, partial_ref
         else:
-            wait_all(copies[step])
-            some_b, some_partial = b.at[0, span], partial.at[0, span]
+            wait_all(copies[i - 1])
+            some_b, some_partial = b.at[level, span], partial.at[level, span]
         piece = dot(some_b[...], rounded, 1, 0)
         for j in range(CHUNK):
             extra = piece[block(j)] * spread(columns[step], 0, j, heads)
@@ -741,7 +711,6 @@
     state_shape = (levels, 1, heads, HDIM, STATE)
     state_scratch = pltpu.VMEM((STATE, columns), F32)
     packs_scratch = pltpu.VMEM((steps, BLOCK, 128), F32)
-    pair_scratch = pltpu.VMEM(pair_shape, F32)
     dma = pltpu.SemaphoreType.DMA
 
     far = lambda array: pin(array, pltpu.HBM)
@@ -774,20 +743,19 @@
         "states",
         6,
         in_specs=[anywhere] * 4,
-        out_specs=[anywhere, anywhere],
-        out_shape=[pltpu.HBM(first_shape, F32), pltpu.HBM(rows_shape, F32)],
+        out_specs=[vmem, anywhere],
+        out_shape=[pltpu.VMEM(first_shape, F32), pltpu.HBM(rows_shape, F32)],
         scratch_shapes=[
             pltpu.VMEM((levels * blocks * 8, BLOCK), F32),
             pltpu.VMEM(rows_shape, F32),
             pltpu.VMEM(decay.shape, F32),
-            pltpu.VMEM(first_shape, F32),
             pltpu.VMEM(root_state.shape[1:], F32),
             pair_of_levels(columns),
             pair_of_levels(STATE),
             dma,
             dma,
             dma((4, 2)),
-            dma((3,)),
+            dma,
         ],
     )(decay, root, x, b)
     got = exchange(send)
@@ -814,14 +782,13 @@
     )(far(cum_rows), root, gain, x, gate, b, c, out_grad)
 
     got, sums0 = lax.optimization_barrier((got, sums0))
-    picked = call(
+    picked, decays = call(
         functools.partial(pick_body, heads),
         "pick",
         1,
         in_specs=[smem, vmem],
-        out_specs=anywhere,
-        out_shape=pltpu.HBM(pair_shape, F32),
-        scratch_shapes=[pair_scratch, dma((4,))],
+        out_specs=[vmem, vmem],
+        out_shape=[pltpu.VMEM(pair_shape, F32), pltpu.VMEM((segments, 8, HDIM), F32)],
     )(parent_ids, near(got))
 
     picked, late_rows = lax.optimization_barrier((picked, cum_rows))
@@ -843,16 +810,16 @@
         out_specs=[
             flat(columns, both),
             pl.BlockSpec((1, STATE, SPAN), lambda l, k: (l, 0, k)),
-            pl.BlockSpec((SPAN, columns), lambda l, k: (0, 0)),
+            pl.BlockSpec((FIRST, columns), lambda l, k: (0, 0)),
         ]
         + [anywhere] * 4,
         out_shape=[
             pltpu.HBM((2, length, columns), BF16),
             pltpu.HBM((2, STATE, length), BF16),
-            pltpu.VMEM((SPAN, columns), BF16),
-            pltpu.VMEM((SPAN, columns), BF16),
-            pltpu.VMEM((SPAN, STATE), BF16),
-            pltpu.VMEM((SPAN, columns), BF16),
+            pltpu.VMEM((FIRST, columns), BF16),
+            pltpu.VMEM((FIRST, columns), BF16),
+            pltpu.VMEM((FIRST, STATE), BF16),
+            pltpu.VMEM((FIRST, columns), BF16),
             pltpu.VMEM((2 * steps,) + rows_shape[1:], F32),
         ],
         scratch_shapes=[state_scratch, packs_scratch, dma((4,))],
@@ -863,22 +830,20 @@
         "readout",
         5,
         in_specs=[anywhere] * 5 + [vmem] * 8,
-        out_specs=[vmem] * 4 + [anywhere],
+        out_specs=[vmem] * 5,
         out_shape=[
             pltpu.VMEM((2, length, columns), F32),
             pltpu.VMEM((2, length, columns), F32),
             pltpu.VMEM((2, STATE, length), BF16),
             pltpu.VMEM((2 * steps,) + rows_shape[1:], F32),
-            pltpu.HBM(sums_shape, F32),
+            pltpu.VMEM(sums_shape, F32),
         ],
         scratch_shapes=[
             pair_of_levels(columns),
             pair_of_levels(columns),
             pair_of_levels(columns),
             pair_of_levels(STATE),
-            pltpu.VMEM(sums_shape, F32),
-            dma((2 * steps - 1, 4)),
-            dma,
+            dma((2 * steps, 4)),
             dma,
         ],
     )(
@@ -903,9 +868,9 @@
         "grads",
         4,
         in_specs=[vmem] * 5,
-        out_specs=[anywhere, anywhere],
-        out_shape=[pltpu.HBM((2, length, columns), BF16), pltpu.HBM(pair_shape, F32)],
-        scratch_shapes=[pair_of_levels(columns), pair_scratch, dma((2 * steps,)), dma((2,))],
+        out_specs=[anywhere, vmem],
+        out_shape=[pltpu.HBM((2, length, columns), BF16), pltpu.VMEM(pair_shape, F32)],
+        scratch_shapes=[pair_of_levels(columns), dma((2 * steps,))],
     )(near(lines), near(turned), near(scaled_act), near(gated_act), near(totals))
     got_back = exchange(send_back)
 
@@ -936,16 +901,14 @@
         "fold",
         1,
         in_specs=[smem, vmem, vmem],
-        out_specs=anywhere,
-        out_shape=pltpu.HBM(pair_shape, F32),
-        scratch_shapes=[pair_scratch, dma((2,))],
-    )(parent_ids, got[:, pair_shape[1] :], near(got_back))
+        out_specs=vmem,
+        out_shape=pltpu.VMEM(pair_shape, F32),
+    )(parent_ids, near(decays), near(got_back))
 
     folded, late_rows = lax.optimization_barrier((folded, cum_rows))
     ends = exchange(folded)
     down_back = lambda l, k: (2 - l, steps - 1 - k)
     both_down_back = lambda l, k: (1 - l, steps - 1 - k)
-    late = lambda l, k: (l, jnp.where(l == 0, steps - 1, steps - 1 - k))
     *given, near_partial, near_state, near_b, near_rows = call(
         functools.partial(back_body, heads, steps),
         "back",
@@ -961,7 +924,7 @@
         out_specs=[
             tokens(columns, down_back),
             state_grads(down_back),
-            pl.BlockSpec((SPAN, columns), lambda *g: (late(*g)[1], 0)),
+            pl.BlockSpec((SPAN, columns), lambda *g: (0, 0)),
             pl.BlockSpec((heads, HDIM, STATE), lambda *g: (0, 0, 0)),
             anywhere,
             anywhere,
@@ -969,9 +932,9 @@
         out_shape=[
             pltpu.HBM(ssm_input.shape, BF16),
             pltpu.HBM(state_shape, F32),
-            pltpu.VMEM((length, columns), BF16),
+            pltpu.VMEM((SPAN, columns), BF16),
             pltpu.VMEM(state_shape[2:], F32),
-            pltpu.VMEM((length, STATE), BF16),
+            pltpu.VMEM((SPAN, STATE), BF16),
             pltpu.VMEM((2 * steps,) + rows_shape[1:], F32),
         ],
         input_output_aliases={6: 0, 7: 1},
@@ -987,11 +950,11 @@
         out_shape=[pltpu.HBM(ssm_input.shape, BF16), pltpu.HBM(state_shape, F32)],
         input_output_aliases={1: 0, 2: 1},
         scratch_shapes=[
-            pltpu.VMEM((1, length, STATE), BF16),
-            pltpu.VMEM((1, length, columns), BF16),
+            pair_of_levels(STATE),
+            pair_of_levels(columns),
             pair_of_levels(columns),
             pltpu.VMEM((2,) + state_shape[2:], F32),
-            dma((steps, 2)),
+            dma((2 * steps - 1, 2)),
             dma,
             dma((2 * steps,)),
             dma((2,)),

time: 116 us -> 113 us (0.974)
  local copies, waits for them, and re-layouts: 3.65 us -> 0.02 us
  waiting for transfers between devices: 19.8 us -> 22.2 us
  starting transfers between devices: 20.3 us -> 19 us
    unnamed x14 -> x6, local copies, waits for them, and re-layouts: 3.64 us -> 0.01 us
    all_to_all x1, waiting for transfers between devices: 2.23 us -> 3.84 us  [shards(): starts = exchange(picked)]
    all_to_all x1, starting transfers between devices: 4.92 us -> 3.62 us  [shards(): got_back = exchange(send_back)]
where the time goes in v4:
time: 113 us; the launch traced here: 112 us
  Pallas kernels  57.9 us (51%)
  waiting for transfers between devices  22.2 us (20%)
  starting transfers between devices  19 us (17%)
  blocking collectives  12 us (11%)
    all_to_all x1, blocking collectives, shards(): lax.all_to_all(sums, 'head', split_axis=0, concat_axis=0, tiled=True)  12 us
    pallas_call x1, Pallas kernels, shards(): call(functools.partial(back_body, heads, steps), 'back', 8, grid=(2, step...  9.32 us
    pallas_call x1, Pallas kernels, shards(): call(functools.partial(local_body, heads, steps), 'local', 7, grid=(2, st...  8.98 us
    pallas_call x1, Pallas kernels, shards(): call(functools.partial(forward0_body, heads, steps), 'forward0', 6, grid=...  8.33 us
    all_to_all x1, starting transfers between devices, shards(): got = exchange(send)  8.15 us
    all_to_all x1, waiting for transfers between devices, shards(): got_back = exchange(send_back)  7.56 us
    pallas_call x1, Pallas kernels, shards(): call(functools.partial(back0_body, heads, steps, features), 'back0', 6, g...  7.34 us
    all_to_all x1, waiting for transfers between devices, shards(): got = exchange(send)  6.82 us
  transfers between devices with their start and end apart: 4, of which 4 were waited for; matrix products, arithmetic and copies ran while one was open for 0% of the time, Pallas kernels for 30%

profile of v4, /device:TPU:0, one launch (start us, length us, event | category | flops | bytes accessed | tf_op | source)
XLA Modules:
  0.0 112.0 jit_solution(9954065866491425520)
XLA Ops:
  0.6 0.0 copy-start.2
  0.6 6.6 %states.1 = (f32[16,104,128]{2,1,0:T(8,128)}, f32[6,24,256]{2,1,0:T(8,128)}) custom-call(f32[3,3,1,1536]{3,2,1,0:T(1,128)} %bitcast.1, f32[1,3,128,256]{3,2,1,0:T(8,128)} %root_ref.1, bf16[3,1,1536,384]{3,2,1,0:T(8,128)(2,1)} %x_ref.3, bf16[3,1,1536,256]{3,2,1,0:T(8,128)(2,1)} %b_hbm.5), custom_call_target="tpu_custom_call" | custom-call | flops 6000000000 | bytes 18000000 | tf_op jit(solution)/shard_map/states/pallas_call | solution.py:741
  7.3 8.1 %all-to-all-start = ((f32[16,104,128]{2,1,0:T(8,128)}), f32[16,104,128]{2,1,0:T(8,128)S(1)}, u32[]{:S(2)}, u32[]{:S(2)}) async-start(f32[16,104,128]{2,1,0:T(8,128)} %get-tuple-element.39), calls=%async_computation | async-start | bytes 1703936 | tf_op jit(solution)/shard_map/all_to_all | solution.py:761
  15.4 0.0 copy-done.2
  15.4 0.0 copy-start
  15.5 8.3 %forward0.1 = (bf16[1,1536,384]{2,1,0:T(8,128)(2,1)}, f32[8,384]{1,0:T(8,128)}) custom-call(f32[6,24,256]{2,1,0:T(8,128)} %get-tuple-element.65.rows_ref.rows_hbm, f32[1,3,128,256]{3,2,1,0:T(8,128)} %root_ref.1, f32[1,384]{1,0:T(1,128)S(1)} %reshape.7.gain_ref, bf16[3,1,1536,384]{3,2,1,0:T(8,128)(2,1)} %x_ref.3, bf16[3,1,1536,384]{3,2,1,0:T(8,128)(2,1)} %gate_ref.3, ...), custom_call_target="tpu_custom_call" | custom-call | flops 6000000000 | bytes 18000000 | tf_op jit(solution)/shard_map/forward0/pallas_call | solution.py:764
  23.8 6.8 %all-to-all-done.got_ref = f32[16,104,128]{2,1,0:T(8,128)S(1)} async-done(((f32[16,104,128]{2,1,0:T(8,128)}), f32[16,104,128]{2,1,0:T(8,128)S(1)}, u32[]{:S(2)}, u32[]{:S(2)}) %all-to-all-start) | async-done | bytes 852000 | tf_op jit(solution)/shard_map/all_to_all | solution.py:761
  30.6 0.0 copy-done
  30.6 1.5 %pick.1 = (f32[16,96,128]{2,1,0:T(8,128)}, f32[16,8,128]{2,1,0:T(8,128)S(1)}) custom-call(s32[2,16]{1,0:T(2,128)S(1)} %copy-done, f32[16,104,128]{2,1,0:T(8,128)S(1)} %all-to-all-done.got_ref), custom_call_target="tpu_custom_call" | custom-call | flops 1000000000 | bytes 3000000 | tf_op jit(solution)/shard_map/pick/pallas_call | solution.py:785
  32.1 3.6 %all-to-all-start.1 = ((f32[16,96,128]{2,1,0:T(8,128)}), f32[16,96,128]{2,1,0:T(8,128)S(1)}, u32[]{:S(2)}, u32[]{:S(2)}) async-start(f32[16,96,128]{2,1,0:T(8,128)} %get-tuple-element.53), calls=%async_computation.1 | async-start | bytes 1572864 | tf_op jit(solution)/shard_map/all_to_all | solution.py:795
  35.8 0.0 copy-start.1
  35.8 9.0 %local.1 = (bf16[2,1536,384]{2,1,0:T(8,128)(2,1)}, bf16[2,256,1536]{2,1,0:T(8,128)(2,1)}, bf16[512,384]{1,0:T(8,128)(2,1)S(1)}, bf16[512,384]{1,0:T(8,128)(2,1)S...) custom-call(f32[6,24,256]{2,1,0:T(8,128)} %get-tuple-element.65.rows_ref.rows_hbm, ...), custom_call_target="tpu_custom_call" | custom-call | flops 7000000000 | bytes 21000000 | tf_op jit(solution)/shard_map/local/pallas_call | solution.py:798
  44.8 3.8 %all-to-all-done.1.start_ref = f32[16,96,128]{2,1,0:T(8,128)S(1)} async-done(((f32[16,96,128]{2,1,0:T(8,128)}), f32[16,96,128]{2,1,0:T(8,128)S(1)}, u32[]{:S(2)}, u32[]{:S(2)}) %all-to-all-start.1) | async-done | bytes 786464 | tf_op jit(solution)/shard_map/all_to_all | solution.py:795
  48.6 0.0 copy-done.1
  48.6 5.7 %readout.1 = (f32[2,1536,384]{2,1,0:T(8,128)S(1)}, f32[2,1536,384]{2,1,0:T(8,128)S(1)}, bf16[2,256,1536]{2,1,0:T(8,128)(2,1)S(1)}, f32[4,24,256]{2,1,0:T(8,128)S(1)}, f32[8,8,1152]{2,1,0:T(8,128)S(1)}) custom-call(bf16[2,1536,384]{2,1,0:T(8,128)(2,1)} %get-tuple-element.46.local_hbm, bf16[3,1,1536,384]{3,2,1,0:T(8,128)(2,1)} %gate_ref.3, ...), custom_call_target="tpu_custom_call" | custom-call | flops 5000000000 | bytes 15000000 | tf_op jit(solution)/shard_map/readout/pallas_call | solution.py:828
  54.3 12.0 %all_to_all.25.total_ref = f32[8,8,1152]{2,1,0:T(8,128)S(1)} all-to-all(f32[8,8,1152]{2,1,0:T(8,128)S(1)} %get-tuple-element.59), channel_id=1, replica_groups=mesh['seg'=16,'head'=8] {'head'}, dimensions={0} | all-to-all | bytes 589824 | tf_op jit(solution)/shard_map/all_to_all | solution.py:864
  66.3 3.8 %grads.1 = (bf16[2,1536,384]{2,1,0:T(8,128)(2,1)}, f32[16,96,128]{2,1,0:T(8,128)}) custom-call(f32[4,24,256]{2,1,0:T(8,128)S(1)} %get-tuple-element.55.lines_ref, bf16[2,256,1536]{2,1,0:T(8,128)(2,1)S(1)} %get-tuple-element.56.turned_ref, f32[2,1536,384]{2,1,0:T(8,128)S(1)} %get-tuple-element.57.scaled_act_ref, ...), custom_call_target="tpu_custom_call" | custom-call | flops 4000000000 | bytes 12000000 | tf_op jit(solution)/shard_map/grads/pallas_call | solution.py:866
  70.1 3.6 %all-to-all-start.3 = ((f32[16,96,128]{2,1,0:T(8,128)}), f32[16,96,128]{2,1,0:T(8,128)S(1)}, u32[]{:S(2)}, u32[]{:S(2)}) async-start(f32[16,96,128]{2,1,0:T(8,128)} %get-tuple-element.60), calls=%async_computation.3 | async-start | bytes 1572864 | tf_op jit(solution)/shard_map/all_to_all | solution.py:875
  73.7 7.3 %back0.1 = (bf16[3,1,1536,384]{3,2,1,0:T(8,128)(2,1)}, f32[3,1,3,128,256]{4,3,2,1,0:T(8,128)}) custom-call(f32[6,24,256]{2,1,0:T(8,128)} %get-tuple-element.65.rows_ref.rows_hbm, f32[1,384]{1,0:T(1,128)S(1)} %reshape.7.gain_ref, f32[8,8,1152]{2,1,0:T(8,128)S(1)} %all_to_all.25.total_ref, bf16[3,1,1536,384]{3,2,1,0:T(8,128)(2,1)} %gate_ref.3, ...), custom_call_target="tpu_custom_call" | custom-call | flops 6000000000 | bytes 18000000 | tf_op jit(solution)/shard_map/back0/pallas_call | solution.py:878
  81.1 7.6 %all-to-all-done.3.got_ref = f32[16,96,128]{2,1,0:T(8,128)S(1)} async-done(((f32[16,96,128]{2,1,0:T(8,128)}), f32[16,96,128]{2,1,0:T(8,128)S(1)}, u32[]{:S(2)}, u32[]{:S(2)}) %all-to-all-start.3) | async-done | bytes 786464 | tf_op jit(solution)/shard_map/all_to_all | solution.py:875
  88.6 1.8 %fold.1 = f32[16,96,128]{2,1,0:T(8,128)} custom-call(s32[2,16]{1,0:T(2,128)S(1)} %copy-done, f32[16,8,128]{2,1,0:T(8,128)S(1)} %get-tuple-element.43.decay_ref, f32[16,96,128]{2,1,0:T(8,128)S(1)} %all-to-all-done.3.got_ref), custom_call_target="tpu_custom_call" | custom-call | flops 1000000000 | bytes 3000000 | tf_op jit(solution)/shard_map/fold/pallas_call | solution.py:899
  90.4 3.6 %all-to-all-start.4 = ((f32[16,96,128]{2,1,0:T(8,128)}), f32[16,96,128]{2,1,0:T(8,128)S(1)}, u32[]{:S(2)}, u32[]{:S(2)}) async-start(f32[16,96,128]{2,1,0:T(8,128)} %fold.1), calls=%async_computation.4 | async-start | bytes 1572864 | tf_op jit(solution)/shard_map/all_to_all | solution.py:909
  94.0 9.3 %back.1 = (bf16[3,1,1536,384]{3,2,1,0:T(8,128)(2,1)}, f32[3,1,3,128,256]{4,3,2,1,0:T(8,128)}, bf16[768,384]{1,0:T(8,128)(2,1)S(1)}, f32[3,128,256]{2,1,0:T(8,128...) custom-call(f32[6,24,256]{2,1,0:T(8,128)} %get-tuple-element.65.rows, ...), custom_call_target="tpu_custom_call", output_to_operand_aliasing={{0}: (6, {}), {1}: (7, {})} | custom-call | flops 8000000000 | bytes 24000000 | tf_op jit(solution)/shard_map/back/pallas_call | solution.py:912
  103.3 4.0 %all-to-all-done.4.end_ref = f32[16,96,128]{2,1,0:T(8,128)S(1)} async-done(((f32[16,96,128]{2,1,0:T(8,128)}), f32[16,96,128]{2,1,0:T(8,128)S(1)}, u32[]{:S(2)}, u32[]{:S(2)}) %all-to-all-start.4) | async-done | bytes 786464 | tf_op jit(solution)/shard_map/all_to_all | solution.py:909
  107.3 4.6 %inputs.1 = (bf16[3,1,1536,384]{3,2,1,0:T(8,128)(2,1)}, f32[3,1,3,128,256]{4,3,2,1,0:T(8,128)}) custom-call(bf16[3,1,1536,256]{3,2,1,0:T(8,128)(2,1)} %b_hbm.5, bf16[3,1,1536,384]{3,2,1,0:T(8,128)(2,1)} %get-tuple-element.69.partial_hbm, f32[3,1,3,128,256]{4,3,2,1,0:T(8,128)} %get-tuple-element.70.local_hbm, ...), custom_call_target="tpu_custom_call", output_to_operand_aliasing={{0}: (1, {}), {1}: (2, {})} | custom-call | flops 4000000000 | bytes 12000000 | tf_op jit(solution)/shard_map/inputs/pallas_call | solution.py:944
  (1 shorter events, 0.0 us)
Async XLA Ops:
  0.6 14.8 %copy-start.2 = (f32[384]{0:T(512)S(1)}, f32[384]{0:T(512)}, u32[]{:S(2)}) copy-start(f32[384]{0:T(512)} %param.15) | copy-start | bytes 4612
  7.3 23.3 %all-to-all-start = ((f32[16,104,128]{2,1,0:T(8,128)}), f32[16,104,128]{2,1,0:T(8,128)S(1)}, u32[]{:S(2)}, u32[]{:S(2)}) async-start(f32[16,104,128]{2,1,0:T(8,128)} %get-tuple-element.39), calls=%async_computation | async-start | bytes 1703936 | tf_op jit(solution)/shard_map/all_to_all | solution.py:761
  15.4 15.2 %copy-start = (s32[2,16]{1,0:T(2,128)S(1)}, s32[2,16]{1,0:T(2,128)}, u32[]{:S(2)}) copy-start(s32[2,16]{1,0:T(2,128)} %parent_ref.3) | copy-start | bytes 388
  32.1 16.5 %all-to-all-start.1 = ((f32[16,96,128]{2,1,0:T(8,128)}), f32[16,96,128]{2,1,0:T(8,128)S(1)}, u32[]{:S(2)}, u32[]{:S(2)}) async-start(f32[16,96,128]{2,1,0:T(8,128)} %get-tuple-element.53), calls=%async_computation.1 | async-start | bytes 1572864 | tf_op jit(solution)/shard_map/all_to_all | solution.py:795
  35.8 12.8 %copy-start.1 = (f32[8,384]{1,0:T(8,128)S(1)}, f32[8,384]{1,0:T(8,128)}, u32[]{:S(2)}) copy-start(f32[8,384]{1,0:T(8,128)} %get-tuple-element.54.first_sums_ref) | copy-start | bytes 36868
  70.1 18.5 %all-to-all-start.3 = ((f32[16,96,128]{2,1,0:T(8,128)}), f32[16,96,128]{2,1,0:T(8,128)S(1)}, u32[]{:S(2)}, u32[]{:S(2)}) async-start(f32[16,96,128]{2,1,0:T(8,128)} %get-tuple-element.60), calls=%async_computation.3 | async-start | bytes 1572864 | tf_op jit(solution)/shard_map/all_to_all | solution.py:875
  90.4 16.9 %all-to-all-start.4 = ((f32[16,96,128]{2,1,0:T(8,128)}), f32[16,96,128]{2,1,0:T(8,128)S(1)}, u32[]{:S(2)}, u32[]{:S(2)}) async-start(f32[16,96,128]{2,1,0:T(8,128)} %fold.1), calls=%async_computation.4 | async-start | bytes 1572864 | tf_op jit(solution)/shard_map/all_to_all | solution.py:909

commit v5 on v4

--- a/solution.py
+++ b/solution.py
@@ -346,18 +346,18 @@
     act = silu(gate.astype(F32))
     gated = ssm_out * act
     scaled = out_grad.astype(F32) * gain
-    squares = jnp.sum(gated * gated, axis=1, keepdims=True)
-    products = jnp.sum(scaled * gated, axis=1, keepdims=True)
-    pair = jnp.concatenate([squares, products, jnp.zeros((BLOCK, 6), F32)], axis=1).T
-    return gated, scaled * act, gated * act, pair
+    ones = jnp.ones((8, gated.shape[1]), BF16)
+    squares = dot(ones, (gated * gated).astype(BF16), 1, 1)
+    products = dot(ones, (scaled * gated).astype(BF16), 1, 1)
+    return gated, scaled * act, gated * act, (squares[:1], products[:1])
 
 
 def store_sums(sums, step, at, pairs):
-    both = jnp.concatenate(pairs, axis=1)
     for q in range(2):
+        line = jnp.concatenate([pair[q] for pair in pairs], axis=1)
         for half in range(2):
-            sums[4 * step + 2 * q + half : 4 * step + 2 * q + half + 1, at : at + FOLD] = both[
-                q : q + 1, half * FOLD : (half + 1) * FOLD
+            sums[4 * step + 2 * q + half : 4 * step + 2 * q + half + 1, at : at + FOLD] = line[
+                :, half * FOLD : (half + 1) * FOLD
             ]
 
 

time: 113 us -> 112 us (level)
  Pallas kernels: 57.9 us -> 56.5 us
where the time goes in v5:
time: 112 us; the launch traced here: 111 us
  Pallas kernels  56.5 us (50%)
  waiting for transfers between devices  23 us (21%)
  starting transfers between devices  19 us (17%)
  blocking collectives  12 us (11%)
    all_to_all x1, blocking collectives, shards(): lax.all_to_all(sums, 'head', split_axis=0, concat_axis=0, tiled=True)  12 us
    pallas_call x1, Pallas kernels, shards(): call(functools.partial(back_body, heads, steps), 'back', 8, grid=(2, step...  9.31 us
    pallas_call x1, Pallas kernels, shards(): call(functools.partial(local_body, heads, steps), 'local', 7, grid=(2, st...  8.98 us
    all_to_all x1, starting transfers between devices, shards(): got = exchange(send)  8.15 us
    all_to_all x1, waiting for transfers between devices, shards(): got = exchange(send)  7.61 us
    all_to_all x1, waiting for transfers between devices, shards(): got_back = exchange(send_back)  7.56 us
    pallas_call x1, Pallas kernels, shards(): call(functools.partial(forward0_body, heads, steps), 'forward0', 6, grid=...  7.55 us
    pallas_call x1, Pallas kernels, shards(): call(functools.partial(back0_body, heads, steps, features), 'back0', 6, g...  7.33 us
  transfers between devices with their start and end apart: 4, of which 4 were waited for; matrix products, arithmetic and copies ran while one was open for 0% of the time, Pallas kernels for 30%

profile of v5, /device:TPU:0, one launch (start us, length us, event | category | flops | bytes accessed | tf_op | source)
XLA Modules:
  0.0 111.5 jit_solution(14440966507957480387)
XLA Ops:
  0.6 0.0 copy-start.2
  0.6 6.6 %states.1 = (f32[16,104,128]{2,1,0:T(8,128)}, f32[6,24,256]{2,1,0:T(8,128)}) custom-call(f32[3,3,1,1536]{3,2,1,0:T(1,128)} %bitcast.1, f32[1,3,128,256]{3,2,1,0:T(8,128)} %root_ref.1, bf16[3,1,1536,384]{3,2,1,0:T(8,128)(2,1)} %x_ref.3, bf16[3,1,1536,256]{3,2,1,0:T(8,128)(2,1)} %b_hbm.5), custom_call_target="tpu_custom_call" | custom-call | flops 6000000000 | bytes 18000000 | tf_op jit(solution)/shard_map/states/pallas_call | solution.py:741
  7.3 8.1 %all-to-all-start = ((f32[16,104,128]{2,1,0:T(8,128)}), f32[16,104,128]{2,1,0:T(8,128)S(1)}, u32[]{:S(2)}, u32[]{:S(2)}) async-start(f32[16,104,128]{2,1,0:T(8,128)} %get-tuple-element.39), calls=%async_computation | async-start | bytes 1703936 | tf_op jit(solution)/shard_map/all_to_all | solution.py:761
  15.4 0.0 copy-done.2
  15.4 0.0 copy-start
  15.5 7.5 %forward0.1 = (bf16[1,1536,384]{2,1,0:T(8,128)(2,1)}, f32[8,384]{1,0:T(8,128)}) custom-call(f32[6,24,256]{2,1,0:T(8,128)} %get-tuple-element.65.rows_ref.rows_hbm, f32[1,3,128,256]{3,2,1,0:T(8,128)} %root_ref.1, f32[1,384]{1,0:T(1,128)S(1)} %reshape.7.gain_ref, bf16[3,1,1536,384]{3,2,1,0:T(8,128)(2,1)} %x_ref.3, bf16[3,1,1536,384]{3,2,1,0:T(8,128)(2,1)} %gate_ref.3, ...), custom_call_target="tpu_custom_call" | custom-call | flops 6000000000 | bytes 18000000 | tf_op jit(solution)/shard_map/forward0/pallas_call | solution.py:764
  23.0 7.6 %all-to-all-done.got_ref = f32[16,104,128]{2,1,0:T(8,128)S(1)} async-done(((f32[16,104,128]{2,1,0:T(8,128)}), f32[16,104,128]{2,1,0:T(8,128)S(1)}, u32[]{:S(2)}, u32[]{:S(2)}) %all-to-all-start) | async-done | bytes 852000 | tf_op jit(solution)/shard_map/all_to_all | solution.py:761
  30.6 0.0 copy-done
  30.6 1.5 %pick.1 = (f32[16,96,128]{2,1,0:T(8,128)}, f32[16,8,128]{2,1,0:T(8,128)S(1)}) custom-call(s32[2,16]{1,0:T(2,128)S(1)} %copy-done, f32[16,104,128]{2,1,0:T(8,128)S(1)} %all-to-all-done.got_ref), custom_call_target="tpu_custom_call" | custom-call | flops 1000000000 | bytes 3000000 | tf_op jit(solution)/shard_map/pick/pallas_call | solution.py:785
  32.1 3.6 %all-to-all-start.1 = ((f32[16,96,128]{2,1,0:T(8,128)}), f32[16,96,128]{2,1,0:T(8,128)S(1)}, u32[]{:S(2)}, u32[]{:S(2)}) async-start(f32[16,96,128]{2,1,0:T(8,128)} %get-tuple-element.53), calls=%async_computation.1 | async-start | bytes 1572864 | tf_op jit(solution)/shard_map/all_to_all | solution.py:795
  35.8 0.0 copy-start.1
  35.8 9.0 %local.1 = (bf16[2,1536,384]{2,1,0:T(8,128)(2,1)}, bf16[2,256,1536]{2,1,0:T(8,128)(2,1)}, bf16[512,384]{1,0:T(8,128)(2,1)S(1)}, bf16[512,384]{1,0:T(8,128)(2,1)S...) custom-call(f32[6,24,256]{2,1,0:T(8,128)} %get-tuple-element.65.rows_ref.rows_hbm, ...), custom_call_target="tpu_custom_call" | custom-call | flops 7000000000 | bytes 21000000 | tf_op jit(solution)/shard_map/local/pallas_call | solution.py:798
  44.8 3.8 %all-to-all-done.1.start_ref = f32[16,96,128]{2,1,0:T(8,128)S(1)} async-done(((f32[16,96,128]{2,1,0:T(8,128)}), f32[16,96,128]{2,1,0:T(8,128)S(1)}, u32[]{:S(2)}, u32[]{:S(2)}) %all-to-all-start.1) | async-done | bytes 786464 | tf_op jit(solution)/shard_map/all_to_all | solution.py:795
  48.6 0.0 copy-done.1
  48.6 5.2 %readout.1 = (f32[2,1536,384]{2,1,0:T(8,128)S(1)}, f32[2,1536,384]{2,1,0:T(8,128)S(1)}, bf16[2,256,1536]{2,1,0:T(8,128)(2,1)S(1)}, f32[4,24,256]{2,1,0:T(8,128)S(1)}, f32[8,8,1152]{2,1,0:T(8,128)S(1)}) custom-call(bf16[2,1536,384]{2,1,0:T(8,128)(2,1)} %get-tuple-element.46.local_hbm, bf16[3,1,1536,384]{3,2,1,0:T(8,128)(2,1)} %gate_ref.3, ...), custom_call_target="tpu_custom_call" | custom-call | flops 5000000000 | bytes 15000000 | tf_op jit(solution)/shard_map/readout/pallas_call | solution.py:828
  53.8 12.0 %all_to_all.25.total_ref = f32[8,8,1152]{2,1,0:T(8,128)S(1)} all-to-all(f32[8,8,1152]{2,1,0:T(8,128)S(1)} %get-tuple-element.59), channel_id=1, replica_groups=mesh['seg'=16,'head'=8] {'head'}, dimensions={0} | all-to-all | bytes 589824 | tf_op jit(solution)/shard_map/all_to_all | solution.py:864
  65.8 3.8 %grads.1 = (bf16[2,1536,384]{2,1,0:T(8,128)(2,1)}, f32[16,96,128]{2,1,0:T(8,128)}) custom-call(f32[4,24,256]{2,1,0:T(8,128)S(1)} %get-tuple-element.55.lines_ref, bf16[2,256,1536]{2,1,0:T(8,128)(2,1)S(1)} %get-tuple-element.56.turned_ref, f32[2,1536,384]{2,1,0:T(8,128)S(1)} %get-tuple-element.57.scaled_act_ref, ...), custom_call_target="tpu_custom_call" | custom-call | flops 4000000000 | bytes 12000000 | tf_op jit(solution)/shard_map/grads/pallas_call | solution.py:866
  69.5 3.6 %all-to-all-start.3 = ((f32[16,96,128]{2,1,0:T(8,128)}), f32[16,96,128]{2,1,0:T(8,128)S(1)}, u32[]{:S(2)}, u32[]{:S(2)}) async-start(f32[16,96,128]{2,1,0:T(8,128)} %get-tuple-element.60), calls=%async_computation.3 | async-start | bytes 1572864 | tf_op jit(solution)/shard_map/all_to_all | solution.py:875
  73.2 7.3 %back0.1 = (bf16[3,1,1536,384]{3,2,1,0:T(8,128)(2,1)}, f32[3,1,3,128,256]{4,3,2,1,0:T(8,128)}) custom-call(f32[6,24,256]{2,1,0:T(8,128)} %get-tuple-element.65.rows_ref.rows_hbm, f32[1,384]{1,0:T(1,128)S(1)} %reshape.7.gain_ref, f32[8,8,1152]{2,1,0:T(8,128)S(1)} %all_to_all.25.total_ref, bf16[3,1,1536,384]{3,2,1,0:T(8,128)(2,1)} %gate_ref.3, ...), custom_call_target="tpu_custom_call" | custom-call | flops 6000000000 | bytes 18000000 | tf_op jit(solution)/shard_map/back0/pallas_call | solution.py:878
  80.5 7.6 %all-to-all-done.3.got_ref = f32[16,96,128]{2,1,0:T(8,128)S(1)} async-done(((f32[16,96,128]{2,1,0:T(8,128)}), f32[16,96,128]{2,1,0:T(8,128)S(1)}, u32[]{:S(2)}, u32[]{:S(2)}) %all-to-all-start.3) | async-done | bytes 786464 | tf_op jit(solution)/shard_map/all_to_all | solution.py:875
  88.1 1.8 %fold.1 = f32[16,96,128]{2,1,0:T(8,128)} custom-call(s32[2,16]{1,0:T(2,128)S(1)} %copy-done, f32[16,8,128]{2,1,0:T(8,128)S(1)} %get-tuple-element.43.decay_ref, f32[16,96,128]{2,1,0:T(8,128)S(1)} %all-to-all-done.3.got_ref), custom_call_target="tpu_custom_call" | custom-call | flops 1000000000 | bytes 3000000 | tf_op jit(solution)/shard_map/fold/pallas_call | solution.py:899
  89.8 3.6 %all-to-all-start.4 = ((f32[16,96,128]{2,1,0:T(8,128)}), f32[16,96,128]{2,1,0:T(8,128)S(1)}, u32[]{:S(2)}, u32[]{:S(2)}) async-start(f32[16,96,128]{2,1,0:T(8,128)} %fold.1), calls=%async_computation.4 | async-start | bytes 1572864 | tf_op jit(solution)/shard_map/all_to_all | solution.py:909
  93.4 9.3 %back.1 = (bf16[3,1,1536,384]{3,2,1,0:T(8,128)(2,1)}, f32[3,1,3,128,256]{4,3,2,1,0:T(8,128)}, bf16[768,384]{1,0:T(8,128)(2,1)S(1)}, f32[3,128,256]{2,1,0:T(8,128...) custom-call(f32[6,24,256]{2,1,0:T(8,128)} %get-tuple-element.65.rows, ...), custom_call_target="tpu_custom_call", output_to_operand_aliasing={{0}: (6, {}), {1}: (7, {})} | custom-call | flops 8000000000 | bytes 24000000 | tf_op jit(solution)/shard_map/back/pallas_call | solution.py:912
  102.8 4.0 %all-to-all-done.4.end_ref = f32[16,96,128]{2,1,0:T(8,128)S(1)} async-done(((f32[16,96,128]{2,1,0:T(8,128)}), f32[16,96,128]{2,1,0:T(8,128)S(1)}, u32[]{:S(2)}, u32[]{:S(2)}) %all-to-all-start.4) | async-done | bytes 786464 | tf_op jit(solution)/shard_map/all_to_all | solution.py:909
  106.7 4.5 %inputs.1 = (bf16[3,1,1536,384]{3,2,1,0:T(8,128)(2,1)}, f32[3,1,3,128,256]{4,3,2,1,0:T(8,128)}) custom-call(bf16[3,1,1536,256]{3,2,1,0:T(8,128)(2,1)} %b_hbm.5, bf16[3,1,1536,384]{3,2,1,0:T(8,128)(2,1)} %get-tuple-element.69.partial_hbm, f32[3,1,3,128,256]{4,3,2,1,0:T(8,128)} %get-tuple-element.70.local_hbm, ...), custom_call_target="tpu_custom_call", output_to_operand_aliasing={{0}: (1, {}), {1}: (2, {})} | custom-call | flops 4000000000 | bytes 12000000 | tf_op jit(solution)/shard_map/inputs/pallas_call | solution.py:944
  (1 shorter events, 0.0 us)
Async XLA Ops:
  0.6 14.8 %copy-start.2 = (f32[384]{0:T(512)S(1)}, f32[384]{0:T(512)}, u32[]{:S(2)}) copy-start(f32[384]{0:T(512)} %param.15) | copy-start | bytes 4612
  7.3 23.3 %all-to-all-start = ((f32[16,104,128]{2,1,0:T(8,128)}), f32[16,104,128]{2,1,0:T(8,128)S(1)}, u32[]{:S(2)}, u32[]{:S(2)}) async-start(f32[16,104,128]{2,1,0:T(8,128)} %get-tuple-element.39), calls=%async_computation | async-start | bytes 1703936 | tf_op jit(solution)/shard_map/all_to_all | solution.py:761
  15.4 15.2 %copy-start = (s32[2,16]{1,0:T(2,128)S(1)}, s32[2,16]{1,0:T(2,128)}, u32[]{:S(2)}) copy-start(s32[2,16]{1,0:T(2,128)} %parent_ref.3) | copy-start | bytes 388
  32.1 16.5 %all-to-all-start.1 = ((f32[16,96,128]{2,1,0:T(8,128)}), f32[16,96,128]{2,1,0:T(8,128)S(1)}, u32[]{:S(2)}, u32[]{:S(2)}) async-start(f32[16,96,128]{2,1,0:T(8,128)} %get-tuple-element.53), calls=%async_computation.1 | async-start | bytes 1572864 | tf_op jit(solution)/shard_map/all_to_all | solution.py:795
  35.8 12.8 %copy-start.1 = (f32[8,384]{1,0:T(8,128)S(1)}, f32[8,384]{1,0:T(8,128)}, u32[]{:S(2)}) copy-start(f32[8,384]{1,0:T(8,128)} %get-tuple-element.54.first_sums_ref) | copy-start | bytes 36868
  69.5 18.5 %all-to-all-start.3 = ((f32[16,96,128]{2,1,0:T(8,128)}), f32[16,96,128]{2,1,0:T(8,128)S(1)}, u32[]{:S(2)}, u32[]{:S(2)}) async-start(f32[16,96,128]{2,1,0:T(8,128)} %get-tuple-element.60), calls=%async_computation.3 | async-start | bytes 1572864 | tf_op jit(solution)/shard_map/all_to_all | solution.py:875
  89.8 16.9 %all-to-all-start.4 = ((f32[16,96,128]{2,1,0:T(8,128)}), f32[16,96,128]{2,1,0:T(8,128)S(1)}, u32[]{:S(2)}, u32[]{:S(2)}) async-start(f32[16,96,128]{2,1,0:T(8,128)} %fold.1), calls=%async_computation.4 | async-start | bytes 1572864 | tf_op jit(solution)/shard_map/all_to_all | solution.py:909

commit v6 on v5

--- a/solution.py
+++ b/solution.py
@@ -68,6 +68,15 @@
         ],
         axis=1,
     )
+
+
+def spread_rows(lines, width):
+    high = lines.astype(BF16)
+    low = (lines - high.astype(F32)).astype(BF16)
+    row = lax.broadcasted_iota(jnp.int32, (16, width), 0)
+    lane = lax.broadcasted_iota(jnp.int32, (16, width), 1)
+    chosen = jnp.where((row & 7) == (lane >> 7), 1.0, 0.0).astype(BF16)
+    return dot(jnp.concatenate([high, low], axis=0), chosen, 0, 0)
 
 
 def block(j):
@@ -361,13 +370,13 @@
             ]
 
 
-def norm_columns(total, step, at, features):
+def norm_rows(total, step, at, features):
     lines = [total[4 * step + i : 4 * step + i + 1, at : at + FOLD] for i in range(4)]
     squares = jnp.concatenate(lines[:2], axis=1) / features
     dots = jnp.concatenate(lines[2:], axis=1) / features
     inv_rms = lax.rsqrt(squares + EPSILON)
     back = inv_rms * inv_rms * inv_rms * dots
-    return jnp.concatenate([inv_rms, back, jnp.zeros((6, SPAN), F32)], axis=0).T
+    return jnp.concatenate([inv_rms, back, jnp.zeros((6, SPAN), F32)], axis=0)
 
 
 def ssm_gradient(j, norm, gain, gate, out_grad, gated):
@@ -479,12 +488,11 @@
     copies.append([turned_copy])
     start_all(copies[0] + copies[1])
     sums[0, :, :FOLD] = first_sums_ref[...]
-    columns = []
+    decays = []
     for at in range(2):
-        decays = level_decays(rows_ref.at[pl.ds(at * steps, steps)], False)
-        for step, line in enumerate(decays):
-            lines[at * steps + step] = line
-            columns.append(line.T)
+        decays += level_decays(rows_ref.at[pl.ds(at * steps, steps)], False)
+    for chunk, line in enumerate(decays):
+        lines[chunk] = line
     pairs = []
     for i, (at, first, count) in enumerate([(0, 0, early)] + pieces):
         if first == 0:
@@ -502,7 +510,8 @@
         for number in range(first, first + count):
             step, j = number // CHUNK, number % CHUNK
             mine = block(number - first)
-            carried = piece[mine] * spread(columns[at * steps + step], 0, j, heads)
+            line = decays[at * steps + step][8 * j : 8 * j + 8]
+            carried = piece[mine] * spread_rows(line, heads * HDIM)
             place = block(number)
             _, scaled_act[at, place], gated_act[at, place], pair = gated_sums(
                 carried + refs[1][mine].astype(F32), refs[2][mine], refs[3][mine], gain_ref[...]
@@ -522,11 +531,15 @@
     outs = []
     for at in (1, 0):
         for step in range(steps):
-            norm = norm_columns(total, step, (at + 1) * FOLD, features)
-            span = slice(step * SPAN, (step + 1) * SPAN)
-            inv_rms, back = norm[:, 0:1], norm[:, 1:2]
-            grad = inv_rms * scaled_act_ref[at, span] - back * gated_act_ref[at, span]
-            grads[at, span] = grad.astype(BF16)
+            norm = norm_rows(total, step, (at + 1) * FOLD, features)
+            for j in range(CHUNK):
+                place = block(step * CHUNK + j)
+                factors = spread_rows(norm[:, block(j)], 2 * HDIM)
+                inv_rms, back = factors[:, :HDIM], factors[:, HDIM:]
+                for h in range(heads):
+                    grad = inv_rms * scaled_act_ref[at, place, head(h)]
+                    grad = grad - back * gated_act_ref[at, place, head(h)]
+                    grads[at, place, head(h)] = grad.astype(BF16)
             span = pl.ds(step * SPAN, SPAN)
             outs.append(
                 pltpu.make_async_copy(
@@ -573,7 +586,7 @@
         pack(rows_ref, packs)
         total = jnp.sum(total_ref[...], axis=0)
         for part in range(steps):
-            norms[part] = norm_columns(total, part, 0, features)
+            norms[part] = norm_rows(total, part, 0, features).T
         state[...] = jnp.zeros_like(state)
 
     norm = norms[step]
@@ -655,7 +668,7 @@
             ends = [gather_pieces(end_ref, 1 - level, h, heads) for h in range(heads)]
             rounded = jnp.concatenate(ends, axis=1).astype(BF16)
             level_rows = rows_ref.at[pl.ds(level * steps, steps)]
-            columns = [line.T for line in level_decays(level_rows, True)]
+            decays = level_decays(level_rows, True)
             total = level_decays(level_rows, False)[-1][8 * (CHUNK - 1) :, BLOCK - 1 :]
             if level == 0:
                 local_copy.wait()
@@ -676,7 +689,8 @@
             some_b, some_partial = b.at[level, span], partial.at[level, span]
         piece = dot(some_b[...], rounded, 1, 0)
         for j in range(CHUNK):
-            extra = piece[block(j)] * spread(columns[step], 0, j, heads)
+            line = decays[step][8 * j : 8 * j + 8]
+            extra = piece[block(j)] * spread_rows(line, heads * HDIM)
             grads[level, block(step * CHUNK + j)] = (
                 some_partial[block(j)].astype(F32) + extra
             ).astype(BF16)

time: 112 us -> 113 us (level)
    pallas_call x1, Pallas kernels: 5.15 us -> 6.52 us  [shards(): call(functools.partial(readout_body, heads, steps), 'readout', 5, in_spec...]
where the time goes in v6:
time: 113 us; the launch traced here: 112 us
  Pallas kernels  57 us (50%)
  waiting for transfers between devices  23.1 us (20%)
  starting transfers between devices  19 us (17%)
  blocking collectives  12 us (11%)
    all_to_all x1, blocking collectives, shards(): lax.all_to_all(sums, 'head', split_axis=0, concat_axis=0, tiled=True)  12 us
    pallas_call x1, Pallas kernels, shards(): call(functools.partial(back_body, heads, steps), 'back', 8, grid=(2, step...  9.3 us
    pallas_call x1, Pallas kernels, shards(): call(functools.partial(local_body, heads, steps), 'local', 7, grid=(2, st...  8.96 us
    all_to_all x1, starting transfers between devices, shards(): got = exchange(send)  8.15 us
    all_to_all x1, waiting for transfers between devices, shards(): got = exchange(send)  7.61 us
    all_to_all x1, waiting for transfers between devices, shards(): got_back = exchange(send_back)  7.6 us
    pallas_call x1, Pallas kernels, shards(): call(functools.partial(forward0_body, heads, steps), 'forward0', 6, grid=...  7.55 us
    pallas_call x1, Pallas kernels, shards(): call(functools.partial(back0_body, heads, steps, features), 'back0', 6, g...  7.33 us
  transfers between devices with their start and end apart: 4, of which 4 were waited for; matrix products, arithmetic and copies ran while one was open for 0% of the time, Pallas kernels for 30%

profile of v6, /device:TPU:0, one launch (start us, length us, event | category | flops | bytes accessed | tf_op | source)
XLA Modules:
  0.0 112.0 jit_solution(1129745552782256890)
XLA Ops:
  0.6 0.0 copy-start.2
  0.6 6.6 %states.1 = (f32[16,104,128]{2,1,0:T(8,128)}, f32[6,24,256]{2,1,0:T(8,128)}) custom-call(f32[3,3,1,1536]{3,2,1,0:T(1,128)} %bitcast.1, f32[1,3,128,256]{3,2,1,0:T(8,128)} %root_ref.1, bf16[3,1,1536,384]{3,2,1,0:T(8,128)(2,1)} %x_ref.3, bf16[3,1,1536,256]{3,2,1,0:T(8,128)(2,1)} %b_hbm.5), custom_call_target="tpu_custom_call" | custom-call | flops 6000000000 | bytes 18000000 | tf_op jit(solution)/shard_map/states/pallas_call | solution.py:755
  7.3 8.1 %all-to-all-start = ((f32[16,104,128]{2,1,0:T(8,128)}), f32[16,104,128]{2,1,0:T(8,128)S(1)}, u32[]{:S(2)}, u32[]{:S(2)}) async-start(f32[16,104,128]{2,1,0:T(8,128)} %get-tuple-element.39), calls=%async_computation | async-start | bytes 1703936 | tf_op jit(solution)/shard_map/all_to_all | solution.py:775
  15.4 0.0 copy-done.2
  15.4 0.0 copy-start
  15.5 7.5 %forward0.1 = (bf16[1,1536,384]{2,1,0:T(8,128)(2,1)}, f32[8,384]{1,0:T(8,128)}) custom-call(f32[6,24,256]{2,1,0:T(8,128)} %get-tuple-element.65.rows_ref.rows_hbm, f32[1,3,128,256]{3,2,1,0:T(8,128)} %root_ref.1, f32[1,384]{1,0:T(1,128)S(1)} %reshape.7.gain_ref, bf16[3,1,1536,384]{3,2,1,0:T(8,128)(2,1)} %x_ref.3, bf16[3,1,1536,384]{3,2,1,0:T(8,128)(2,1)} %gate_ref.3, ...), custom_call_target="tpu_custom_call" | custom-call | flops 6000000000 | bytes 18000000 | tf_op jit(solution)/shard_map/forward0/pallas_call | solution.py:778
  23.0 7.6 %all-to-all-done.got_ref = f32[16,104,128]{2,1,0:T(8,128)S(1)} async-done(((f32[16,104,128]{2,1,0:T(8,128)}), f32[16,104,128]{2,1,0:T(8,128)S(1)}, u32[]{:S(2)}, u32[]{:S(2)}) %all-to-all-start) | async-done | bytes 852000 | tf_op jit(solution)/shard_map/all_to_all | solution.py:775
  30.6 0.0 copy-done
  30.6 1.5 %pick.1 = (f32[16,96,128]{2,1,0:T(8,128)}, f32[16,8,128]{2,1,0:T(8,128)S(1)}) custom-call(s32[2,16]{1,0:T(2,128)S(1)} %copy-done, f32[16,104,128]{2,1,0:T(8,128)S(1)} %all-to-all-done.got_ref), custom_call_target="tpu_custom_call" | custom-call | flops 1000000000 | bytes 3000000 | tf_op jit(solution)/shard_map/pick/pallas_call | solution.py:799
  32.1 3.6 %all-to-all-start.1 = ((f32[16,96,128]{2,1,0:T(8,128)}), f32[16,96,128]{2,1,0:T(8,128)S(1)}, u32[]{:S(2)}, u32[]{:S(2)}) async-start(f32[16,96,128]{2,1,0:T(8,128)} %get-tuple-element.53), calls=%async_computation.1 | async-start | bytes 1572864 | tf_op jit(solution)/shard_map/all_to_all | solution.py:809
  35.8 0.0 copy-start.1
  35.8 9.0 %local.1 = (bf16[2,1536,384]{2,1,0:T(8,128)(2,1)}, bf16[2,256,1536]{2,1,0:T(8,128)(2,1)}, bf16[512,384]{1,0:T(8,128)(2,1)S(1)}, bf16[512,384]{1,0:T(8,128)(2,1)S...) custom-call(f32[6,24,256]{2,1,0:T(8,128)} %get-tuple-element.65.rows_ref.rows_hbm, ...), custom_call_target="tpu_custom_call" | custom-call | flops 7000000000 | bytes 21000000 | tf_op jit(solution)/shard_map/local/pallas_call | solution.py:812
  44.8 3.9 %all-to-all-done.1.start_ref = f32[16,96,128]{2,1,0:T(8,128)S(1)} async-done(((f32[16,96,128]{2,1,0:T(8,128)}), f32[16,96,128]{2,1,0:T(8,128)S(1)}, u32[]{:S(2)}, u32[]{:S(2)}) %all-to-all-start.1) | async-done | bytes 786464 | tf_op jit(solution)/shard_map/all_to_all | solution.py:809
  48.6 0.0 copy-done.1
  48.6 6.5 %readout.1 = (f32[2,1536,384]{2,1,0:T(8,128)S(1)}, f32[2,1536,384]{2,1,0:T(8,128)S(1)}, bf16[2,256,1536]{2,1,0:T(8,128)(2,1)S(1)}, f32[4,24,256]{2,1,0:T(8,128)S(1)}, f32[8,8,1152]{2,1,0:T(8,128)S(1)}) custom-call(bf16[2,1536,384]{2,1,0:T(8,128)(2,1)} %get-tuple-element.46.local_hbm, bf16[3,1,1536,384]{3,2,1,0:T(8,128)(2,1)} %gate_ref.3, ...), custom_call_target="tpu_custom_call" | custom-call | flops 5000000000 | bytes 15000000 | tf_op jit(solution)/shard_map/readout/pallas_call | solution.py:842
  55.1 12.0 %all_to_all.25.total_ref = f32[8,8,1152]{2,1,0:T(8,128)S(1)} all-to-all(f32[8,8,1152]{2,1,0:T(8,128)S(1)} %get-tuple-element.59), channel_id=1, replica_groups=mesh['seg'=16,'head'=8] {'head'}, dimensions={0} | all-to-all | bytes 589824 | tf_op jit(solution)/shard_map/all_to_all | solution.py:878
  67.1 3.3 %grads.1 = (bf16[2,1536,384]{2,1,0:T(8,128)(2,1)}, f32[16,96,128]{2,1,0:T(8,128)}) custom-call(f32[4,24,256]{2,1,0:T(8,128)S(1)} %get-tuple-element.55.lines_ref, bf16[2,256,1536]{2,1,0:T(8,128)(2,1)S(1)} %get-tuple-element.56.turned_ref, f32[2,1536,384]{2,1,0:T(8,128)S(1)} %get-tuple-element.57.scaled_act_ref, ...), custom_call_target="tpu_custom_call" | custom-call | flops 4000000000 | bytes 12000000 | tf_op jit(solution)/shard_map/grads/pallas_call | solution.py:880
  70.4 3.6 %all-to-all-start.3 = ((f32[16,96,128]{2,1,0:T(8,128)}), f32[16,96,128]{2,1,0:T(8,128)S(1)}, u32[]{:S(2)}, u32[]{:S(2)}) async-start(f32[16,96,128]{2,1,0:T(8,128)} %get-tuple-element.60), calls=%async_computation.3 | async-start | bytes 1572864 | tf_op jit(solution)/shard_map/all_to_all | solution.py:889
  74.0 7.3 %back0.1 = (bf16[3,1,1536,384]{3,2,1,0:T(8,128)(2,1)}, f32[3,1,3,128,256]{4,3,2,1,0:T(8,128)}) custom-call(f32[6,24,256]{2,1,0:T(8,128)} %get-tuple-element.65.rows_ref.rows_hbm, f32[1,384]{1,0:T(1,128)S(1)} %reshape.7.gain_ref, f32[8,8,1152]{2,1,0:T(8,128)S(1)} %all_to_all.25.total_ref, bf16[3,1,1536,384]{3,2,1,0:T(8,128)(2,1)} %gate_ref.3, ...), custom_call_target="tpu_custom_call" | custom-call | flops 6000000000 | bytes 18000000 | tf_op jit(solution)/shard_map/back0/pallas_call | solution.py:892
  81.4 7.6 %all-to-all-done.3.got_ref = f32[16,96,128]{2,1,0:T(8,128)S(1)} async-done(((f32[16,96,128]{2,1,0:T(8,128)}), f32[16,96,128]{2,1,0:T(8,128)S(1)}, u32[]{:S(2)}, u32[]{:S(2)}) %all-to-all-start.3) | async-done | bytes 786464 | tf_op jit(solution)/shard_map/all_to_all | solution.py:889
  89.0 1.7 %fold.1 = f32[16,96,128]{2,1,0:T(8,128)} custom-call(s32[2,16]{1,0:T(2,128)S(1)} %copy-done, f32[16,8,128]{2,1,0:T(8,128)S(1)} %get-tuple-element.43.decay_ref, f32[16,96,128]{2,1,0:T(8,128)S(1)} %all-to-all-done.3.got_ref), custom_call_target="tpu_custom_call" | custom-call | flops 1000000000 | bytes 3000000 | tf_op jit(solution)/shard_map/fold/pallas_call | solution.py:913
  90.7 3.6 %all-to-all-start.4 = ((f32[16,96,128]{2,1,0:T(8,128)}), f32[16,96,128]{2,1,0:T(8,128)S(1)}, u32[]{:S(2)}, u32[]{:S(2)}) async-start(f32[16,96,128]{2,1,0:T(8,128)} %fold.1), calls=%async_computation.4 | async-start | bytes 1572864 | tf_op jit(solution)/shard_map/all_to_all | solution.py:923
  94.3 9.3 %back.1 = (bf16[3,1,1536,384]{3,2,1,0:T(8,128)(2,1)}, f32[3,1,3,128,256]{4,3,2,1,0:T(8,128)}, bf16[768,384]{1,0:T(8,128)(2,1)S(1)}, f32[3,128,256]{2,1,0:T(8,128...) custom-call(f32[6,24,256]{2,1,0:T(8,128)} %get-tuple-element.65.rows, ...), custom_call_target="tpu_custom_call", output_to_operand_aliasing={{0}: (6, {}), {1}: (7, {})} | custom-call | flops 8000000000 | bytes 24000000 | tf_op jit(solution)/shard_map/back/pallas_call | solution.py:926
  103.6 4.0 %all-to-all-done.4.end_ref = f32[16,96,128]{2,1,0:T(8,128)S(1)} async-done(((f32[16,96,128]{2,1,0:T(8,128)}), f32[16,96,128]{2,1,0:T(8,128)S(1)}, u32[]{:S(2)}, u32[]{:S(2)}) %all-to-all-start.4) | async-done | bytes 786464 | tf_op jit(solution)/shard_map/all_to_all | solution.py:923
  107.7 4.2 %inputs.1 = (bf16[3,1,1536,384]{3,2,1,0:T(8,128)(2,1)}, f32[3,1,3,128,256]{4,3,2,1,0:T(8,128)}) custom-call(bf16[3,1,1536,256]{3,2,1,0:T(8,128)(2,1)} %b_hbm.5, bf16[3,1,1536,384]{3,2,1,0:T(8,128)(2,1)} %get-tuple-element.69.partial_hbm, f32[3,1,3,128,256]{4,3,2,1,0:T(8,128)} %get-tuple-element.70.local_hbm, ...), custom_call_target="tpu_custom_call", output_to_operand_aliasing={{0}: (1, {}), {1}: (2, {})} | custom-call | flops 4000000000 | bytes 12000000 | tf_op jit(solution)/shard_map/inputs/pallas_call | solution.py:958
  (1 shorter events, 0.0 us)
Async XLA Ops:
  0.6 14.8 %copy-start.2 = (f32[384]{0:T(512)S(1)}, f32[384]{0:T(512)}, u32[]{:S(2)}) copy-start(f32[384]{0:T(512)} %param.15) | copy-start | bytes 4612
  7.3 23.3 %all-to-all-start = ((f32[16,104,128]{2,1,0:T(8,128)}), f32[16,104,128]{2,1,0:T(8,128)S(1)}, u32[]{:S(2)}, u32[]{:S(2)}) async-start(f32[16,104,128]{2,1,0:T(8,128)} %get-tuple-element.39), calls=%async_computation | async-start | bytes 1703936 | tf_op jit(solution)/shard_map/all_to_all | solution.py:775
  15.4 15.2 %copy-start = (s32[2,16]{1,0:T(2,128)S(1)}, s32[2,16]{1,0:T(2,128)}, u32[]{:S(2)}) copy-start(s32[2,16]{1,0:T(2,128)} %parent_ref.3) | copy-start | bytes 388
  32.1 16.5 %all-to-all-start.1 = ((f32[16,96,128]{2,1,0:T(8,128)}), f32[16,96,128]{2,1,0:T(8,128)S(1)}, u32[]{:S(2)}, u32[]{:S(2)}) async-start(f32[16,96,128]{2,1,0:T(8,128)} %get-tuple-element.53), calls=%async_computation.1 | async-start | bytes 1572864 | tf_op jit(solution)/shard_map/all_to_all | solution.py:809
  35.8 12.8 %copy-start.1 = (f32[8,384]{1,0:T(8,128)S(1)}, f32[8,384]{1,0:T(8,128)}, u32[]{:S(2)}) copy-start(f32[8,384]{1,0:T(8,128)} %get-tuple-element.54.first_sums_ref) | copy-start | bytes 36868
  70.4 18.6 %all-to-all-start.3 = ((f32[16,96,128]{2,1,0:T(8,128)}), f32[16,96,128]{2,1,0:T(8,128)S(1)}, u32[]{:S(2)}, u32[]{:S(2)}) async-start(f32[16,96,128]{2,1,0:T(8,128)} %get-tuple-element.60), calls=%async_computation.3 | async-start | bytes 1572864 | tf_op jit(solution)/shard_map/all_to_all | solution.py:889
  90.7 16.9 %all-to-all-start.4 = ((f32[16,96,128]{2,1,0:T(8,128)}), f32[16,96,128]{2,1,0:T(8,128)S(1)}, u32[]{:S(2)}, u32[]{:S(2)}) async-start(f32[16,96,128]{2,1,0:T(8,128)} %fold.1), calls=%async_computation.4 | async-start | bytes 1572864 | tf_op jit(solution)/shard_map/all_to_all | solution.py:923

commit v7 on v6

--- a/solution.py
+++ b/solution.py
@@ -491,8 +491,10 @@
     decays = []
     for at in range(2):
         decays += level_decays(rows_ref.at[pl.ds(at * steps, steps)], False)
+    columns = []
     for chunk, line in enumerate(decays):
         lines[chunk] = line
+        columns.append(line.T)
     pairs = []
     for i, (at, first, count) in enumerate([(0, 0, early)] + pieces):
         if first == 0:
@@ -510,8 +512,7 @@
         for number in range(first, first + count):
             step, j = number // CHUNK, number % CHUNK
             mine = block(number - first)
-            line = decays[at * steps + step][8 * j : 8 * j + 8]
-            carried = piece[mine] * spread_rows(line, heads * HDIM)
+            carried = piece[mine] * spread(columns[at * steps + step], 0, j, heads)
             place = block(number)
             _, scaled_act[at, place], gated_act[at, place], pair = gated_sums(
                 carried + refs[1][mine].astype(F32), refs[2][mine], refs[3][mine], gain_ref[...]

time: 113 us -> 111 us (0.982)
  Pallas kernels: 57 us -> 55.7 us
    pallas_call x1, Pallas kernels: 6.52 us -> 5.16 us  [shards(): call(functools.partial(readout_body, heads, steps), 'readout', 5, in_spec...]
where the time goes in v7:
time: 111 us
  Pallas kernels  55.7 us (50%)
  waiting for transfers between devices  23 us (21%)
  starting transfers between devices  19 us (17%)
  blocking collectives  12 us (11%)
    all_to_all x1, blocking collectives, shards(): lax.all_to_all(sums, 'head', split_axis=0, concat_axis=0, tiled=True)  12 us
    pallas_call x1, Pallas kernels, shards(): call(functools.partial(back_body, heads, steps), 'back', 8, grid=(2, step...  9.31 us
    pallas_call x1, Pallas kernels, shards(): call(functools.partial(local_body, heads, steps), 'local', 7, grid=(2, st...  8.97 us
    all_to_all x1, starting transfers between devices, shards(): got = exchange(send)  8.15 us
    all_to_all x1, waiting for transfers between devices, shards(): got = exchange(send)  7.61 us
    all_to_all x1, waiting for transfers between devices, shards(): got_back = exchange(send_back)  7.57 us
    pallas_call x1, Pallas kernels, shards(): call(functools.partial(forward0_body, heads, steps), 'forward0', 6, grid=...  7.55 us
    pallas_call x1, Pallas kernels, shards(): call(functools.partial(back0_body, heads, steps, features), 'back0', 6, g...  7.34 us
  transfers between devices with their start and end apart: 4, of which 4 were waited for; matrix products, arithmetic and copies ran while one was open for 0% of the time, Pallas kernels for 30%

profile of v7, /device:TPU:0, one launch (start us, length us, event | category | flops | bytes accessed | tf_op | source)
XLA Modules:
  0.0 110.6 jit_solution(1615625398761610245)
XLA Ops:
  0.6 0.0 copy-start.2
  0.6 6.6 %states.1 = (f32[16,104,128]{2,1,0:T(8,128)}, f32[6,24,256]{2,1,0:T(8,128)}) custom-call(f32[3,3,1,1536]{3,2,1,0:T(1,128)} %bitcast.1, f32[1,3,128,256]{3,2,1,0:T(8,128)} %root_ref.1, bf16[3,1,1536,384]{3,2,1,0:T(8,128)(2,1)} %x_ref.3, bf16[3,1,1536,256]{3,2,1,0:T(8,128)(2,1)} %b_hbm.5), custom_call_target="tpu_custom_call" | custom-call | flops 6000000000 | bytes 18000000 | tf_op jit(solution)/shard_map/states/pallas_call | solution.py:756
  7.3 8.1 %all-to-all-start = ((f32[16,104,128]{2,1,0:T(8,128)}), f32[16,104,128]{2,1,0:T(8,128)S(1)}, u32[]{:S(2)}, u32[]{:S(2)}) async-start(f32[16,104,128]{2,1,0:T(8,128)} %get-tuple-element.39), calls=%async_computation | async-start | bytes 1703936 | tf_op jit(solution)/shard_map/all_to_all | solution.py:776
  15.4 0.0 copy-done.2
  15.4 0.0 copy-start
  15.5 7.5 %forward0.1 = (bf16[1,1536,384]{2,1,0:T(8,128)(2,1)}, f32[8,384]{1,0:T(8,128)}) custom-call(f32[6,24,256]{2,1,0:T(8,128)} %get-tuple-element.65.rows_ref.rows_hbm, f32[1,3,128,256]{3,2,1,0:T(8,128)} %root_ref.1, f32[1,384]{1,0:T(1,128)S(1)} %reshape.7.gain_ref, bf16[3,1,1536,384]{3,2,1,0:T(8,128)(2,1)} %x_ref.3, bf16[3,1,1536,384]{3,2,1,0:T(8,128)(2,1)} %gate_ref.3, ...), custom_call_target="tpu_custom_call" | custom-call | flops 6000000000 | bytes 18000000 | tf_op jit(solution)/shard_map/forward0/pallas_call | solution.py:779
  23.0 7.6 %all-to-all-done.got_ref = f32[16,104,128]{2,1,0:T(8,128)S(1)} async-done(((f32[16,104,128]{2,1,0:T(8,128)}), f32[16,104,128]{2,1,0:T(8,128)S(1)}, u32[]{:S(2)}, u32[]{:S(2)}) %all-to-all-start) | async-done | bytes 852000 | tf_op jit(solution)/shard_map/all_to_all | solution.py:776
  30.6 0.0 copy-done
  30.6 1.5 %pick.1 = (f32[16,96,128]{2,1,0:T(8,128)}, f32[16,8,128]{2,1,0:T(8,128)S(1)}) custom-call(s32[2,16]{1,0:T(2,128)S(1)} %copy-done, f32[16,104,128]{2,1,0:T(8,128)S(1)} %all-to-all-done.got_ref), custom_call_target="tpu_custom_call" | custom-call | flops 1000000000 | bytes 3000000 | tf_op jit(solution)/shard_map/pick/pallas_call | solution.py:800
  32.1 3.6 %all-to-all-start.1 = ((f32[16,96,128]{2,1,0:T(8,128)}), f32[16,96,128]{2,1,0:T(8,128)S(1)}, u32[]{:S(2)}, u32[]{:S(2)}) async-start(f32[16,96,128]{2,1,0:T(8,128)} %get-tuple-element.53), calls=%async_computation.1 | async-start | bytes 1572864 | tf_op jit(solution)/shard_map/all_to_all | solution.py:810
  35.8 0.0 copy-start.1
  35.8 9.0 %local.1 = (bf16[2,1536,384]{2,1,0:T(8,128)(2,1)}, bf16[2,256,1536]{2,1,0:T(8,128)(2,1)}, bf16[512,384]{1,0:T(8,128)(2,1)S(1)}, bf16[512,384]{1,0:T(8,128)(2,1)S...) custom-call(f32[6,24,256]{2,1,0:T(8,128)} %get-tuple-element.65.rows_ref.rows_hbm, ...), custom_call_target="tpu_custom_call" | custom-call | flops 7000000000 | bytes 21000000 | tf_op jit(solution)/shard_map/local/pallas_call | solution.py:813
  44.7 3.8 %all-to-all-done.1.start_ref = f32[16,96,128]{2,1,0:T(8,128)S(1)} async-done(((f32[16,96,128]{2,1,0:T(8,128)}), f32[16,96,128]{2,1,0:T(8,128)S(1)}, u32[]{:S(2)}, u32[]{:S(2)}) %all-to-all-start.1) | async-done | bytes 786464 | tf_op jit(solution)/shard_map/all_to_all | solution.py:810
  48.6 0.0 copy-done.1
  48.6 5.2 %readout.1 = (f32[2,1536,384]{2,1,0:T(8,128)S(1)}, f32[2,1536,384]{2,1,0:T(8,128)S(1)}, bf16[2,256,1536]{2,1,0:T(8,128)(2,1)S(1)}, f32[4,24,256]{2,1,0:T(8,128)S(1)}, f32[8,8,1152]{2,1,0:T(8,128)S(1)}) custom-call(bf16[2,1536,384]{2,1,0:T(8,128)(2,1)} %get-tuple-element.46.local_hbm, bf16[3,1,1536,384]{3,2,1,0:T(8,128)(2,1)} %gate_ref.3, ...), custom_call_target="tpu_custom_call" | custom-call | flops 5000000000 | bytes 15000000 | tf_op jit(solution)/shard_map/readout/pallas_call | solution.py:843
  53.8 12.0 %all_to_all.25.total_ref = f32[8,8,1152]{2,1,0:T(8,128)S(1)} all-to-all(f32[8,8,1152]{2,1,0:T(8,128)S(1)} %get-tuple-element.59), channel_id=1, replica_groups=mesh['seg'=16,'head'=8] {'head'}, dimensions={0} | all-to-all | bytes 589824 | tf_op jit(solution)/shard_map/all_to_all | solution.py:879
  65.8 3.3 %grads.1 = (bf16[2,1536,384]{2,1,0:T(8,128)(2,1)}, f32[16,96,128]{2,1,0:T(8,128)}) custom-call(f32[4,24,256]{2,1,0:T(8,128)S(1)} %get-tuple-element.55.lines_ref, bf16[2,256,1536]{2,1,0:T(8,128)(2,1)S(1)} %get-tuple-element.56.turned_ref, f32[2,1536,384]{2,1,0:T(8,128)S(1)} %get-tuple-element.57.scaled_act_ref, ...), custom_call_target="tpu_custom_call" | custom-call | flops 4000000000 | bytes 12000000 | tf_op jit(solution)/shard_map/grads/pallas_call | solution.py:881
  69.0 3.6 %all-to-all-start.3 = ((f32[16,96,128]{2,1,0:T(8,128)}), f32[16,96,128]{2,1,0:T(8,128)S(1)}, u32[]{:S(2)}, u32[]{:S(2)}) async-start(f32[16,96,128]{2,1,0:T(8,128)} %get-tuple-element.60), calls=%async_computation.3 | async-start | bytes 1572864 | tf_op jit(solution)/shard_map/all_to_all | solution.py:890
  72.7 7.3 %back0.1 = (bf16[3,1,1536,384]{3,2,1,0:T(8,128)(2,1)}, f32[3,1,3,128,256]{4,3,2,1,0:T(8,128)}) custom-call(f32[6,24,256]{2,1,0:T(8,128)} %get-tuple-element.65.rows_ref.rows_hbm, f32[1,384]{1,0:T(1,128)S(1)} %reshape.7.gain_ref, f32[8,8,1152]{2,1,0:T(8,128)S(1)} %all_to_all.25.total_ref, bf16[3,1,1536,384]{3,2,1,0:T(8,128)(2,1)} %gate_ref.3, ...), custom_call_target="tpu_custom_call" | custom-call | flops 6000000000 | bytes 18000000 | tf_op jit(solution)/shard_map/back0/pallas_call | solution.py:893
  80.0 7.6 %all-to-all-done.3.got_ref = f32[16,96,128]{2,1,0:T(8,128)S(1)} async-done(((f32[16,96,128]{2,1,0:T(8,128)}), f32[16,96,128]{2,1,0:T(8,128)S(1)}, u32[]{:S(2)}, u32[]{:S(2)}) %all-to-all-start.3) | async-done | bytes 786464 | tf_op jit(solution)/shard_map/all_to_all | solution.py:890
  87.6 1.8 %fold.1 = f32[16,96,128]{2,1,0:T(8,128)} custom-call(s32[2,16]{1,0:T(2,128)S(1)} %copy-done, f32[16,8,128]{2,1,0:T(8,128)S(1)} %get-tuple-element.43.decay_ref, f32[16,96,128]{2,1,0:T(8,128)S(1)} %all-to-all-done.3.got_ref), custom_call_target="tpu_custom_call" | custom-call | flops 1000000000 | bytes 3000000 | tf_op jit(solution)/shard_map/fold/pallas_call | solution.py:914
  89.3 3.6 %all-to-all-start.4 = ((f32[16,96,128]{2,1,0:T(8,128)}), f32[16,96,128]{2,1,0:T(8,128)S(1)}, u32[]{:S(2)}, u32[]{:S(2)}) async-start(f32[16,96,128]{2,1,0:T(8,128)} %fold.1), calls=%async_computation.4 | async-start | bytes 1572864 | tf_op jit(solution)/shard_map/all_to_all | solution.py:924
  93.0 9.3 %back.1 = (bf16[3,1,1536,384]{3,2,1,0:T(8,128)(2,1)}, f32[3,1,3,128,256]{4,3,2,1,0:T(8,128)}, bf16[768,384]{1,0:T(8,128)(2,1)S(1)}, f32[3,128,256]{2,1,0:T(8,128...) custom-call(f32[6,24,256]{2,1,0:T(8,128)} %get-tuple-element.65.rows, ...), custom_call_target="tpu_custom_call", output_to_operand_aliasing={{0}: (6, {}), {1}: (7, {})} | custom-call | flops 8000000000 | bytes 24000000 | tf_op jit(solution)/shard_map/back/pallas_call | solution.py:927
  102.3 4.0 %all-to-all-done.4.end_ref = f32[16,96,128]{2,1,0:T(8,128)S(1)} async-done(((f32[16,96,128]{2,1,0:T(8,128)}), f32[16,96,128]{2,1,0:T(8,128)S(1)}, u32[]{:S(2)}, u32[]{:S(2)}) %all-to-all-start.4) | async-done | bytes 786464 | tf_op jit(solution)/shard_map/all_to_all | solution.py:924
  106.3 4.2 %inputs.1 = (bf16[3,1,1536,384]{3,2,1,0:T(8,128)(2,1)}, f32[3,1,3,128,256]{4,3,2,1,0:T(8,128)}) custom-call(bf16[3,1,1536,256]{3,2,1,0:T(8,128)(2,1)} %b_hbm.5, bf16[3,1,1536,384]{3,2,1,0:T(8,128)(2,1)} %get-tuple-element.69.partial_hbm, f32[3,1,3,128,256]{4,3,2,1,0:T(8,128)} %get-tuple-element.70.local_hbm, ...), custom_call_target="tpu_custom_call", output_to_operand_aliasing={{0}: (1, {}), {1}: (2, {})} | custom-call | flops 4000000000 | bytes 12000000 | tf_op jit(solution)/shard_map/inputs/pallas_call | solution.py:959
  (1 shorter events, 0.0 us)
Async XLA Ops:
  0.6 14.8 %copy-start.2 = (f32[384]{0:T(512)S(1)}, f32[384]{0:T(512)}, u32[]{:S(2)}) copy-start(f32[384]{0:T(512)} %param.15) | copy-start | bytes 4612
  7.3 23.3 %all-to-all-start = ((f32[16,104,128]{2,1,0:T(8,128)}), f32[16,104,128]{2,1,0:T(8,128)S(1)}, u32[]{:S(2)}, u32[]{:S(2)}) async-start(f32[16,104,128]{2,1,0:T(8,128)} %get-tuple-element.39), calls=%async_computation | async-start | bytes 1703936 | tf_op jit(solution)/shard_map/all_to_all | solution.py:776
  15.4 15.2 %copy-start = (s32[2,16]{1,0:T(2,128)S(1)}, s32[2,16]{1,0:T(2,128)}, u32[]{:S(2)}) copy-start(s32[2,16]{1,0:T(2,128)} %parent_ref.3) | copy-start | bytes 388
  32.1 16.5 %all-to-all-start.1 = ((f32[16,96,128]{2,1,0:T(8,128)}), f32[16,96,128]{2,1,0:T(8,128)S(1)}, u32[]{:S(2)}, u32[]{:S(2)}) async-start(f32[16,96,128]{2,1,0:T(8,128)} %get-tuple-element.53), calls=%async_computation.1 | async-start | bytes 1572864 | tf_op jit(solution)/shard_map/all_to_all | solution.py:810
  35.8 12.8 %copy-start.1 = (f32[8,384]{1,0:T(8,128)S(1)}, f32[8,384]{1,0:T(8,128)}, u32[]{:S(2)}) copy-start(f32[8,384]{1,0:T(8,128)} %get-tuple-element.54.first_sums_ref) | copy-start | bytes 36868
  69.0 18.5 %all-to-all-start.3 = ((f32[16,96,128]{2,1,0:T(8,128)}), f32[16,96,128]{2,1,0:T(8,128)S(1)}, u32[]{:S(2)}, u32[]{:S(2)}) async-start(f32[16,96,128]{2,1,0:T(8,128)} %get-tuple-element.60), calls=%async_computation.3 | async-start | bytes 1572864 | tf_op jit(solution)/shard_map/all_to_all | solution.py:890
  89.3 16.9 %all-to-all-start.4 = ((f32[16,96,128]{2,1,0:T(8,128)}), f32[16,96,128]{2,1,0:T(8,128)S(1)}, u32[]{:S(2)}, u32[]{:S(2)}) async-start(f32[16,96,128]{2,1,0:T(8,128)} %fold.1), calls=%async_computation.4 | async-start | bytes 1572864 | tf_op jit(solution)/shard_map/all_to_all | solution.py:924

commit v8 on v6

--- a/solution.py
+++ b/solution.py
@@ -124,6 +124,15 @@
         copy.wait()
 
 
+def part_copies(send, send_out, sems):
+    half = send.shape[1] // 16 * 8
+    parts = [pl.ds(0, half), pl.ds(half, send.shape[1] - half)]
+    return [
+        pltpu.make_async_copy(send.at[:, part], send_out.at[:, part], sems.at[i])
+        for i, part in enumerate(parts)
+    ]
+
+
 def piece_copies(sources, targets, sems, pieces):
     result = []
     for i, (at, first, count) in enumerate(pieces):
@@ -148,8 +157,8 @@
     return lasts, before, after
 
 
-def states_body(heads, steps, decay_hbm, root_hbm, x_hbm, b_hbm, send, rows_out, rates, rows, decay,
-                root, x, b, decay_sem, root_sem, sems, out_sem):
+def states_body(heads, steps, decay_hbm, root_hbm, x_hbm, b_hbm, send_out, rows_out, rates, rows,
+                decay, send, root, x, b, decay_sem, root_sem, sems, out_sem, send_sems):
     blocks = steps * CHUNK
     decay_copy = pltpu.make_async_copy(decay_hbm, decay, decay_sem)
     decay_copy.start()
@@ -201,9 +210,11 @@
 
     root_copy.wait()
     states = [(root[h] * totals[0][h : h + 1]).T for h in range(heads)]
+    outs = part_copies(send, send_out, send_sems)
     for i, (level, first, count) in enumerate(pieces):
         if (level, first) == (1, 0):
             scatter_pieces(send, 0, states)
+            outs[0].start()
             states = [jnp.zeros((STATE, HDIM), F32)] * heads
         wait_all(copies[i])
         if i > 0:
@@ -223,7 +234,8 @@
     decays = jnp.broadcast_to(totals[1], (8, HDIM))
     for piece in range(send.shape[0]):
         send[piece, send.shape[1] - 8 :] = decays
-    rows_copy.wait()
+    outs[1].start()
+    wait_all(outs + [rows_copy])
 
 
 def level_decays(rows, to_end):
@@ -261,11 +273,13 @@
         ).T
 
 
-def pick_body(heads, parent_ref, got_ref, send, decay_out):
+def pick_body(heads, parent_ref, got_ref, send_out, decay_out, send, sems):
     segments = got_ref.shape[0]
     rows = STATE // segments
     pair = send.shape[1]
     half = pair // 2
+    quarter = segments // 4
+    copies = []
     for seg in range(segments):
         first = parent_ref[0, seg]
         second = parent_ref[1, seg]
@@ -277,15 +291,24 @@
             a = slice(h * rows, (h + 1) * rows)
             b = slice(half + h * rows, half + (h + 1) * rows)
             send[seg, b] = decay[h : h + 1] * got_ref[root, a] + got_ref[second, b]
-
-
-def fold_body(heads, parent_ref, decay_ref, got_ref, send):
+        if (seg + 1) % quarter == 0:
+            part = pl.ds(seg + 1 - quarter, quarter)
+            copies.append(
+                pltpu.make_async_copy(send.at[part], send_out.at[part], sems.at[len(copies)])
+            )
+            copies[-1].start()
+    wait_all(copies)
+
+
+def fold_body(heads, parent_ref, decay_ref, got_ref, send_out, send, sems):
     rows = STATE // got_ref.shape[0]
     half = send.shape[1] // 2
     send[...] = jnp.zeros_like(send)
     for seg in range(got_ref.shape[0]):
         second = parent_ref[1, seg]
         send[second, :half] += got_ref[seg, :half]
+    copies = part_copies(send, send_out, sems)
+    copies[0].start()
     for seg in range(got_ref.shape[0]):
         first = parent_ref[0, seg]
         decay = decay_ref[seg]
@@ -293,6 +316,8 @@
             a = slice(h * rows, (h + 1) * rows)
             b = slice(half + h * rows, half + (h + 1) * rows)
             send[first, b] += decay[h : h + 1] * send[seg, a] + got_ref[seg, b]
+    copies[1].start()
+    wait_all(copies)
 
 
 def causal_mask(transposed):
@@ -418,7 +443,23 @@
             store_sums(sums_ref, part, 0, pairs)
 
 
-def local_body(heads, steps, rows_ref, x_ref, b_ref, c_ref, gate_hbm, c_hbm, out_grad_hbm,
+def scale_body(heads, steps, rows_ref, c_ref, out_ref, lines):
+    step = pl.program_id(1)
+
+    @pl.when(step == 0)
+    def _():
+        for part, line in enumerate(level_decays(rows_ref, False)):
+            lines[part] = line
+
+    columns = lines[step].T
+    for j in range(CHUNK):
+        c = c_ref[0, 0, block(j)].astype(F32)
+        for h in range(heads):
+            decay = columns[:, 8 * j + h : 8 * j + h + 1]
+            out_ref[0, h, block(j)] = (c * decay).astype(BF16)
+
+
+def local_body(heads, steps, rows_ref, x_ref, b_ref, c_ref, gate_hbm, scaled_hbm, out_grad_hbm,
                rows_hbm, out_ref, turned_ref, first_ref, gate_out, c_out, out_grad_out, rows_out,
                state, packs, sems):
     level, step = pl.program_id(0), pl.program_id(1)
@@ -428,7 +469,7 @@
         for i, (source, target) in enumerate(
             [
                 (gate_hbm.at[1, 0, span], gate_out),
-                (c_hbm.at[1, 0, span], c_out),
+                (scaled_hbm.at[0, :, span], c_out),
                 (out_grad_hbm.at[1, 0, span], out_grad_out),
                 (rows_hbm.at[pl.ds(steps, 2 * steps)], rows_out),
             ]
@@ -466,7 +507,7 @@
         wait_all(copies)
 
 
-def readout_body(heads, steps, local_hbm, gate_hbm, c_hbm, out_grad_hbm, turned_hbm, local_ref,
+def readout_body(heads, steps, local_hbm, gate_hbm, scaled_hbm, out_grad_hbm, turned_hbm, local_ref,
                  gate_ref, c_ref, out_grad_ref, rows_ref, start_ref, gain_ref, first_sums_ref,
                  scaled_act, gated_act, turned, lines, sums, local, gate, out_grad, c, sems,
                  turned_sem):
@@ -475,12 +516,12 @@
     pieces += [(at, step * CHUNK, CHUNK) for at in range(2) for step in range(steps)][1:]
     copies = piece_copies(
         [
-            lambda at, span: c_hbm.at[at + 1, 0, span],
             lambda at, span: local_hbm.at[at, span],
             lambda at, span: gate_hbm.at[at + 1, 0, span],
             lambda at, span: out_grad_hbm.at[at + 1, 0, span],
-        ],
-        [c, local, gate, out_grad],
+        ]
+        + [lambda at, span, h=h: scaled_hbm.at[at, h, span] for h in range(heads)],
+        [local, gate, out_grad] + [c.at[h] for h in range(heads)],
         sems,
         pieces,
     )
@@ -496,25 +537,25 @@
     pairs = []
     for i, (at, first, count) in enumerate([(0, 0, early)] + pieces):
         if first == 0:
-            start = jnp.concatenate(
-                [gather_pieces(start_ref, at, h, heads) for h in range(heads)], axis=1
-            ).astype(BF16)
+            starts = [gather_pieces(start_ref, at, h, heads).astype(BF16) for h in range(heads)]
         if i == 0:
-            refs = [c_ref, local_ref, gate_ref, out_grad_ref]
+            refs = [local_ref, gate_ref, out_grad_ref]
+            scaled = [c_ref.at[h] for h in range(heads)]
         else:
             wait_all(copies[i - 1])
             start_all(sum(copies[i + 1 : i + 2], []))
             span = slice(first * BLOCK, (first + count) * BLOCK)
-            refs = [buffer.at[at, span] for buffer in (c, local, gate, out_grad)]
-        piece = dot(refs[0][...], start, 1, 0)
+            refs = [buffer.at[at, span] for buffer in (local, gate, out_grad)]
+            scaled = [c.at[h, at, span] for h in range(heads)]
+        piece = jnp.concatenate(
+            [dot(scaled[h][...], starts[h], 1, 0) for h in range(heads)], axis=1
+        )
         for number in range(first, first + count):
             step, j = number // CHUNK, number % CHUNK
             mine = block(number - first)
-            line = decays[at * steps + step][8 * j : 8 * j + 8]
-            carried = piece[mine] * spread_rows(line, heads * HDIM)
             place = block(number)
             _, scaled_act[at, place], gated_act[at, place], pair = gated_sums(
-                carried + refs[1][mine].astype(F32), refs[2][mine], refs[3][mine], gain_ref[...]
+                piece[mine] + refs[0][mine].astype(F32), refs[1][mine], refs[2][mine], gain_ref[...]
             )
             pairs.append(pair)
             if j == CHUNK - 1:
@@ -526,8 +567,9 @@
 
 
 def grads_body(heads, steps, features, lines_ref, turned_ref, scaled_act_ref, gated_act_ref,
-               total_ref, grad_out, send, grads, grad_sems):
+               total_ref, grad_out, send_out, grads, send, grad_sems, sems):
     total = jnp.sum(total_ref[...], axis=0)
+    sends = part_copies(send, send_out, sems)
     outs = []
     for at in (1, 0):
         for step in range(steps):
@@ -560,6 +602,8 @@
                 decayed = (turned * line).astype(BF16)
                 states[h] = states[h] + dot(decayed, grads[at, span, head(h)], 1, 0)
         scatter_pieces(send, 1 - at, states)
+        outs.append(sends[1 - at])
+        outs[-1].start()
     wait_all(outs)
 
 
@@ -757,12 +801,13 @@
         "states",
         6,
         in_specs=[anywhere] * 4,
-        out_specs=[vmem, anywhere],
-        out_shape=[pltpu.VMEM(first_shape, F32), pltpu.HBM(rows_shape, F32)],
+        out_specs=[anywhere, anywhere],
+        out_shape=[pltpu.HBM(first_shape, F32), pltpu.HBM(rows_shape, F32)],
         scratch_shapes=[
             pltpu.VMEM((levels * blocks * 8, BLOCK), F32),
             pltpu.VMEM(rows_shape, F32),
             pltpu.VMEM(decay.shape, F32),
+            pltpu.VMEM(first_shape, F32),
             pltpu.VMEM(root_state.shape[1:], F32),
             pair_of_levels(columns),
             pair_of_levels(STATE),
@@ -770,6 +815,7 @@
             dma,
             dma((4, 2)),
             dma,
+            dma((2,)),
         ],
     )(decay, root, x, b)
     got = exchange(send)
@@ -795,20 +841,32 @@
         scratch_shapes=[state_scratch, packs_scratch],
     )(far(cum_rows), root, gain, x, gate, b, c, out_grad)
 
-    got, sums0 = lax.optimization_barrier((got, sums0))
+    both = lambda l, k: (l, k)
+    later = lambda l, k: (l + 1, k)
+    scaled = call(
+        functools.partial(scale_body, heads, steps),
+        "scale",
+        3,
+        grid=(2, steps),
+        in_specs=[level_rows(later), tokens(STATE, later)],
+        out_specs=pl.BlockSpec((1, heads, SPAN, STATE), lambda l, k: (l, 0, k, 0)),
+        out_shape=pltpu.HBM((2, heads, length, STATE), BF16),
+        scratch_shapes=[pltpu.VMEM((steps,) + rows_shape[1:], F32)],
+    )(far(cum_rows), c)
+
+    got, sums0, scaled = lax.optimization_barrier((got, sums0, scaled))
     picked, decays = call(
         functools.partial(pick_body, heads),
         "pick",
         1,
         in_specs=[smem, vmem],
-        out_specs=[vmem, vmem],
-        out_shape=[pltpu.VMEM(pair_shape, F32), pltpu.VMEM((segments, 8, HDIM), F32)],
+        out_specs=[anywhere, vmem],
+        out_shape=[pltpu.HBM(pair_shape, F32), pltpu.VMEM((segments, 8, HDIM), F32)],
+        scratch_shapes=[pltpu.VMEM(pair_shape, F32), dma((4,))],
     )(parent_ids, near(got))
 
     picked, late_rows = lax.optimization_barrier((picked, cum_rows))
     starts = exchange(picked)
-    both = lambda l, k: (l, k)
-    later = lambda l, k: (l + 1, k)
     local, turned, *first = call(
         functools.partial(local_body, heads, steps),
         "local",
@@ -832,12 +890,12 @@
             pltpu.HBM((2, STATE, length), BF16),
             pltpu.VMEM((FIRST, columns), BF16),
             pltpu.VMEM((FIRST, columns), BF16),
-            pltpu.VMEM((FIRST, STATE), BF16),
+            pltpu.VMEM((heads, FIRST, STATE), BF16),
             pltpu.VMEM((FIRST, columns), BF16),
             pltpu.VMEM((2 * steps,) + rows_shape[1:], F32),
         ],
         scratch_shapes=[state_scratch, packs_scratch, dma((4,))],
-    )(far(late_rows), x, b, c, gate, c, out_grad, far(late_rows))
+    )(far(late_rows), x, b, c, gate, far(scaled), out_grad, far(late_rows))
 
     scaled_act, gated_act, turned, lines, sums = call(
         functools.partial(readout_body, heads, steps),
@@ -856,14 +914,14 @@
             pair_of_levels(columns),
             pair_of_levels(columns),
             pair_of_levels(columns),
-            pair_of_levels(STATE),
-            dma((2 * steps, 4)),
+            pltpu.VMEM((heads, 2, length, STATE), BF16),
+            dma((2 * steps, 3 + heads)),
             dma,
         ],
     )(
         far(local),
         gate,
-        c,
+        far(scaled),
         out_grad,
         far(turned),
         near(first[0]),
@@ -882,9 +940,14 @@
         "grads",
         4,
         in_specs=[vmem] * 5,
-        out_specs=[anywhere, vmem],
-        out_shape=[pltpu.HBM((2, length, columns), BF16), pltpu.VMEM(pair_shape, F32)],
-        scratch_shapes=[pair_of_levels(columns), dma((2 * steps,))],
+        out_specs=[anywhere, anywhere],
+        out_shape=[pltpu.HBM((2, length, columns), BF16), pltpu.HBM(pair_shape, F32)],
+        scratch_shapes=[
+            pair_of_levels(columns),
+            pltpu.VMEM(pair_shape, F32),
+            dma((2 * steps,)),
+            dma((2,)),
+        ],
     )(near(lines), near(turned), near(scaled_act), near(gated_act), near(totals))
     got_back = exchange(send_back)
 
@@ -915,8 +978,9 @@
         "fold",
         1,
         in_specs=[smem, vmem, vmem],
-        out_specs=vmem,
-        out_shape=pltpu.VMEM(pair_shape, F32),
+        out_specs=anywhere,
+        out_shape=pltpu.HBM(pair_shape, F32),
+        scratch_shapes=[pltpu.VMEM(pair_shape, F32), dma((2,))],
     )(parent_ids, near(decays), near(got_back))
 
     folded, late_rows = lax.optimization_barrier((folded, cum_rows))

time: 113 us -> 114 us (level)
  waiting for transfers between devices: 23.1 us -> 18.7 us
  Pallas kernels: 57 us -> 61.3 us
  starting transfers between devices: 19 us -> 20.2 us
    pallas_call x0 -> x1, Pallas kernels: none -> 5.15 us  [shards(): call(functools.partial(scale_body, heads, steps), 'scale', 3, grid=(2, st...]
    all_to_all x1, waiting for transfers between devices: 7.61 us -> 2.48 us  [shards(): got = exchange(send)]
    all_to_all x1, starting transfers between devices: 3.61 us -> 4.76 us  [shards(): starts = exchange(picked)]
  transfers between devices with their start and end apart: 4 -> 4, of which waited for: 4 -> 4; matrix products, arithmetic and copies ran while one was open for 0% -> 0% of each run, Pallas kernels for 30% -> 34%
where the time goes in v8:
time: 114 us; the launch traced here: 113 us
  Pallas kernels  61.3 us (54%)
  starting transfers between devices  20.2 us (18%)
  waiting for transfers between devices  18.7 us (16%)
  blocking collectives  12 us (11%)
    all_to_all x1, blocking collectives, shards(): lax.all_to_all(sums, 'head', split_axis=0, concat_axis=0, tiled=True)  12 us
    pallas_call x1, Pallas kernels, shards(): call(functools.partial(back_body, heads, steps), 'back', 8, grid=(2, step...  9.32 us
    pallas_call x1, Pallas kernels, shards(): call(functools.partial(local_body, heads, steps), 'local', 7, grid=(2, st...  8.97 us
    all_to_all x1, starting transfers between devices, shards(): got = exchange(send)  8.15 us
    all_to_all x1, waiting for transfers between devices, shards(): got_back = exchange(send_back)  7.55 us
    pallas_call x1, Pallas kernels, shards(): call(functools.partial(forward0_body, heads, steps), 'forward0', 6, grid=...  7.53 us
    pallas_call x1, Pallas kernels, shards(): call(functools.partial(back0_body, heads, steps, features), 'back0', 6, g...  7.38 us
    pallas_call x1, Pallas kernels, shards(): call(functools.partial(states_body, heads, steps), 'states', 6, in_specs=...  6.51 us
  transfers between devices with their start and end apart: 4, of which 4 were waited for; matrix products, arithmetic and copies ran while one was open for 0% of the time, Pallas kernels for 34%

profile of v8, /device:TPU:0, one launch (start us, length us, event | category | flops | bytes accessed | tf_op | source)
XLA Modules:
  0.0 113.1 jit_solution(4762165190036299095)
XLA Ops:
  0.6 0.0 copy-start.2
  0.6 6.5 %states.1 = (f32[16,104,128]{2,1,0:T(8,128)}, f32[6,24,256]{2,1,0:T(8,128)}) custom-call(f32[3,3,1,1536]{3,2,1,0:T(1,128)} %bitcast.1, f32[1,3,128,256]{3,2,1,0:T(8,128)} %root_ref.1, bf16[3,1,1536,384]{3,2,1,0:T(8,128)(2,1)} %x_ref.3, bf16[3,1,1536,256]{3,2,1,0:T(8,128)(2,1)} %b_hbm.5), custom_call_target="tpu_custom_call" | custom-call | flops 6000000000 | bytes 18000000 | tf_op jit(solution)/shard_map/states/pallas_call | solution.py:799
  7.2 8.1 %all-to-all-start = ((f32[16,104,128]{2,1,0:T(8,128)}), f32[16,104,128]{2,1,0:T(8,128)S(1)}, u32[]{:S(2)}, u32[]{:S(2)}) async-start(f32[16,104,128]{2,1,0:T(8,128)} %get-tuple-element.40), calls=%async_computation | async-start | bytes 1703936 | tf_op jit(solution)/shard_map/all_to_all | solution.py:821
  15.3 0.0 copy-done.2
  15.3 5.1 %scale.1.scaled_hbm = bf16[2,3,1536,256]{3,2,1,0:T(8,128)(2,1)} custom-call(f32[6,24,256]{2,1,0:T(8,128)} %get-tuple-element.67.rows_ref.rows_hbm, bf16[3,1,1536,256]{3,2,1,0:T(8,128)(2,1)} %c_ref.9), custom_call_target="tpu_custom_call" | custom-call | flops 3000000000 | bytes 9000000 | tf_op jit(solution)/shard_map/scale/pallas_call | solution.py:846
  20.5 0.0 copy-start.1
  20.5 7.5 %forward0.1 = (bf16[1,1536,384]{2,1,0:T(8,128)(2,1)}, f32[8,384]{1,0:T(8,128)}) custom-call(f32[6,24,256]{2,1,0:T(8,128)} %get-tuple-element.67.rows_ref.rows_hbm, f32[1,3,128,256]{3,2,1,0:T(8,128)} %root_ref.1, f32[1,384]{1,0:T(1,128)S(1)} %reshape.7.gain_ref, bf16[3,1,1536,384]{3,2,1,0:T(8,128)(2,1)} %x_ref.3, bf16[3,1,1536,384]{3,2,1,0:T(8,128)(2,1)} %gate_ref.3, ...), custom_call_target="tpu_custom_call" | custom-call | flops 6000000000 | bytes 18000000 | tf_op jit(solution)/shard_map/forward0/pallas_call | solution.py:824
  28.0 2.5 %all-to-all-done.got_ref = f32[16,104,128]{2,1,0:T(8,128)S(1)} async-done(((f32[16,104,128]{2,1,0:T(8,128)}), f32[16,104,128]{2,1,0:T(8,128)S(1)}, u32[]{:S(2)}, u32[]{:S(2)}) %all-to-all-start) | async-done | bytes 852000 | tf_op jit(solution)/shard_map/all_to_all | solution.py:821
  30.5 0.0 copy-done.1
  30.5 1.5 %pick.1 = (f32[16,96,128]{2,1,0:T(8,128)}, f32[16,8,128]{2,1,0:T(8,128)S(1)}) custom-call(s32[2,16]{1,0:T(2,128)S(1)} %copy-done.1, f32[16,104,128]{2,1,0:T(8,128)S(1)} %all-to-all-done.got_ref), custom_call_target="tpu_custom_call" | custom-call | flops 1000000000 | bytes 3000000 | tf_op jit(solution)/shard_map/pick/pallas_call | solution.py:858
  32.0 4.8 %all-to-all-start.1 = ((f32[16,96,128]{2,1,0:T(8,128)}), f32[16,96,128]{2,1,0:T(8,128)S(1)}, u32[]{:S(2)}, u32[]{:S(2)}) async-start(f32[16,96,128]{2,1,0:T(8,128)} %get-tuple-element.55), calls=%async_computation.1 | async-start | bytes 1572864 | tf_op jit(solution)/shard_map/all_to_all | solution.py:869
  36.8 0.0 copy-start
  36.8 9.0 %local.1 = (bf16[2,1536,384]{2,1,0:T(8,128)(2,1)}, bf16[2,256,1536]{2,1,0:T(8,128)(2,1)}, bf16[512,384]{1,0:T(8,128)(2,1)S(1)}, bf16[512,384]{1,0:T(8,128)(2,1)S...) custom-call(f32[6,24,256]{2,1,0:T(8,128)} %get-tuple-element.67.rows_ref.rows_hbm, ...), custom_call_target="tpu_custom_call" | custom-call | flops 7000000000 | bytes 21000000 | tf_op jit(solution)/shard_map/local/pallas_call | solution.py:870
  45.7 4.7 %all-to-all-done.1.start_ref = f32[16,96,128]{2,1,0:T(8,128)S(1)} async-done(((f32[16,96,128]{2,1,0:T(8,128)}), f32[16,96,128]{2,1,0:T(8,128)S(1)}, u32[]{:S(2)}, u32[]{:S(2)}) %all-to-all-start.1) | async-done | bytes 786464 | tf_op jit(solution)/shard_map/all_to_all | solution.py:869
  50.5 0.0 copy-done
  50.5 5.9 %readout.1 = (f32[2,1536,384]{2,1,0:T(8,128)S(1)}, f32[2,1536,384]{2,1,0:T(8,128)S(1)}, bf16[2,256,1536]{2,1,0:T(8,128)(2,1)S(1)}, f32[4,24,256]{2,1,0:T(8,128)S(1)}, f32[8,8,1152]{2,1,0:T(8,128)S(1)}) custom-call(bf16[2,1536,384]{2,1,0:T(8,128)(2,1)} %get-tuple-element.48.local_hbm, bf16[3,1,1536,384]{3,2,1,0:T(8,128)(2,1)} %gate_ref.3, ...), custom_call_target="tpu_custom_call" | custom-call | flops 5000000000 | bytes 15000000 | tf_op jit(solution)/shard_map/readout/pallas_call | solution.py:900
  56.4 12.0 %all_to_all.25.total_ref = f32[8,8,1152]{2,1,0:T(8,128)S(1)} all-to-all(f32[8,8,1152]{2,1,0:T(8,128)S(1)} %get-tuple-element.61), channel_id=1, replica_groups=mesh['seg'=16,'head'=8] {'head'}, dimensions={0} | all-to-all | bytes 589824 | tf_op jit(solution)/shard_map/all_to_all | solution.py:936
  68.4 3.2 %grads.1 = (bf16[2,1536,384]{2,1,0:T(8,128)(2,1)}, f32[16,96,128]{2,1,0:T(8,128)}) custom-call(f32[4,24,256]{2,1,0:T(8,128)S(1)} %get-tuple-element.57.lines_ref, bf16[2,256,1536]{2,1,0:T(8,128)(2,1)S(1)} %get-tuple-element.58.turned_ref, f32[2,1536,384]{2,1,0:T(8,128)S(1)} %get-tuple-element.59.scaled_act_ref, ...), custom_call_target="tpu_custom_call" | custom-call | flops 4000000000 | bytes 12000000 | tf_op jit(solution)/shard_map/grads/pallas_call | solution.py:938
  71.6 3.6 %all-to-all-start.3 = ((f32[16,96,128]{2,1,0:T(8,128)}), f32[16,96,128]{2,1,0:T(8,128)S(1)}, u32[]{:S(2)}, u32[]{:S(2)}) async-start(f32[16,96,128]{2,1,0:T(8,128)} %get-tuple-element.62), calls=%async_computation.3 | async-start | bytes 1572864 | tf_op jit(solution)/shard_map/all_to_all | solution.py:952
  75.3 7.4 %back0.1 = (bf16[3,1,1536,384]{3,2,1,0:T(8,128)(2,1)}, f32[3,1,3,128,256]{4,3,2,1,0:T(8,128)}) custom-call(f32[6,24,256]{2,1,0:T(8,128)} %get-tuple-element.67.rows_ref.rows_hbm, f32[1,384]{1,0:T(1,128)S(1)} %reshape.7.gain_ref, f32[8,8,1152]{2,1,0:T(8,128)S(1)} %all_to_all.25.total_ref, bf16[3,1,1536,384]{3,2,1,0:T(8,128)(2,1)} %gate_ref.3, ...), custom_call_target="tpu_custom_call" | custom-call | flops 6000000000 | bytes 18000000 | tf_op jit(solution)/shard_map/back0/pallas_call | solution.py:955
  82.6 7.6 %all-to-all-done.3.got_ref = f32[16,96,128]{2,1,0:T(8,128)S(1)} async-done(((f32[16,96,128]{2,1,0:T(8,128)}), f32[16,96,128]{2,1,0:T(8,128)S(1)}, u32[]{:S(2)}, u32[]{:S(2)}) %all-to-all-start.3) | async-done | bytes 786464 | tf_op jit(solution)/shard_map/all_to_all | solution.py:952
  90.2 1.7 %fold.1 = f32[16,96,128]{2,1,0:T(8,128)} custom-call(s32[2,16]{1,0:T(2,128)S(1)} %copy-done.1, f32[16,8,128]{2,1,0:T(8,128)S(1)} %get-tuple-element.44.decay_ref, f32[16,96,128]{2,1,0:T(8,128)S(1)} %all-to-all-done.3.got_ref), custom_call_target="tpu_custom_call" | custom-call | flops 1000000000 | bytes 3000000 | tf_op jit(solution)/shard_map/fold/pallas_call | solution.py:976
  91.9 3.6 %all-to-all-start.4 = ((f32[16,96,128]{2,1,0:T(8,128)}), f32[16,96,128]{2,1,0:T(8,128)S(1)}, u32[]{:S(2)}, u32[]{:S(2)}) async-start(f32[16,96,128]{2,1,0:T(8,128)} %fold.1), calls=%async_computation.4 | async-start | bytes 1572864 | tf_op jit(solution)/shard_map/all_to_all | solution.py:987
  95.5 9.3 %back.1 = (bf16[3,1,1536,384]{3,2,1,0:T(8,128)(2,1)}, f32[3,1,3,128,256]{4,3,2,1,0:T(8,128)}, bf16[768,384]{1,0:T(8,128)(2,1)S(1)}, f32[3,128,256]{2,1,0:T(8,128...) custom-call(f32[6,24,256]{2,1,0:T(8,128)} %get-tuple-element.67.rows, ...), custom_call_target="tpu_custom_call", output_to_operand_aliasing={{0}: (6, {}), {1}: (7, {})} | custom-call | flops 8000000000 | bytes 24000000 | tf_op jit(solution)/shard_map/back/pallas_call | solution.py:990
  104.8 4.0 %all-to-all-done.4.end_ref = f32[16,96,128]{2,1,0:T(8,128)S(1)} async-done(((f32[16,96,128]{2,1,0:T(8,128)}), f32[16,96,128]{2,1,0:T(8,128)S(1)}, u32[]{:S(2)}, u32[]{:S(2)}) %all-to-all-start.4) | async-done | bytes 786464 | tf_op jit(solution)/shard_map/all_to_all | solution.py:987
  108.8 4.2 %inputs.1 = (bf16[3,1,1536,384]{3,2,1,0:T(8,128)(2,1)}, f32[3,1,3,128,256]{4,3,2,1,0:T(8,128)}) custom-call(bf16[3,1,1536,256]{3,2,1,0:T(8,128)(2,1)} %b_hbm.5, bf16[3,1,1536,384]{3,2,1,0:T(8,128)(2,1)} %get-tuple-element.71.partial_hbm, f32[3,1,3,128,256]{4,3,2,1,0:T(8,128)} %get-tuple-element.72.local_hbm, ...), custom_call_target="tpu_custom_call", output_to_operand_aliasing={{0}: (1, {}), {1}: (2, {})} | custom-call | flops 4000000000 | bytes 12000000 | tf_op jit(solution)/shard_map/inputs/pallas_call | solution.py:1022
  (1 shorter events, 0.0 us)
Async XLA Ops:
  0.6 14.7 %copy-start.2 = (f32[384]{0:T(512)S(1)}, f32[384]{0:T(512)}, u32[]{:S(2)}) copy-start(f32[384]{0:T(512)} %param.15) | copy-start | bytes 4612
  7.2 23.3 %all-to-all-start = ((f32[16,104,128]{2,1,0:T(8,128)}), f32[16,104,128]{2,1,0:T(8,128)S(1)}, u32[]{:S(2)}, u32[]{:S(2)}) async-start(f32[16,104,128]{2,1,0:T(8,128)} %get-tuple-element.40), calls=%async_computation | async-start | bytes 1703936 | tf_op jit(solution)/shard_map/all_to_all | solution.py:821
  20.5 10.0 %copy-start.1 = (s32[2,16]{1,0:T(2,128)S(1)}, s32[2,16]{1,0:T(2,128)}, u32[]{:S(2)}) copy-start(s32[2,16]{1,0:T(2,128)} %parent_ref.3) | copy-start | bytes 388
  32.0 18.5 %all-to-all-start.1 = ((f32[16,96,128]{2,1,0:T(8,128)}), f32[16,96,128]{2,1,0:T(8,128)S(1)}, u32[]{:S(2)}, u32[]{:S(2)}) async-start(f32[16,96,128]{2,1,0:T(8,128)} %get-tuple-element.55), calls=%async_computation.1 | async-start | bytes 1572864 | tf_op jit(solution)/shard_map/all_to_all | solution.py:869
  36.8 13.7 %copy-start = (f32[8,384]{1,0:T(8,128)S(1)}, f32[8,384]{1,0:T(8,128)}, u32[]{:S(2)}) copy-start(f32[8,384]{1,0:T(8,128)} %get-tuple-element.56.first_sums_ref) | copy-start | bytes 36868
  71.6 18.6 %all-to-all-start.3 = ((f32[16,96,128]{2,1,0:T(8,128)}), f32[16,96,128]{2,1,0:T(8,128)S(1)}, u32[]{:S(2)}, u32[]{:S(2)}) async-start(f32[16,96,128]{2,1,0:T(8,128)} %get-tuple-element.62), calls=%async_computation.3 | async-start | bytes 1572864 | tf_op jit(solution)/shard_map/all_to_all | solution.py:952
  91.9 16.9 %all-to-all-start.4 = ((f32[16,96,128]{2,1,0:T(8,128)}), f32[16,96,128]{2,1,0:T(8,128)S(1)}, u32[]{:S(2)}, u32[]{:S(2)}) async-start(f32[16,96,128]{2,1,0:T(8,128)} %fold.1), calls=%async_computation.4 | async-start | bytes 1572864 | tf_op jit(solution)/shard_map/all_to_all | solution.py:987

commit v9 on v7

--- a/solution.py
+++ b/solution.py
@@ -124,6 +124,15 @@
         copy.wait()
 
 
+def part_copies(send, send_out, sems):
+    half = send.shape[1] // 16 * 8
+    parts = [pl.ds(0, half), pl.ds(half, send.shape[1] - half)]
+    return [
+        pltpu.make_async_copy(send.at[:, part], send_out.at[:, part], sems.at[i])
+        for i, part in enumerate(parts)
+    ]
+
+
 def piece_copies(sources, targets, sems, pieces):
     result = []
     for i, (at, first, count) in enumerate(pieces):
@@ -148,8 +157,8 @@
     return lasts, before, after
 
 
-def states_body(heads, steps, decay_hbm, root_hbm, x_hbm, b_hbm, send, rows_out, rates, rows, decay,
-                root, x, b, decay_sem, root_sem, sems, out_sem):
+def states_body(heads, steps, decay_hbm, root_hbm, x_hbm, b_hbm, send_out, rows_out, rates, rows,
+                decay, send, root, x, b, decay_sem, root_sem, sems, out_sem, send_sems):
     blocks = steps * CHUNK
     decay_copy = pltpu.make_async_copy(decay_hbm, decay, decay_sem)
     decay_copy.start()
@@ -201,9 +210,11 @@
 
     root_copy.wait()
     states = [(root[h] * totals[0][h : h + 1]).T for h in range(heads)]
+    outs = part_copies(send, send_out, send_sems)
     for i, (level, first, count) in enumerate(pieces):
         if (level, first) == (1, 0):
             scatter_pieces(send, 0, states)
+            outs[0].start()
             states = [jnp.zeros((STATE, HDIM), F32)] * heads
         wait_all(copies[i])
         if i > 0:
@@ -223,7 +234,8 @@
     decays = jnp.broadcast_to(totals[1], (8, HDIM))
     for piece in range(send.shape[0]):
         send[piece, send.shape[1] - 8 :] = decays
-    rows_copy.wait()
+    outs[1].start()
+    wait_all(outs + [rows_copy])
 
 
 def level_decays(rows, to_end):
@@ -261,11 +273,13 @@
         ).T
 
 
-def pick_body(heads, parent_ref, got_ref, send, decay_out):
+def pick_body(heads, parent_ref, got_ref, send_out, decay_out, send, sems):
     segments = got_ref.shape[0]
     rows = STATE // segments
     pair = send.shape[1]
     half = pair // 2
+    quarter = segments // 4
+    copies = []
     for seg in range(segments):
         first = parent_ref[0, seg]
         second = parent_ref[1, seg]
@@ -277,15 +291,24 @@
             a = slice(h * rows, (h + 1) * rows)
             b = slice(half + h * rows, half + (h + 1) * rows)
             send[seg, b] = decay[h : h + 1] * got_ref[root, a] + got_ref[second, b]
-
-
-def fold_body(heads, parent_ref, decay_ref, got_ref, send):
+        if (seg + 1) % quarter == 0:
+            part = pl.ds(seg + 1 - quarter, quarter)
+            copies.append(
+                pltpu.make_async_copy(send.at[part], send_out.at[part], sems.at[len(copies)])
+            )
+            copies[-1].start()
+    wait_all(copies)
+
+
+def fold_body(heads, parent_ref, decay_ref, got_ref, send_out, send, sems):
     rows = STATE // got_ref.shape[0]
     half = send.shape[1] // 2
     send[...] = jnp.zeros_like(send)
     for seg in range(got_ref.shape[0]):
         second = parent_ref[1, seg]
         send[second, :half] += got_ref[seg, :half]
+    copies = part_copies(send, send_out, sems)
+    copies[0].start()
     for seg in range(got_ref.shape[0]):
         first = parent_ref[0, seg]
         decay = decay_ref[seg]
@@ -293,6 +316,8 @@
             a = slice(h * rows, (h + 1) * rows)
             b = slice(half + h * rows, half + (h + 1) * rows)
             send[first, b] += decay[h : h + 1] * send[seg, a] + got_ref[seg, b]
+    copies[1].start()
+    wait_all(copies)
 
 
 def causal_mask(transposed):
@@ -527,8 +552,9 @@
 
 
 def grads_body(heads, steps, features, lines_ref, turned_ref, scaled_act_ref, gated_act_ref,
-               total_ref, grad_out, send, grads, grad_sems):
+               total_ref, grad_out, send_out, grads, send, grad_sems, sems):
     total = jnp.sum(total_ref[...], axis=0)
+    sends = part_copies(send, send_out, sems)
     outs = []
     for at in (1, 0):
         for step in range(steps):
@@ -561,6 +587,8 @@
                 decayed = (turned * line).astype(BF16)
                 states[h] = states[h] + dot(decayed, grads[at, span, head(h)], 1, 0)
         scatter_pieces(send, 1 - at, states)
+        outs.append(sends[1 - at])
+        outs[-1].start()
     wait_all(outs)
 
 
@@ -758,12 +786,13 @@
         "states",
         6,
         in_specs=[anywhere] * 4,
-        out_specs=[vmem, anywhere],
-        out_shape=[pltpu.VMEM(first_shape, F32), pltpu.HBM(rows_shape, F32)],
+        out_specs=[anywhere, anywhere],
+        out_shape=[pltpu.HBM(first_shape, F32), pltpu.HBM(rows_shape, F32)],
         scratch_shapes=[
             pltpu.VMEM((levels * blocks * 8, BLOCK), F32),
             pltpu.VMEM(rows_shape, F32),
             pltpu.VMEM(decay.shape, F32),
+            pltpu.VMEM(first_shape, F32),
             pltpu.VMEM(root_state.shape[1:], F32),
             pair_of_levels(columns),
             pair_of_levels(STATE),
@@ -771,6 +800,7 @@
             dma,
             dma((4, 2)),
             dma,
+            dma((2,)),
         ],
     )(decay, root, x, b)
     got = exchange(send)
@@ -802,8 +832,9 @@
         "pick",
         1,
         in_specs=[smem, vmem],
-        out_specs=[vmem, vmem],
-        out_shape=[pltpu.VMEM(pair_shape, F32), pltpu.VMEM((segments, 8, HDIM), F32)],
+        out_specs=[anywhere, vmem],
+        out_shape=[pltpu.HBM(pair_shape, F32), pltpu.VMEM((segments, 8, HDIM), F32)],
+        scratch_shapes=[pltpu.VMEM(pair_shape, F32), dma((4,))],
     )(parent_ids, near(got))
 
     picked, late_rows = lax.optimization_barrier((picked, cum_rows))
@@ -883,9 +914,14 @@
         "grads",
         4,
         in_specs=[vmem] * 5,
-        out_specs=[anywhere, vmem],
-        out_shape=[pltpu.HBM((2, length, columns), BF16), pltpu.VMEM(pair_shape, F32)],
-        scratch_shapes=[pair_of_levels(columns), dma((2 * steps,))],
+        out_specs=[anywhere, anywhere],
+        out_shape=[pltpu.HBM((2, length, columns), BF16), pltpu.HBM(pair_shape, F32)],
+        scratch_shapes=[
+            pair_of_levels(columns),
+            pltpu.VMEM(pair_shape, F32),
+            dma((2 * steps,)),
+            dma((2,)),
+        ],
     )(near(lines), near(turned), near(scaled_act), near(gated_act), near(totals))
     got_back = exchange(send_back)
 
@@ -916,8 +952,9 @@
         "fold",
         1,
         in_specs=[smem, vmem, vmem],
-        out_specs=vmem,
-        out_shape=pltpu.VMEM(pair_shape, F32),
+        out_specs=anywhere,
+        out_shape=pltpu.HBM(pair_shape, F32),
+        scratch_shapes=[pltpu.VMEM(pair_shape, F32), dma((2,))],
     )(parent_ids, near(decays), near(got_back))
 
     folded, late_rows = lax.optimization_barrier((folded, cum_rows))

time: 111 us -> 111 us (level)
  no operation moved by 1% of the time
where the time goes in v9:
time: 111 us; the launch traced here: 110 us
  Pallas kernels  55.4 us (50%)
  waiting for transfers between devices  23 us (21%)
  starting transfers between devices  19 us (17%)
  blocking collectives  12 us (11%)
    all_to_all x1, blocking collectives, shards(): lax.all_to_all(sums, 'head', split_axis=0, concat_axis=0, tiled=True)  12 us
    pallas_call x1, Pallas kernels, shards(): call(functools.partial(back_body, heads, steps), 'back', 8, grid=(2, step...  9.31 us
    pallas_call x1, Pallas kernels, shards(): call(functools.partial(local_body, heads, steps), 'local', 7, grid=(2, st...  8.97 us
    all_to_all x1, starting transfers between devices, shards(): got = exchange(send)  8.15 us
    all_to_all x1, waiting for transfers between devices, shards(): got = exchange(send)  7.61 us
    all_to_all x1, waiting for transfers between devices, shards(): got_back = exchange(send_back)  7.58 us
    pallas_call x1, Pallas kernels, shards(): call(functools.partial(forward0_body, heads, steps), 'forward0', 6, grid=...  7.55 us
    pallas_call x1, Pallas kernels, shards(): call(functools.partial(back0_body, heads, steps, features), 'back0', 6, g...  7.32 us
  transfers between devices with their start and end apart: 4, of which 4 were waited for; matrix products, arithmetic and copies ran while one was open for 0% of the time, Pallas kernels for 30%

profile of v9, /device:TPU:0, one launch (start us, length us, event | category | flops | bytes accessed | tf_op | source)
XLA Modules:
  0.0 110.4 jit_solution(14743331620916415255)
XLA Ops:
  0.6 0.0 copy-start.2
  0.6 6.5 %states.1 = (f32[16,104,128]{2,1,0:T(8,128)}, f32[6,24,256]{2,1,0:T(8,128)}) custom-call(f32[3,3,1,1536]{3,2,1,0:T(1,128)} %bitcast.1, f32[1,3,128,256]{3,2,1,0:T(8,128)} %root_ref.1, bf16[3,1,1536,384]{3,2,1,0:T(8,128)(2,1)} %x_ref.3, bf16[3,1,1536,256]{3,2,1,0:T(8,128)(2,1)} %b_hbm.5), custom_call_target="tpu_custom_call" | custom-call | flops 6000000000 | bytes 18000000 | tf_op jit(solution)/shard_map/states/pallas_call | solution.py:784
  7.2 8.1 %all-to-all-start = ((f32[16,104,128]{2,1,0:T(8,128)}), f32[16,104,128]{2,1,0:T(8,128)S(1)}, u32[]{:S(2)}, u32[]{:S(2)}) async-start(f32[16,104,128]{2,1,0:T(8,128)} %get-tuple-element.39), calls=%async_computation | async-start | bytes 1703936 | tf_op jit(solution)/shard_map/all_to_all | solution.py:806
  15.3 0.0 copy-done.2
  15.3 0.0 copy-start
  15.3 7.5 %forward0.1 = (bf16[1,1536,384]{2,1,0:T(8,128)(2,1)}, f32[8,384]{1,0:T(8,128)}) custom-call(f32[6,24,256]{2,1,0:T(8,128)} %get-tuple-element.65.rows_ref.rows_hbm, f32[1,3,128,256]{3,2,1,0:T(8,128)} %root_ref.1, f32[1,384]{1,0:T(1,128)S(1)} %reshape.7.gain_ref, bf16[3,1,1536,384]{3,2,1,0:T(8,128)(2,1)} %x_ref.3, bf16[3,1,1536,384]{3,2,1,0:T(8,128)(2,1)} %gate_ref.3, ...), custom_call_target="tpu_custom_call" | custom-call | flops 6000000000 | bytes 18000000 | tf_op jit(solution)/shard_map/forward0/pallas_call | solution.py:809
  22.9 7.6 %all-to-all-done.got_ref = f32[16,104,128]{2,1,0:T(8,128)S(1)} async-done(((f32[16,104,128]{2,1,0:T(8,128)}), f32[16,104,128]{2,1,0:T(8,128)S(1)}, u32[]{:S(2)}, u32[]{:S(2)}) %all-to-all-start) | async-done | bytes 852000 | tf_op jit(solution)/shard_map/all_to_all | solution.py:806
  30.5 0.0 copy-done
  30.5 1.5 %pick.1 = (f32[16,96,128]{2,1,0:T(8,128)}, f32[16,8,128]{2,1,0:T(8,128)S(1)}) custom-call(s32[2,16]{1,0:T(2,128)S(1)} %copy-done, f32[16,104,128]{2,1,0:T(8,128)S(1)} %all-to-all-done.got_ref), custom_call_target="tpu_custom_call" | custom-call | flops 1000000000 | bytes 3000000 | tf_op jit(solution)/shard_map/pick/pallas_call | solution.py:830
  32.0 3.6 %all-to-all-start.1 = ((f32[16,96,128]{2,1,0:T(8,128)}), f32[16,96,128]{2,1,0:T(8,128)S(1)}, u32[]{:S(2)}, u32[]{:S(2)}) async-start(f32[16,96,128]{2,1,0:T(8,128)} %get-tuple-element.53), calls=%async_computation.1 | async-start | bytes 1572864 | tf_op jit(solution)/shard_map/all_to_all | solution.py:841
  35.6 0.0 copy-start.1
  35.6 9.0 %local.1 = (bf16[2,1536,384]{2,1,0:T(8,128)(2,1)}, bf16[2,256,1536]{2,1,0:T(8,128)(2,1)}, bf16[512,384]{1,0:T(8,128)(2,1)S(1)}, bf16[512,384]{1,0:T(8,128)(2,1)S...) custom-call(f32[6,24,256]{2,1,0:T(8,128)} %get-tuple-element.65.rows_ref.rows_hbm, ...), custom_call_target="tpu_custom_call" | custom-call | flops 7000000000 | bytes 21000000 | tf_op jit(solution)/shard_map/local/pallas_call | solution.py:844
  44.6 3.8 %all-to-all-done.1.start_ref = f32[16,96,128]{2,1,0:T(8,128)S(1)} async-done(((f32[16,96,128]{2,1,0:T(8,128)}), f32[16,96,128]{2,1,0:T(8,128)S(1)}, u32[]{:S(2)}, u32[]{:S(2)}) %all-to-all-start.1) | async-done | bytes 786464 | tf_op jit(solution)/shard_map/all_to_all | solution.py:841
  48.5 0.0 copy-done.1
  48.5 5.2 %readout.1 = (f32[2,1536,384]{2,1,0:T(8,128)S(1)}, f32[2,1536,384]{2,1,0:T(8,128)S(1)}, bf16[2,256,1536]{2,1,0:T(8,128)(2,1)S(1)}, f32[4,24,256]{2,1,0:T(8,128)S(1)}, f32[8,8,1152]{2,1,0:T(8,128)S(1)}) custom-call(bf16[2,1536,384]{2,1,0:T(8,128)(2,1)} %get-tuple-element.46.local_hbm, bf16[3,1,1536,384]{3,2,1,0:T(8,128)(2,1)} %gate_ref.3, ...), custom_call_target="tpu_custom_call" | custom-call | flops 5000000000 | bytes 15000000 | tf_op jit(solution)/shard_map/readout/pallas_call | solution.py:874
  53.7 12.0 %all_to_all.25.total_ref = f32[8,8,1152]{2,1,0:T(8,128)S(1)} all-to-all(f32[8,8,1152]{2,1,0:T(8,128)S(1)} %get-tuple-element.59), channel_id=1, replica_groups=mesh['seg'=16,'head'=8] {'head'}, dimensions={0} | all-to-all | bytes 589824 | tf_op jit(solution)/shard_map/all_to_all | solution.py:910
  65.6 3.2 %grads.1 = (bf16[2,1536,384]{2,1,0:T(8,128)(2,1)}, f32[16,96,128]{2,1,0:T(8,128)}) custom-call(f32[4,24,256]{2,1,0:T(8,128)S(1)} %get-tuple-element.55.lines_ref, bf16[2,256,1536]{2,1,0:T(8,128)(2,1)S(1)} %get-tuple-element.56.turned_ref, f32[2,1536,384]{2,1,0:T(8,128)S(1)} %get-tuple-element.57.scaled_act_ref, ...), custom_call_target="tpu_custom_call" | custom-call | flops 4000000000 | bytes 12000000 | tf_op jit(solution)/shard_map/grads/pallas_call | solution.py:912
  68.9 3.6 %all-to-all-start.3 = ((f32[16,96,128]{2,1,0:T(8,128)}), f32[16,96,128]{2,1,0:T(8,128)S(1)}, u32[]{:S(2)}, u32[]{:S(2)}) async-start(f32[16,96,128]{2,1,0:T(8,128)} %get-tuple-element.60), calls=%async_computation.3 | async-start | bytes 1572864 | tf_op jit(solution)/shard_map/all_to_all | solution.py:926
  72.5 7.3 %back0.1 = (bf16[3,1,1536,384]{3,2,1,0:T(8,128)(2,1)}, f32[3,1,3,128,256]{4,3,2,1,0:T(8,128)}) custom-call(f32[6,24,256]{2,1,0:T(8,128)} %get-tuple-element.65.rows_ref.rows_hbm, f32[1,384]{1,0:T(1,128)S(1)} %reshape.7.gain_ref, f32[8,8,1152]{2,1,0:T(8,128)S(1)} %all_to_all.25.total_ref, bf16[3,1,1536,384]{3,2,1,0:T(8,128)(2,1)} %gate_ref.3, ...), custom_call_target="tpu_custom_call" | custom-call | flops 6000000000 | bytes 18000000 | tf_op jit(solution)/shard_map/back0/pallas_call | solution.py:929
  79.8 7.6 %all-to-all-done.3.got_ref = f32[16,96,128]{2,1,0:T(8,128)S(1)} async-done(((f32[16,96,128]{2,1,0:T(8,128)}), f32[16,96,128]{2,1,0:T(8,128)S(1)}, u32[]{:S(2)}, u32[]{:S(2)}) %all-to-all-start.3) | async-done | bytes 786464 | tf_op jit(solution)/shard_map/all_to_all | solution.py:926
  87.4 1.7 %fold.1 = f32[16,96,128]{2,1,0:T(8,128)} custom-call(s32[2,16]{1,0:T(2,128)S(1)} %copy-done, f32[16,8,128]{2,1,0:T(8,128)S(1)} %get-tuple-element.43.decay_ref, f32[16,96,128]{2,1,0:T(8,128)S(1)} %all-to-all-done.3.got_ref), custom_call_target="tpu_custom_call" | custom-call | flops 1000000000 | bytes 3000000 | tf_op jit(solution)/shard_map/fold/pallas_call | solution.py:950
  89.1 3.6 %all-to-all-start.4 = ((f32[16,96,128]{2,1,0:T(8,128)}), f32[16,96,128]{2,1,0:T(8,128)S(1)}, u32[]{:S(2)}, u32[]{:S(2)}) async-start(f32[16,96,128]{2,1,0:T(8,128)} %fold.1), calls=%async_computation.4 | async-start | bytes 1572864 | tf_op jit(solution)/shard_map/all_to_all | solution.py:961
  92.7 9.3 %back.1 = (bf16[3,1,1536,384]{3,2,1,0:T(8,128)(2,1)}, f32[3,1,3,128,256]{4,3,2,1,0:T(8,128)}, bf16[768,384]{1,0:T(8,128)(2,1)S(1)}, f32[3,128,256]{2,1,0:T(8,128...) custom-call(f32[6,24,256]{2,1,0:T(8,128)} %get-tuple-element.65.rows, ...), custom_call_target="tpu_custom_call", output_to_operand_aliasing={{0}: (6, {}), {1}: (7, {})} | custom-call | flops 8000000000 | bytes 24000000 | tf_op jit(solution)/shard_map/back/pallas_call | solution.py:964
  102.0 4.0 %all-to-all-done.4.end_ref = f32[16,96,128]{2,1,0:T(8,128)S(1)} async-done(((f32[16,96,128]{2,1,0:T(8,128)}), f32[16,96,128]{2,1,0:T(8,128)S(1)}, u32[]{:S(2)}, u32[]{:S(2)}) %all-to-all-start.4) | async-done | bytes 786464 | tf_op jit(solution)/shard_map/all_to_all | solution.py:961
  106.0 4.2 %inputs.1 = (bf16[3,1,1536,384]{3,2,1,0:T(8,128)(2,1)}, f32[3,1,3,128,256]{4,3,2,1,0:T(8,128)}) custom-call(bf16[3,1,1536,256]{3,2,1,0:T(8,128)(2,1)} %b_hbm.5, bf16[3,1,1536,384]{3,2,1,0:T(8,128)(2,1)} %get-tuple-element.69.partial_hbm, f32[3,1,3,128,256]{4,3,2,1,0:T(8,128)} %get-tuple-element.70.local_hbm, ...), custom_call_target="tpu_custom_call", output_to_operand_aliasing={{0}: (1, {}), {1}: (2, {})} | custom-call | flops 4000000000 | bytes 12000000 | tf_op jit(solution)/shard_map/inputs/pallas_call | solution.py:996
  (1 shorter events, 0.0 us)
Async XLA Ops:
  0.6 14.7 %copy-start.2 = (f32[384]{0:T(512)S(1)}, f32[384]{0:T(512)}, u32[]{:S(2)}) copy-start(f32[384]{0:T(512)} %param.15) | copy-start | bytes 4612
  7.2 23.3 %all-to-all-start = ((f32[16,104,128]{2,1,0:T(8,128)}), f32[16,104,128]{2,1,0:T(8,128)S(1)}, u32[]{:S(2)}, u32[]{:S(2)}) async-start(f32[16,104,128]{2,1,0:T(8,128)} %get-tuple-element.39), calls=%async_computation | async-start | bytes 1703936 | tf_op jit(solution)/shard_map/all_to_all | solution.py:806
  15.3 15.2 %copy-start = (s32[2,16]{1,0:T(2,128)S(1)}, s32[2,16]{1,0:T(2,128)}, u32[]{:S(2)}) copy-start(s32[2,16]{1,0:T(2,128)} %parent_ref.3) | copy-start | bytes 388
  32.0 16.5 %all-to-all-start.1 = ((f32[16,96,128]{2,1,0:T(8,128)}), f32[16,96,128]{2,1,0:T(8,128)S(1)}, u32[]{:S(2)}, u32[]{:S(2)}) async-start(f32[16,96,128]{2,1,0:T(8,128)} %get-tuple-element.53), calls=%async_computation.1 | async-start | bytes 1572864 | tf_op jit(solution)/shard_map/all_to_all | solution.py:841
  35.6 12.8 %copy-start.1 = (f32[8,384]{1,0:T(8,128)S(1)}, f32[8,384]{1,0:T(8,128)}, u32[]{:S(2)}) copy-start(f32[8,384]{1,0:T(8,128)} %get-tuple-element.54.first_sums_ref) | copy-start | bytes 36868
  68.9 18.5 %all-to-all-start.3 = ((f32[16,96,128]{2,1,0:T(8,128)}), f32[16,96,128]{2,1,0:T(8,128)S(1)}, u32[]{:S(2)}, u32[]{:S(2)}) async-start(f32[16,96,128]{2,1,0:T(8,128)} %get-tuple-element.60), calls=%async_computation.3 | async-start | bytes 1572864 | tf_op jit(solution)/shard_map/all_to_all | solution.py:926
  89.1 16.9 %all-to-all-start.4 = ((f32[16,96,128]{2,1,0:T(8,128)}), f32[16,96,128]{2,1,0:T(8,128)S(1)}, u32[]{:S(2)}, u32[]{:S(2)}) async-start(f32[16,96,128]{2,1,0:T(8,128)} %fold.1), calls=%async_computation.4 | async-start | bytes 1572864 | tf_op jit(solution)/shard_map/all_to_all | solution.py:961

commit v10 on v9

--- a/solution.py
+++ b/solution.py
@@ -723,13 +723,15 @@
             grads[level, block(step * CHUNK + j)] = (
                 some_partial[block(j)].astype(F32) + extra
             ).astype(BF16)
-        span = pl.ds(step * SPAN, SPAN)
-        outs.append(
-            pltpu.make_async_copy(
-                grads.at[level, span], input_grad_out.at[level, 0, span], out_sems.at[i]
+            span = pl.ds((step * CHUNK + j) * BLOCK, BLOCK)
+            outs.append(
+                pltpu.make_async_copy(
+                    grads.at[level, span],
+                    input_grad_out.at[level, 0, span],
+                    out_sems.at[i * CHUNK + j],
+                )
             )
-        )
-        outs[-1].start()
+            outs[-1].start()
     wait_all(outs)
 
 
@@ -1008,7 +1010,7 @@
             pltpu.VMEM((2,) + state_shape[2:], F32),
             dma((2 * steps - 1, 2)),
             dma,
-            dma((2 * steps,)),
+            dma((2 * blocks,)),
             dma((2,)),
         ],
     )(b, *given, near(near_b), near(near_partial), near(near_state), near(near_rows), near(ends))

time: 111 us -> 112 us (level)
  no operation moved by 1% of the time
where the time goes in v10:
time: 112 us; the launch traced here: 111 us
  Pallas kernels  55.9 us (50%)
  waiting for transfers between devices  23 us (21%)
  starting transfers between devices  19 us (17%)
  blocking collectives  12 us (11%)
    all_to_all x1, blocking collectives, shards(): lax.all_to_all(sums, 'head', split_axis=0, concat_axis=0, tiled=True)  12 us
    pallas_call x1, Pallas kernels, shards(): call(functools.partial(back_body, heads, steps), 'back', 8, grid=(2, step...  9.3 us
    pallas_call x1, Pallas kernels, shards(): call(functools.partial(local_body, heads, steps), 'local', 7, grid=(2, st...  8.98 us
    all_to_all x1, starting transfers between devices, shards(): got = exchange(send)  8.15 us
    all_to_all x1, waiting for transfers between devices, shards(): got = exchange(send)  7.61 us
    all_to_all x1, waiting for transfers between devices, shards(): got_back = exchange(send_back)  7.58 us
    pallas_call x1, Pallas kernels, shards(): call(functools.partial(forward0_body, heads, steps), 'forward0', 6, grid=...  7.55 us
    pallas_call x1, Pallas kernels, shards(): call(functools.partial(back0_body, heads, steps, features), 'back0', 6, g...  7.32 us
  transfers between devices with their start and end apart: 4, of which 4 were waited for; matrix products, arithmetic and copies ran while one was open for 0% of the time, Pallas kernels for 30%

profile of v10, /device:TPU:0, one launch (start us, length us, event | category | flops | bytes accessed | tf_op | source)
XLA Modules:
  0.0 110.9 jit_solution(9628035198699312992)
XLA Ops:
  0.6 0.0 copy-start.2
  0.6 6.5 %states.1 = (f32[16,104,128]{2,1,0:T(8,128)}, f32[6,24,256]{2,1,0:T(8,128)}) custom-call(f32[3,3,1,1536]{3,2,1,0:T(1,128)} %bitcast.1, f32[1,3,128,256]{3,2,1,0:T(8,128)} %root_ref.1, bf16[3,1,1536,384]{3,2,1,0:T(8,128)(2,1)} %x_ref.3, bf16[3,1,1536,256]{3,2,1,0:T(8,128)(2,1)} %b_hbm.5), custom_call_target="tpu_custom_call" | custom-call | flops 6000000000 | bytes 18000000 | tf_op jit(solution)/shard_map/states/pallas_call | solution.py:786
  7.2 8.1 %all-to-all-start = ((f32[16,104,128]{2,1,0:T(8,128)}), f32[16,104,128]{2,1,0:T(8,128)S(1)}, u32[]{:S(2)}, u32[]{:S(2)}) async-start(f32[16,104,128]{2,1,0:T(8,128)} %get-tuple-element.39), calls=%async_computation | async-start | bytes 1703936 | tf_op jit(solution)/shard_map/all_to_all | solution.py:808
  15.3 0.0 copy-done.2
  15.3 0.0 copy-start
  15.3 7.5 %forward0.1 = (bf16[1,1536,384]{2,1,0:T(8,128)(2,1)}, f32[8,384]{1,0:T(8,128)}) custom-call(f32[6,24,256]{2,1,0:T(8,128)} %get-tuple-element.65.rows_ref.rows_hbm, f32[1,3,128,256]{3,2,1,0:T(8,128)} %root_ref.1, f32[1,384]{1,0:T(1,128)S(1)} %reshape.7.gain_ref, bf16[3,1,1536,384]{3,2,1,0:T(8,128)(2,1)} %x_ref.3, bf16[3,1,1536,384]{3,2,1,0:T(8,128)(2,1)} %gate_ref.3, ...), custom_call_target="tpu_custom_call" | custom-call | flops 6000000000 | bytes 18000000 | tf_op jit(solution)/shard_map/forward0/pallas_call | solution.py:811
  22.9 7.6 %all-to-all-done.got_ref = f32[16,104,128]{2,1,0:T(8,128)S(1)} async-done(((f32[16,104,128]{2,1,0:T(8,128)}), f32[16,104,128]{2,1,0:T(8,128)S(1)}, u32[]{:S(2)}, u32[]{:S(2)}) %all-to-all-start) | async-done | bytes 852000 | tf_op jit(solution)/shard_map/all_to_all | solution.py:808
  30.5 0.0 copy-done
  30.5 1.5 %pick.1 = (f32[16,96,128]{2,1,0:T(8,128)}, f32[16,8,128]{2,1,0:T(8,128)S(1)}) custom-call(s32[2,16]{1,0:T(2,128)S(1)} %copy-done, f32[16,104,128]{2,1,0:T(8,128)S(1)} %all-to-all-done.got_ref), custom_call_target="tpu_custom_call" | custom-call | flops 1000000000 | bytes 3000000 | tf_op jit(solution)/shard_map/pick/pallas_call | solution.py:832
  32.0 3.6 %all-to-all-start.1 = ((f32[16,96,128]{2,1,0:T(8,128)}), f32[16,96,128]{2,1,0:T(8,128)S(1)}, u32[]{:S(2)}, u32[]{:S(2)}) async-start(f32[16,96,128]{2,1,0:T(8,128)} %get-tuple-element.53), calls=%async_computation.1 | async-start | bytes 1572864 | tf_op jit(solution)/shard_map/all_to_all | solution.py:843
  35.6 0.0 copy-start.1
  35.6 9.0 %local.1 = (bf16[2,1536,384]{2,1,0:T(8,128)(2,1)}, bf16[2,256,1536]{2,1,0:T(8,128)(2,1)}, bf16[512,384]{1,0:T(8,128)(2,1)S(1)}, bf16[512,384]{1,0:T(8,128)(2,1)S...) custom-call(f32[6,24,256]{2,1,0:T(8,128)} %get-tuple-element.65.rows_ref.rows_hbm, ...), custom_call_target="tpu_custom_call" | custom-call | flops 7000000000 | bytes 21000000 | tf_op jit(solution)/shard_map/local/pallas_call | solution.py:846
  44.6 3.8 %all-to-all-done.1.start_ref = f32[16,96,128]{2,1,0:T(8,128)S(1)} async-done(((f32[16,96,128]{2,1,0:T(8,128)}), f32[16,96,128]{2,1,0:T(8,128)S(1)}, u32[]{:S(2)}, u32[]{:S(2)}) %all-to-all-start.1) | async-done | bytes 786464 | tf_op jit(solution)/shard_map/all_to_all | solution.py:843
  48.5 0.0 copy-done.1
  48.5 5.2 %readout.1 = (f32[2,1536,384]{2,1,0:T(8,128)S(1)}, f32[2,1536,384]{2,1,0:T(8,128)S(1)}, bf16[2,256,1536]{2,1,0:T(8,128)(2,1)S(1)}, f32[4,24,256]{2,1,0:T(8,128)S(1)}, f32[8,8,1152]{2,1,0:T(8,128)S(1)}) custom-call(bf16[2,1536,384]{2,1,0:T(8,128)(2,1)} %get-tuple-element.46.local_hbm, bf16[3,1,1536,384]{3,2,1,0:T(8,128)(2,1)} %gate_ref.3, ...), custom_call_target="tpu_custom_call" | custom-call | flops 5000000000 | bytes 15000000 | tf_op jit(solution)/shard_map/readout/pallas_call | solution.py:876
  53.6 12.0 %all_to_all.25.total_ref = f32[8,8,1152]{2,1,0:T(8,128)S(1)} all-to-all(f32[8,8,1152]{2,1,0:T(8,128)S(1)} %get-tuple-element.59), channel_id=1, replica_groups=mesh['seg'=16,'head'=8] {'head'}, dimensions={0} | all-to-all | bytes 589824 | tf_op jit(solution)/shard_map/all_to_all | solution.py:912
  65.6 3.2 %grads.1 = (bf16[2,1536,384]{2,1,0:T(8,128)(2,1)}, f32[16,96,128]{2,1,0:T(8,128)}) custom-call(f32[4,24,256]{2,1,0:T(8,128)S(1)} %get-tuple-element.55.lines_ref, bf16[2,256,1536]{2,1,0:T(8,128)(2,1)S(1)} %get-tuple-element.56.turned_ref, f32[2,1536,384]{2,1,0:T(8,128)S(1)} %get-tuple-element.57.scaled_act_ref, ...), custom_call_target="tpu_custom_call" | custom-call | flops 4000000000 | bytes 12000000 | tf_op jit(solution)/shard_map/grads/pallas_call | solution.py:914
  68.9 3.6 %all-to-all-start.3 = ((f32[16,96,128]{2,1,0:T(8,128)}), f32[16,96,128]{2,1,0:T(8,128)S(1)}, u32[]{:S(2)}, u32[]{:S(2)}) async-start(f32[16,96,128]{2,1,0:T(8,128)} %get-tuple-element.60), calls=%async_computation.3 | async-start | bytes 1572864 | tf_op jit(solution)/shard_map/all_to_all | solution.py:928
  72.5 7.3 %back0.1 = (bf16[3,1,1536,384]{3,2,1,0:T(8,128)(2,1)}, f32[3,1,3,128,256]{4,3,2,1,0:T(8,128)}) custom-call(f32[6,24,256]{2,1,0:T(8,128)} %get-tuple-element.65.rows_ref.rows_hbm, f32[1,384]{1,0:T(1,128)S(1)} %reshape.7.gain_ref, f32[8,8,1152]{2,1,0:T(8,128)S(1)} %all_to_all.25.total_ref, bf16[3,1,1536,384]{3,2,1,0:T(8,128)(2,1)} %gate_ref.3, ...), custom_call_target="tpu_custom_call" | custom-call | flops 6000000000 | bytes 18000000 | tf_op jit(solution)/shard_map/back0/pallas_call | solution.py:931
  79.8 7.6 %all-to-all-done.3.got_ref = f32[16,96,128]{2,1,0:T(8,128)S(1)} async-done(((f32[16,96,128]{2,1,0:T(8,128)}), f32[16,96,128]{2,1,0:T(8,128)S(1)}, u32[]{:S(2)}, u32[]{:S(2)}) %all-to-all-start.3) | async-done | bytes 786464 | tf_op jit(solution)/shard_map/all_to_all | solution.py:928
  87.4 1.7 %fold.1 = f32[16,96,128]{2,1,0:T(8,128)} custom-call(s32[2,16]{1,0:T(2,128)S(1)} %copy-done, f32[16,8,128]{2,1,0:T(8,128)S(1)} %get-tuple-element.43.decay_ref, f32[16,96,128]{2,1,0:T(8,128)S(1)} %all-to-all-done.3.got_ref), custom_call_target="tpu_custom_call" | custom-call | flops 1000000000 | bytes 3000000 | tf_op jit(solution)/shard_map/fold/pallas_call | solution.py:952
  89.1 3.6 %all-to-all-start.4 = ((f32[16,96,128]{2,1,0:T(8,128)}), f32[16,96,128]{2,1,0:T(8,128)S(1)}, u32[]{:S(2)}, u32[]{:S(2)}) async-start(f32[16,96,128]{2,1,0:T(8,128)} %fold.1), calls=%async_computation.4 | async-start | bytes 1572864 | tf_op jit(solution)/shard_map/all_to_all | solution.py:963
  92.7 9.3 %back.1 = (bf16[3,1,1536,384]{3,2,1,0:T(8,128)(2,1)}, f32[3,1,3,128,256]{4,3,2,1,0:T(8,128)}, bf16[768,384]{1,0:T(8,128)(2,1)S(1)}, f32[3,128,256]{2,1,0:T(8,128...) custom-call(f32[6,24,256]{2,1,0:T(8,128)} %get-tuple-element.65.rows, ...), custom_call_target="tpu_custom_call", output_to_operand_aliasing={{0}: (6, {}), {1}: (7, {})} | custom-call | flops 8000000000 | bytes 24000000 | tf_op jit(solution)/shard_map/back/pallas_call | solution.py:966
  102.0 4.0 %all-to-all-done.4.end_ref = f32[16,96,128]{2,1,0:T(8,128)S(1)} async-done(((f32[16,96,128]{2,1,0:T(8,128)}), f32[16,96,128]{2,1,0:T(8,128)S(1)}, u32[]{:S(2)}, u32[]{:S(2)}) %all-to-all-start.4) | async-done | bytes 786464 | tf_op jit(solution)/shard_map/all_to_all | solution.py:963
  106.0 4.7 %inputs.1 = (bf16[3,1,1536,384]{3,2,1,0:T(8,128)(2,1)}, f32[3,1,3,128,256]{4,3,2,1,0:T(8,128)}) custom-call(bf16[3,1,1536,256]{3,2,1,0:T(8,128)(2,1)} %b_hbm.5, bf16[3,1,1536,384]{3,2,1,0:T(8,128)(2,1)} %get-tuple-element.69.partial_hbm, f32[3,1,3,128,256]{4,3,2,1,0:T(8,128)} %get-tuple-element.70.local_hbm, ...), custom_call_target="tpu_custom_call", output_to_operand_aliasing={{0}: (1, {}), {1}: (2, {})} | custom-call | flops 4000000000 | bytes 12000000 | tf_op jit(solution)/shard_map/inputs/pallas_call | solution.py:998
  (1 shorter events, 0.0 us)
Async XLA Ops:
  0.6 14.7 %copy-start.2 = (f32[384]{0:T(512)S(1)}, f32[384]{0:T(512)}, u32[]{:S(2)}) copy-start(f32[384]{0:T(512)} %param.15) | copy-start | bytes 4612
  7.2 23.3 %all-to-all-start = ((f32[16,104,128]{2,1,0:T(8,128)}), f32[16,104,128]{2,1,0:T(8,128)S(1)}, u32[]{:S(2)}, u32[]{:S(2)}) async-start(f32[16,104,128]{2,1,0:T(8,128)} %get-tuple-element.39), calls=%async_computation | async-start | bytes 1703936 | tf_op jit(solution)/shard_map/all_to_all | solution.py:808
  15.3 15.2 %copy-start = (s32[2,16]{1,0:T(2,128)S(1)}, s32[2,16]{1,0:T(2,128)}, u32[]{:S(2)}) copy-start(s32[2,16]{1,0:T(2,128)} %parent_ref.3) | copy-start | bytes 388
  32.0 16.5 %all-to-all-start.1 = ((f32[16,96,128]{2,1,0:T(8,128)}), f32[16,96,128]{2,1,0:T(8,128)S(1)}, u32[]{:S(2)}, u32[]{:S(2)}) async-start(f32[16,96,128]{2,1,0:T(8,128)} %get-tuple-element.53), calls=%async_computation.1 | async-start | bytes 1572864 | tf_op jit(solution)/shard_map/all_to_all | solution.py:843
  35.6 12.8 %copy-start.1 = (f32[8,384]{1,0:T(8,128)S(1)}, f32[8,384]{1,0:T(8,128)}, u32[]{:S(2)}) copy-start(f32[8,384]{1,0:T(8,128)} %get-tuple-element.54.first_sums_ref) | copy-start | bytes 36868
  68.9 18.5 %all-to-all-start.3 = ((f32[16,96,128]{2,1,0:T(8,128)}), f32[16,96,128]{2,1,0:T(8,128)S(1)}, u32[]{:S(2)}, u32[]{:S(2)}) async-start(f32[16,96,128]{2,1,0:T(8,128)} %get-tuple-element.60), calls=%async_computation.3 | async-start | bytes 1572864 | tf_op jit(solution)/shard_map/all_to_all | solution.py:928
  89.1 16.9 %all-to-all-start.4 = ((f32[16,96,128]{2,1,0:T(8,128)}), f32[16,96,128]{2,1,0:T(8,128)S(1)}, u32[]{:S(2)}, u32[]{:S(2)}) async-start(f32[16,96,128]{2,1,0:T(8,128)} %fold.1), calls=%async_computation.4 | async-start | bytes 1572864 | tf_op jit(solution)/shard_map/all_to_all | solution.py:963
